TPU v7x, 32 devices: a whole 2x2x4 slice. The times are simulated.
32 devices in a mesh: pts: 8 (over y, x, core), lmk: 4 (over z).
Axes of the slice: x: 2, y: 2, z: 4, core: 2. Of those that a mesh axis runs over, the one named last changes fastest.
Arguments:
- points: bfloat16 [2048, 768], P('pts'), may hold values from -6 to 6
- landmarks: bfloat16 [384, 768], P('lmk'), may hold values from -6 to 6
- panels: bfloat16 [8, 384, 2048], P('pts', None, 'lmk'), may hold values from -0.3125 to 0.3125
- panel_index: int32 [1], replicated, may hold values from 0 to 7
- assignment: int32 [2048], P('pts'), may hold values from 0 to 4095, as said below
Outputs:
- centroid_sums: float32 [4096, 2048], P('pts', 'lmk')
- cluster_counts: int32 [4096], P('pts')
Inputs may be any that keep to these rules, and one draw needn't show every extreme that they name: `assignment`: owner of a cluster c is c // 512. In each aligned block of 256 points (the points of one device) at most 64 points have clusters of one owner; one owner, the same for every block, has exactly 64 points in every block.
All inputs are finite; a program needn't handle non-finite values.
Results may differ from a plain program's by a relative error of at most 0.0017.
Values may be sent and summed in bfloat16 or wider, within the bound.
No kernel may reach another device: no remote copies, remote signals or barrier semaphores. Data moves between devices by JAX's collectives and lax.ppermute only.
A program may use at most 64 MiB of HBM per device.

v0:
```python
import math

import jax
import jax.numpy as jnp
from jax import lax
from jax.experimental import pallas as pl
from jax.experimental.pallas import tpu as pltpu
from jax.sharding import PartitionSpec as P

CLUSTERS = 4096
LANES = 128
VMEM_LIMIT = 48 * 1024 * 1024
NT = (((1,), (1,)), ((), ()))


def unit_rows(values_in):
    widened = values_in.astype(jnp.float32)
    scale = lax.rsqrt(jnp.mean(widened * widened, axis=1, keepdims=True) + 1e-06)
    return (widened * scale).astype(jnp.bfloat16)


def place_kernel(groups, capacity, *refs):
    points_out, tags_out = refs[-2:]
    for core in range(2):
        points_ref, assignment_ref = refs[2 * core : 2 * core + 2]
        point_rows = points_ref.shape[0]
        ids = assignment_ref[...]
        owned = CLUSTERS // groups
        owners = lax.div(ids, owned)
        tags = ids - owners * owned + 1
        hits = lax.broadcasted_iota(jnp.int32, (groups, point_rows), 0) == owners
        earlier = lax.broadcasted_iota(
            jnp.int32, (point_rows, point_rows), 0
        ) < lax.broadcasted_iota(jnp.int32, (point_rows, point_rows), 1)
        before = jnp.dot(
            hits.astype(jnp.float32).astype(jnp.bfloat16),
            earlier.astype(jnp.float32).astype(jnp.bfloat16),
            preferred_element_type=jnp.float32,
        )
        rank = jnp.sum(jnp.where(hits, before, 0.0), axis=0, keepdims=True).astype(jnp.int32)
        slots = owners * capacity + rank
        placed = (
            (lax.broadcasted_iota(jnp.int32, (groups * capacity, point_rows), 0) == slots)
            .astype(jnp.float32)
            .astype(jnp.bfloat16)
        )
        points_out[core] = jnp.dot(
            placed, unit_rows(points_ref[...]), preferred_element_type=jnp.float32
        ).astype(jnp.bfloat16)
        if core == 0:
            high = lax.div(tags, 256)
            which = lax.broadcasted_iota(jnp.int32, (tags_out.shape[1], point_rows), 0)
            coded = jnp.where(which == 0, high, jnp.where(which == 1, tags - high * 256, 0))
            tags_out[...] = lax.dot_general(
                placed,
                coded.astype(jnp.float32).astype(jnp.bfloat16),
                NT,
                preferred_element_type=jnp.float32,
            ).astype(jnp.bfloat16)


def marks_kernel(place_ref, after_ref, *refs):
    halves, marks_ref, keep_ref = refs[:-2], refs[-2], refs[-1]
    half = halves[0].shape[0]
    for away, block in enumerate(halves):
        first = pl.multiple_of(lax.bitwise_xor(place_ref[0], away) * half, 16)
        marks_ref[pl.ds(first, half), :] = unit_rows(block[...])
    keep_ref[...] = jnp.full(keep_ref.shape, place_ref[1], jnp.int32)


def rows_kernel(groups, capacity, points_ref, tags_ref, marks_ref, out_ref):
    marks = marks_ref.shape[0]
    no_tags = jnp.zeros(tags_ref.shape, jnp.bfloat16)
    for core, tags in enumerate((tags_ref[...], no_tags)):
        scores = lax.dot_general(
            points_ref[core], marks_ref[...], NT, preferred_element_type=jnp.float32
        )
        rows = jnp.exp(scores * (0.5 / math.sqrt(points_ref.shape[2]))).astype(jnp.bfloat16)
        if len(out_ref.shape) == 4:
            for group in range(groups):
                here = slice(group * capacity, (group + 1) * capacity)
                out_ref[group, core, :, :marks] = rows[here]
                out_ref[group, core, :, marks:] = tags[here]
        else:
            out_ref[core, :, :marks] = rows
            out_ref[core, :, marks:] = tags


def sums_kernel(scale, even_ref, odd_ref, mine_ref, other_ref, totals_ref, counts_ref, panel_ref):
    slots, lanes = even_ref.shape
    owned, marks = totals_ref.shape[0], mine_ref.shape[0]
    for side, half in enumerate((mine_ref, other_ref)):
        panel_ref[side, :marks, :] = half[...]
        panel_ref[side, marks:, :] = jnp.zeros((lanes - marks, half.shape[1]), jnp.bfloat16)
    features = (
        jnp.dot(even_ref[...], panel_ref[0], preferred_element_type=jnp.float32)
        + jnp.dot(odd_ref[...], panel_ref[1], preferred_element_type=jnp.float32)
    ).astype(jnp.bfloat16)
    which = lax.broadcasted_iota(jnp.int32, (8, lanes - marks), 1)
    weights = jnp.where(which == 0, 256.0, jnp.where(which == 1, 1.0, 0.0)).astype(jnp.bfloat16)
    tags = lax.dot_general(weights, even_ref[:, marks:], NT, preferred_element_type=jnp.float32)
    tags += lax.dot_general(weights, odd_ref[:, marks:], NT, preferred_element_type=jnp.float32)
    tags = tags[:1].astype(jnp.int32)
    member = (
        (lax.broadcasted_iota(jnp.int32, (owned, slots), 0) + 1 == tags)
        .astype(jnp.float32)
        .astype(jnp.bfloat16)
    )
    totals_ref[...] = jnp.dot(member, features, preferred_element_type=jnp.float32) * scale
    counts_ref[...] = lax.dot_general(
        jnp.ones((8, slots), jnp.bfloat16), member, NT, preferred_element_type=jnp.float32
    )[:1].astype(jnp.int32)


def call(kernel, shapes, *operands, place=None, scratch=()):
    held = pl.BlockSpec(memory_space=pltpu.VMEM)
    first = [] if place is None else [place]
    return pl.pallas_call(
        kernel,
        out_shape=shapes,
        in_specs=[pl.BlockSpec(memory_space=pltpu.SMEM)] * len(first) + [held] * len(operands),
        out_specs=(held,) * len(shapes) if isinstance(shapes, tuple) else held,
        scratch_shapes=scratch,
        compiler_params=pltpu.CompilerParams(vmem_limit_bytes=VMEM_LIMIT),
    )(*first, *operands)


def array(shape, dtype=jnp.bfloat16):
    return jax.ShapeDtypeStruct(shape, dtype)


def swap(block, axis, mask):
    return lax.ppermute(block, axis, [(i, i ^ mask) for i in range(lax.axis_size(axis))])


def spread(panel, parts, holder):
    me = lax.axis_index("pts")
    sides = panel.reshape(parts, 2, -1, panel.shape[1])
    mine, other = (
        lax.dynamic_index_in_dim(sides, side, 1, keepdims=False).reshape(-1, panel.shape[1])
        for side in (me % 2, 1 - me % 2)
    )
    return jnp.where(((holder ^ me) & 1) == 0, mine, swap(other, "pts", 1))


def exchange(rows, groups, capacity):
    slots, lanes = groups * capacity, rows.shape[-1]
    if rows.ndim == 3:
        rows = rows.reshape(2, groups, capacity, lanes).swapaxes(0, 1)
    arrived = lax.all_to_all(
        rows.reshape(groups, 2 * capacity, lanes), "pts", split_axis=0, concat_axis=0, tiled=True
    ).reshape(groups // 2, 2, 2 * capacity, lanes)
    core = lax.axis_index("pts") % 2
    even = lax.dynamic_index_in_dim(arrived, core, 1, keepdims=False)
    odd = lax.dynamic_index_in_dim(arrived, 1 - core, 1, keepdims=False)
    odd = jnp.concatenate([odd[:, capacity:], odd[:, :capacity]], axis=1)
    return even.reshape(slots, lanes), odd.reshape(slots, lanes)


def body(points, landmarks, panels, panel_index, assignment):
    groups, parts = lax.axis_size("pts"), lax.axis_size("lmk")
    point_rows, width = points.shape
    capacity = 2 * point_rows // groups
    slots = groups * capacity
    owned = CLUSTERS // groups
    depth, columns = panels.shape[1:]
    half = landmarks.shape[0] // 2
    lanes = -(-(depth // 2 + 2) // LANES) * LANES
    me = lax.axis_index("pts")
    mine = lax.dynamic_slice_in_dim(landmarks, (me % 2) * half, half, 0)
    halves = [mine] + [swap(mine, "lmk", mask) for mask in range(1, parts)]
    differs = panel_index[0] ^ me
    panel = spread(panels[0], parts, panel_index[0])
    masks = [1 << bit for bit in range(1, groups.bit_length() - 1)]
    panel_met = swap(panel, "pts", masks[0])
    place = jnp.stack([lax.axis_index("lmk"), (differs & masks[0]) == 0]).astype(jnp.int32)
    assignment = assignment.reshape(1, point_rows)
    placed, tags = call(
        lambda *refs: place_kernel(groups, capacity, *refs),
        (array((2, slots, width)), array((slots, lanes - depth // 2))),
        points,
        assignment,
        swap(points, "pts", 1),
        swap(assignment, "pts", 1),
    )
    marks, keep = call(
        marks_kernel,
        (array((depth // 2, width)), array((1, columns), jnp.int32)),
        tags,
        *halves,
        place=place,
    )
    rows = call(
        lambda *refs: rows_kernel(groups, capacity, *refs),
        array((groups, 2, capacity, lanes) if capacity % 16 == 0 else (2, slots, lanes)),
        placed,
        tags,
        marks,
    )
    panel = jnp.where(keep != 0, panel, panel_met)
    for mask in masks[1:]:
        panel = jnp.where((differs & mask) == 0, panel, swap(panel, "pts", mask))
    even, odd = exchange(rows, groups, capacity)
    totals, counts = call(
        lambda *refs: sums_kernel(CLUSTERS / (point_rows * groups), *refs),
        (array((owned, columns), jnp.float32), array((1, owned), jnp.int32)),
        even,
        odd,
        panel,
        swap(panel, "pts", 1),
        scratch=[pltpu.VMEM((2, lanes, columns), jnp.bfloat16)],
    )
    return (totals, counts.reshape(owned))


def solution(mesh):
    in_specs = (P("pts", None), P("lmk", None), P("pts", None, "lmk"), P(), P("pts"))
    out_specs = (P("pts", "lmk"), P("pts"))
    return jax.shard_map(body, mesh=mesh, in_specs=in_specs, out_specs=out_specs, check_vma=False)
```

profile of v0, /device:TPU:0, one launch (start us, length us, event | category | flops | bytes accessed | tf_op | source)
XLA Modules:
  0.0 36.6 jit_solution(3296657453833600721)
XLA Ops:
  0.6 0.0 copy-start
  0.6 0.0 copy-start.1
  0.7 0.0 copy-start.2
  0.7 1.1 %constant_dynamic-slice_fusion.1 = (bf16[4,1,48,512]{3,2,1,0:T(8,128)(2,1)S(1)}, bf16[4,1,48,512]{3,2,1,0:T(8,128)(2,1)S(1)}) fusion(bf16[4,2,48,512]{3,2,1,0:T(8,128)(2,1)} %bitcast.25, s32[]{:T(128)S(6)} %select_n.46, s32[]{:T(128)S(6)} %select_n.47), kind=kLoop, calls=%fused_computation.7 | loop fusion | bytes 786440 | tf_op jit(solution)/shard_map/jit(dynamic_index_in_dim)/dynamic_slice | solution.py:140
  1.8 0.5 %collective-permute-start.5 = (bf16[192,512]{1,0:T(8,128)(2,1)S(1)}, bf16[192,512]{1,0:T(8,128)(2,1)S(1)}, u32[]{:S(2)}, u32[]{:S(2)}) collective-permute-start(bf16[192,512]{1,0:T(8,128)(2,1)S(1)} %bitcast.26), channel_id=1, source_target_pairs={{0,4},{4,0},{8,12},{12,8},{16,20},{20,16},{24,28},{28,24},{1,5},{5... | collective-permute-start | bytes 589832 | tf_op jit(solution)/shard_map/ppermute | solution.py:133
  2.3 0.1 collective-permute-start
  2.4 3.1 %collective-permute-start.2 = (bf16[48,768]{1,0:T(8,128)(2,1)S(1)}, bf16[48,768]{1,0:T(8,128)(2,1)S(1)}, u32[]{:S(2)}, u32[]{:S(2)}) collective-permute-start(bf16[48,768]{1,0:T(8,128)(2,1)S(1)} %constant_dynamic-slice_fusion.3.refs_0_), channel_id=1, source_target_pairs={{0,1},{1,0},{2,3},{3,2},{4,5},{5,4},{6,7},{7,6},{8,9},{9,8},{10,11... | collective-permute-start | bytes 221192 | tf_op jit(solution)/shard_map/ppermute | solution.py:133
  5.5 2.6 %collective-permute-start.3 = (bf16[48,768]{1,0:T(8,128)(2,1)S(1)}, bf16[48,768]{1,0:T(8,128)(2,1)S(1)}, u32[]{:S(2)}, u32[]{:S(2)}) collective-permute-start(bf16[48,768]{1,0:T(8,128)(2,1)S(1)} %constant_dynamic-slice_fusion.3.refs_0_), channel_id=1, source_target_pairs={{0,2},{1,3},{2,0},{3,1},{4,6},{5,7},{6,4},{7,5},{8,10},{9,11},{10,... | collective-permute-start | bytes 221192 | tf_op jit(solution)/shard_map/ppermute | solution.py:133
  8.1 0.0 collective-permute-start.4
  8.8 0.1 collective-permute-start.1
  8.9 1.3 %collective-permute-done.1.refs_3_ = s32[1,256]{1,0:T(1,128)S(1)} collective-permute-done((s32[1,256]{1,0:T(1,128)}, s32[1,256]{1,0:T(1,128)S(1)}, u32[]{:S(2)}, u32[]{:S(2)}) %collective-permute-start.1) | collective-permute-done | bytes 1056 | tf_op jit(solution)/shard_map/ppermute | solution.py:133
  10.2 1.7 %collective-permute-start.6 = (bf16[192,512]{1,0:T(8,128)(2,1)S(1)}, bf16[192,512]{1,0:T(8,128)(2,1)S(1)}, u32[]{:S(2)}, u32[]{:S(2)}) collective-permute-start(bf16[192,512]{1,0:T(8,128)(2,1)S(1)} %bitcast_select_fusion), channel_id=1, source_target_pairs={{0,8},{4,12},{8,0},{12,4},{16,24},{20,28},{24,16},{28,20},{1,9},{5... | collective-permute-start | bytes 589832 | tf_op jit(solution)/shard_map/ppermute | solution.py:133
  11.9 0.1 pad_add_fusion.place_ref
  12.0 1.1 %shard_map.68 = (bf16[2,512,768]{2,1,0:T(8,128)(2,1)S(1)}, bf16[512,64]{1,0:T(8,128)(2,1)S(1)}) custom-call(bf16[256,768]{1,0:T(8,128)(2,1)S(1)} %copy-done.1, s32[1,256]{1,0:T(1,128)S(1)} %bitcast.23, bf16[256,768]{1,0:T(8,128)(2,1)S(1)} %collective-permute-done.refs_2_, s32[1,256]{1,0:T(1,128)S(1)} %collective-permute-done.1.refs_3_), custom_call_target="tpu_custom_call" | custom-call | tf_op jit(solution)/shard_map/pallas_call | solution.py:118
  13.1 0.4 %collective-permute-done.3.refs_2_ = bf16[48,768]{1,0:T(8,128)(2,1)S(1)} collective-permute-done((bf16[48,768]{1,0:T(8,128)(2,1)S(1)}, bf16[48,768]{1,0:T(8,128)(2,1)S(1)}, u32[]{:S(2)}, u32[]{:S(2)}) %collective-permute-start.3) | collective-permute-done | bytes 73760 | tf_op jit(solution)/shard_map/ppermute | solution.py:133
  13.5 0.8 %collective-permute-done.4.refs_3_ = bf16[48,768]{1,0:T(8,128)(2,1)S(1)} collective-permute-done((bf16[48,768]{1,0:T(8,128)(2,1)S(1)}, bf16[48,768]{1,0:T(8,128)(2,1)S(1)}, u32[]{:S(2)}, u32[]{:S(2)}) %collective-permute-start.4) | collective-permute-done | bytes 73760 | tf_op jit(solution)/shard_map/ppermute | solution.py:133
  14.3 0.7 %shard_map.69 = (bf16[192,768]{1,0:T(8,128)(2,1)S(1)}, s32[1,512]{1,0:T(1,128)S(1)}) custom-call(s32[2]{0:T(128)S(1)} %pad_add_fusion.place_ref, bf16[512,64]{1,0:T(8,128)(2,1)S(1)} %get-tuple-element.9.after_ref.refs_1_, bf16[48,768]{1,0:T(8,128)(2,1)S(1)} %constant_dynamic-slice_fusion.3.refs_0_, bf16[48,768]{1,0:T(8,128)(2,1)S(1)} %collective-permute-done.2.refs_1_, ...), custom_call_target="tpu_custom_call" | custom-call | tf_op jit(solution)/shard_map/pallas_call | solution.py:118
  15.0 1.4 %shard_map.70 = bf16[8,2,64,256]{3,2,1,0:T(8,128)(2,1)} custom-call(bf16[2,512,768]{2,1,0:T(8,128)(2,1)S(1)} %get-tuple-element.8.refs_0_, bf16[512,64]{1,0:T(8,128)(2,1)S(1)} %get-tuple-element.9.after_ref.refs_1_, bf16[192,768]{1,0:T(8,128)(2,1)S(1)} %get-tuple-element.10.refs_2_), custom_call_target="tpu_custom_call" | custom-call | tf_op jit(solution)/shard_map/pallas_call | solution.py:118
  16.4 3.7 %all-to-all-start = ((bf16[8,128,256]{2,1,0:T(8,128)(2,1)}), bf16[8,128,256]{2,1,0:T(8,128)(2,1)S(1)}, u32[]{:S(2)}, u32[]{:S(2)}) async-start(bf16[8,128,256]{2,1,0:T(8,128)(2,1)} %bitcast.4), calls=%async_computation | async-start | bytes 1048576 | tf_op jit(solution)/shard_map/all_to_all | solution.py:150
  20.2 2.1 %collective-permute-start.7 = (bf16[192,512]{1,0:T(8,128)(2,1)S(1)}, bf16[192,512]{1,0:T(8,128)(2,1)S(1)}, u32[]{:S(2)}, u32[]{:S(2)}) collective-permute-start(bf16[192,512]{1,0:T(8,128)(2,1)S(1)} %broadcast_select_fusion), channel_id=1, source_target_pairs={{0,16},{4,20},{8,24},{12,28},{16,0},{20,4},{24,8},{28,12},{1,17},{... | collective-permute-start | bytes 589832 | tf_op jit(solution)/shard_map/ppermute | solution.py:133
  22.3 10.9 %collective-permute-done.7 = bf16[192,512]{1,0:T(8,128)(2,1)S(1)} collective-permute-done((bf16[192,512]{1,0:T(8,128)(2,1)S(1)}, bf16[192,512]{1,0:T(8,128)(2,1)S(1)}, u32[]{:S(2)}, u32[]{:S(2)}) %collective-permute-start.7) | collective-permute-done | bytes 196640 | tf_op jit(solution)/shard_map/ppermute | solution.py:133
  33.2 0.1 collective-permute-start.8
  33.4 1.3 %collective-permute-done.8.refs_3_ = bf16[192,512]{1,0:T(8,128)(2,1)S(1)} collective-permute-done((bf16[192,512]{1,0:T(8,128)(2,1)S(1)}, bf16[192,512]{1,0:T(8,128)(2,1)S(1)}, u32[]{:S(2)}, u32[]{:S(2)}) %collective-permute-start.8) | collective-permute-done | bytes 196640 | tf_op jit(solution)/shard_map/ppermute | solution.py:133
  34.8 1.9 %shard_map.71 = (f32[512,512]{1,0:T(8,128)}, s32[1,512]{1,0:T(1,128)}) custom-call(bf16[512,256]{1,0:T(8,128)(2,1)S(1)} %bitcast.20, bf16[512,256]{1,0:T(8,128)(2,1)S(1)} %bitcast.21, bf16[192,512]{1,0:T(8,128)(2,1)S(1)} %broadcast_select_fusion.1.refs_2_, bf16[192,512]{1,0:T(8,128)(2,1)S(1)} %collective-permute-done.8.refs_3_), custom_call_target="tpu_custom_call" | custom-call | tf_op jit(solution)/shard_map/pallas_call | solution.py:118
  (16 shorter events, 0.2 us)
Async XLA Ops:
  0.6 1.8 %copy-start = (bf16[96,768]{1,0:T(8,128)(2,1)S(1)}, bf16[96,768]{1,0:T(8,128)(2,1)}, u32[]{:S(2)}) copy-start(bf16[96,768]{1,0:T(8,128)(2,1)} %param.6) | copy-start | bytes 442372
  0.6 11.3 %copy-start.1 = (bf16[256,768]{1,0:T(8,128)(2,1)S(1)}, bf16[256,768]{1,0:T(8,128)(2,1)}, u32[]{:S(2)}) copy-start(bf16[256,768]{1,0:T(8,128)(2,1)} %refs_0_.1) | copy-start | bytes 1179652
  0.7 11.3 %copy-start.2 = (s32[256]{0:T(256)S(1)}, s32[256]{0:T(256)}, u32[]{:S(2)}) copy-start(s32[256]{0:T(256)} %param.9) | copy-start | bytes 3076
  1.8 6.9 %collective-permute-start.5 = (bf16[192,512]{1,0:T(8,128)(2,1)S(1)}, bf16[192,512]{1,0:T(8,128)(2,1)S(1)}, u32[]{:S(2)}, u32[]{:S(2)}) collective-permute-start(bf16[192,512]{1,0:T(8,128)(2,1)S(1)} %bitcast.26), channel_id=1, source_target_pairs={{0,4},{4,0},{8,12},{12,8},{16,20},{20,16},{24,28},{28,24},{1,5},{5... | collective-permute-start | bytes 589832 | tf_op jit(solution)/shard_map/ppermute | solution.py:133
  2.3 9.6 %collective-permute-start = (bf16[256,768]{1,0:T(8,128)(2,1)}, bf16[256,768]{1,0:T(8,128)(2,1)S(1)}, u32[]{:S(2)}, u32[]{:S(2)}) collective-permute-start(bf16[256,768]{1,0:T(8,128)(2,1)} %refs_0_.1), channel_id=1, source_target_pairs={{0,4},{4,0},{8,12},{12,8},{16,20},{20,16},{24,28},{28,24},{1,5},{5... | collective-permute-start | bytes 1179656 | tf_op jit(solution)/shard_map/ppermute | solution.py:133
  2.4 10.7 %collective-permute-start.2 = (bf16[48,768]{1,0:T(8,128)(2,1)S(1)}, bf16[48,768]{1,0:T(8,128)(2,1)S(1)}, u32[]{:S(2)}, u32[]{:S(2)}) collective-permute-start(bf16[48,768]{1,0:T(8,128)(2,1)S(1)} %constant_dynamic-slice_fusion.3.refs_0_), channel_id=1, source_target_pairs={{0,1},{1,0},{2,3},{3,2},{4,5},{5,4},{6,7},{7,6},{8,9},{9,8},{10,11... | collective-permute-start | bytes 221192 | tf_op jit(solution)/shard_map/ppermute | solution.py:133
  5.5 8.0 %collective-permute-start.3 = (bf16[48,768]{1,0:T(8,128)(2,1)S(1)}, bf16[48,768]{1,0:T(8,128)(2,1)S(1)}, u32[]{:S(2)}, u32[]{:S(2)}) collective-permute-start(bf16[48,768]{1,0:T(8,128)(2,1)S(1)} %constant_dynamic-slice_fusion.3.refs_0_), channel_id=1, source_target_pairs={{0,2},{1,3},{2,0},{3,1},{4,6},{5,7},{6,4},{7,5},{8,10},{9,11},{10,... | collective-permute-start | bytes 221192 | tf_op jit(solution)/shard_map/ppermute | solution.py:133
  8.1 6.3 %collective-permute-start.4 = (bf16[48,768]{1,0:T(8,128)(2,1)S(1)}, bf16[48,768]{1,0:T(8,128)(2,1)S(1)}, u32[]{:S(2)}, u32[]{:S(2)}) collective-permute-start(bf16[48,768]{1,0:T(8,128)(2,1)S(1)} %constant_dynamic-slice_fusion.3.refs_0_), channel_id=1, source_target_pairs={{0,3},{1,2},{2,1},{3,0},{4,7},{5,6},{6,5},{7,4},{8,11},{9,10},{10,... | collective-permute-start | bytes 221192 | tf_op jit(solution)/shard_map/ppermute | solution.py:133
  8.8 1.4 %collective-permute-start.1 = (s32[1,256]{1,0:T(1,128)}, s32[1,256]{1,0:T(1,128)S(1)}, u32[]{:S(2)}, u32[]{:S(2)}) collective-permute-start(s32[1,256]{1,0:T(1,128)} %bitcast.22), channel_id=1, source_target_pairs={{0,4},{4,0},{8,12},{12,8},{16,20},{20,16},{24,28},{28,24},{1,5},{5... | collective-permute-start | bytes 3080 | tf_op jit(solution)/shard_map/ppermute | solution.py:133
  10.2 10.0 %collective-permute-start.6 = (bf16[192,512]{1,0:T(8,128)(2,1)S(1)}, bf16[192,512]{1,0:T(8,128)(2,1)S(1)}, u32[]{:S(2)}, u32[]{:S(2)}) collective-permute-start(bf16[192,512]{1,0:T(8,128)(2,1)S(1)} %bitcast_select_fusion), channel_id=1, source_target_pairs={{0,8},{4,12},{8,0},{12,4},{16,24},{20,28},{24,16},{28,20},{1,9},{5... | collective-permute-start | bytes 589832 | tf_op jit(solution)/shard_map/ppermute | solution.py:133
  16.4 16.9 %all-to-all-start = ((bf16[8,128,256]{2,1,0:T(8,128)(2,1)}), bf16[8,128,256]{2,1,0:T(8,128)(2,1)S(1)}, u32[]{:S(2)}, u32[]{:S(2)}) async-start(bf16[8,128,256]{2,1,0:T(8,128)(2,1)} %bitcast.4), calls=%async_computation | async-start | bytes 1048576 | tf_op jit(solution)/shard_map/all_to_all | solution.py:150
  20.2 13.0 %collective-permute-start.7 = (bf16[192,512]{1,0:T(8,128)(2,1)S(1)}, bf16[192,512]{1,0:T(8,128)(2,1)S(1)}, u32[]{:S(2)}, u32[]{:S(2)}) collective-permute-start(bf16[192,512]{1,0:T(8,128)(2,1)S(1)} %broadcast_select_fusion), channel_id=1, source_target_pairs={{0,16},{4,20},{8,24},{12,28},{16,0},{20,4},{24,8},{28,12},{1,17},{... | collective-permute-start | bytes 589832 | tf_op jit(solution)/shard_map/ppermute | solution.py:133
  33.2 1.5 %collective-permute-start.8 = (bf16[192,512]{1,0:T(8,128)(2,1)S(1)}, bf16[192,512]{1,0:T(8,128)(2,1)S(1)}, u32[]{:S(2)}, u32[]{:S(2)}) collective-permute-start(bf16[192,512]{1,0:T(8,128)(2,1)S(1)} %broadcast_select_fusion.1.refs_2_), channel_id=1, source_target_pairs={{0,4},{4,0},{8,12},{12,8},{16,20},{20,16},{24,28},{28,24},{1,5},{5... | collective-permute-start | bytes 589832 | tf_op jit(solution)/shard_map/ppermute | solution.py:133
where the time goes:
time: 36.9 us; the launch traced here: 36.6 us
  waiting for transfers between devices  14.8 us (40%)
  starting transfers between devices  13.9 us (38%)
  Pallas kernels  5.09 us (14%)
  between operations  1.45 us (4%)
  local copies, waits for them, and re-layouts  1.21 us (3%)
    ppermute x9, waiting for transfers between devices, swap(): lax.ppermute(block, axis, [(i, i ^ mask) for i in range(lax.axis_size(axi...  14.8 us
    ppermute x9, starting transfers between devices, swap(): lax.ppermute(block, axis, [(i, i ^ mask) for i in range(lax.axis_size(axi...  10.2 us
    pallas_call x4, Pallas kernels, call(): pl.pallas_call(kernel, out_shape=shapes, in_specs=[pl.BlockSpec(memory_sp...  5.09 us
    all_to_all x1, starting transfers between devices, exchange(): lax.all_to_all(rows.reshape(groups, 2 * capacity, lanes), 'pts', split_ax...  3.72 us
    dynamic_slice x1, local copies, waits for them, and re-layouts, spread(): lax.dynamic_index_in_dim(sides, side, 1, keepdims=False)  1.12 us
  transfers between devices with their start and end apart: 10, of which 5 were waited for; matrix products, arithmetic and copies ran while one was open for 1% of the time, Pallas kernels for 9%

commit v1 on v0

--- a/solution.py
+++ b/solution.py
@@ -68,6 +68,14 @@
     keep_ref[...] = jnp.full(keep_ref.shape, place_ref[1], jnp.int32)
 
 
+def pick_kernel(keep_ref, mine_ref, met_ref, *refs):
+    refs[-1][...] = jnp.where(keep_ref[0] != 0, mine_ref[...], met_ref[...])
+
+
+def pass_kernel(block_ref, after_ref, out_ref):
+    out_ref[...] = block_ref[...]
+
+
 def rows_kernel(groups, capacity, points_ref, tags_ref, marks_ref, out_ref):
     marks = marks_ref.shape[0]
     no_tags = jnp.zeros(tags_ref.shape, jnp.bfloat16)
@@ -86,12 +94,16 @@
             out_ref[core, :, marks:] = tags
 
 
-def sums_kernel(scale, even_ref, odd_ref, mine_ref, other_ref, totals_ref, counts_ref, panel_ref):
+def sums_kernel(scale, even_ref, odd_ref, mine_ref, *refs):
+    others, (totals_ref, counts_ref, panel_ref) = refs[:-3], refs[-3:]
     slots, lanes = even_ref.shape
     owned, marks = totals_ref.shape[0], mine_ref.shape[0]
-    for side, half in enumerate((mine_ref, other_ref)):
-        panel_ref[side, :marks, :] = half[...]
-        panel_ref[side, marks:, :] = jnp.zeros((lanes - marks, half.shape[1]), jnp.bfloat16)
+    panel_ref[0, :marks, :] = mine_ref[...]
+    first = 0
+    for other in others:
+        panel_ref[1, first : first + other.shape[0], :] = other[...]
+        first += other.shape[0]
+    panel_ref[:, marks:, :] = jnp.zeros((2, lanes - marks, mine_ref.shape[1]), jnp.bfloat16)
     features = (
         jnp.dot(even_ref[...], panel_ref[0], preferred_element_type=jnp.float32)
         + jnp.dot(odd_ref[...], panel_ref[1], preferred_element_type=jnp.float32)
@@ -133,14 +145,17 @@
     return lax.ppermute(block, axis, [(i, i ^ mask) for i in range(lax.axis_size(axis))])
 
 
-def spread(panel, parts, holder):
-    me = lax.axis_index("pts")
+def pick(keep, mine, met, *after):
+    keep = keep.astype(jnp.int32).reshape(1)
+    return call(pick_kernel, array(mine.shape), mine, met, *after, place=keep)
+
+
+def sides_of(panel, parts, core):
     sides = panel.reshape(parts, 2, -1, panel.shape[1])
-    mine, other = (
+    return (
         lax.dynamic_index_in_dim(sides, side, 1, keepdims=False).reshape(-1, panel.shape[1])
-        for side in (me % 2, 1 - me % 2)
-    )
-    return jnp.where(((holder ^ me) & 1) == 0, mine, swap(other, "pts", 1))
+        for side in (core, 1 - core)
+    )
 
 
 def exchange(rows, groups, capacity):
@@ -167,21 +182,23 @@
     half = landmarks.shape[0] // 2
     lanes = -(-(depth // 2 + 2) // LANES) * LANES
     me = lax.axis_index("pts")
-    mine = lax.dynamic_slice_in_dim(landmarks, (me % 2) * half, half, 0)
-    halves = [mine] + [swap(mine, "lmk", mask) for mask in range(1, parts)]
+    marks = lax.dynamic_slice_in_dim(landmarks, (me % 2) * half, half, 0)
+    halves = [marks] + [swap(marks, "lmk", mask) for mask in range(1, parts)]
+    assignment = assignment.reshape(1, point_rows)
+    points_met, assignment_met = swap(points, "pts", 1), swap(assignment, "pts", 1)
     differs = panel_index[0] ^ me
-    panel = spread(panels[0], parts, panel_index[0])
+    mine, other = sides_of(panels[0], parts, me % 2)
+    panel = pick((differs & 1) == 0, mine, swap(other, "pts", 1), points_met, assignment_met)
     masks = [1 << bit for bit in range(1, groups.bit_length() - 1)]
     panel_met = swap(panel, "pts", masks[0])
     place = jnp.stack([lax.axis_index("lmk"), (differs & masks[0]) == 0]).astype(jnp.int32)
-    assignment = assignment.reshape(1, point_rows)
     placed, tags = call(
         lambda *refs: place_kernel(groups, capacity, *refs),
         (array((2, slots, width)), array((slots, lanes - depth // 2))),
         points,
         assignment,
-        swap(points, "pts", 1),
-        swap(assignment, "pts", 1),
+        points_met,
+        assignment_met,
     )
     marks, keep = call(
         marks_kernel,
@@ -200,6 +217,9 @@
     panel = jnp.where(keep != 0, panel, panel_met)
     for mask in masks[1:]:
         panel = jnp.where((differs & mask) == 0, panel, swap(panel, "pts", mask))
+    cut = panel.shape[0] // 2
+    others = [swap(panel[:cut], "pts", 1)]
+    others.append(swap(call(pass_kernel, array((cut, columns)), panel[cut:], others[0]), "pts", 1))
     even, odd = exchange(rows, groups, capacity)
     totals, counts = call(
         lambda *refs: sums_kernel(CLUSTERS / (point_rows * groups), *refs),
@@ -207,7 +227,7 @@
         even,
         odd,
         panel,
-        swap(panel, "pts", 1),
+        *others,
         scratch=[pltpu.VMEM((2, lanes, columns), jnp.bfloat16)],
     )
     return (totals, counts.reshape(owned))

time: 36.9 us -> 35.6 us (0.965)
  waiting for transfers between devices: 14.8 us -> 13.6 us
    ppermute x9 -> x10, waiting for transfers between devices: 14.8 us -> 4.46 us  [swap(): lax.ppermute(block, axis, [(i, i ^ mask) for i in range(lax.axis_size(axi...]
    all_to_all x1, waiting for transfers between devices: 0.01 us -> 9.15 us  [exchange(): lax.all_to_all(rows.reshape(groups, 2 * capacity, lanes), 'pts', split_ax...]
    ppermute x9 -> x10, starting transfers between devices: 10.2 us -> 10.3 us  [swap(): lax.ppermute(block, axis, [(i, i ^ mask) for i in range(lax.axis_size(axi...]
    pallas_call x4 -> x6, Pallas kernels: 5.09 us -> 5.13 us  [call(): pl.pallas_call(kernel, out_shape=shapes, in_specs=[pl.BlockSpec(memory_sp...]
  transfers between devices with their start and end apart: 10 -> 11, of which waited for: 5 -> 4; matrix products, arithmetic and copies ran while one was open for 1% -> 4% of each run, Pallas kernels for 9% -> 9%
where the time goes in v1:
time: 35.6 us; the launch traced here: 35.4 us
  starting transfers between devices  13.8 us (39%)
  waiting for transfers between devices  13.6 us (38%)
  Pallas kernels  5.13 us (14%)
  between operations  1.47 us (4%)
  local copies, waits for them, and re-layouts  1.14 us (3%)
    ppermute x10, starting transfers between devices, swap(): lax.ppermute(block, axis, [(i, i ^ mask) for i in range(lax.axis_size(axi...  10.3 us
    all_to_all x1, waiting for transfers between devices, exchange(): lax.all_to_all(rows.reshape(groups, 2 * capacity, lanes), 'pts', split_ax...  9.15 us
    pallas_call x6, Pallas kernels, call(): pl.pallas_call(kernel, out_shape=shapes, in_specs=[pl.BlockSpec(memory_sp...  5.13 us
    ppermute x10, waiting for transfers between devices, swap(): lax.ppermute(block, axis, [(i, i ^ mask) for i in range(lax.axis_size(axi...  4.46 us
    all_to_all x1, starting transfers between devices, exchange(): lax.all_to_all(rows.reshape(groups, 2 * capacity, lanes), 'pts', split_ax...  3.49 us
    dynamic_slice x1, local copies, waits for them, and re-layouts, sides_of(): lax.dynamic_index_in_dim(sides, side, 1, keepdims=False)  1.05 us
  transfers between devices with their start and end apart: 11, of which 4 were waited for; matrix products, arithmetic and copies ran while one was open for 4% of the time, Pallas kernels for 9%

profile of v1, /device:TPU:0, one launch (start us, length us, event | category | flops | bytes accessed | tf_op | source)
XLA Modules:
  0.0 35.4 jit_solution(10654110295717521298)
XLA Ops:
  0.6 0.0 copy-start
  0.7 0.0 copy-start.2
  0.7 0.5 %collective-permute-start = (bf16[256,768]{1,0:T(8,128)(2,1)}, bf16[256,768]{1,0:T(8,128)(2,1)S(1)}, u32[]{:S(2)}, u32[]{:S(2)}) collective-permute-start(bf16[256,768]{1,0:T(8,128)(2,1)} %refs_0_.1), channel_id=1, source_target_pairs={{0,4},{4,0},{8,12},{12,8},{16,20},{20,16},{24,28},{28,24},{1,5},{5... | collective-permute-start | bytes 1179656 | tf_op jit(solution)/shard_map/ppermute | solution.py:145
  1.2 1.0 %constant_dynamic-slice_fusion = (bf16[4,1,48,512]{3,2,1,0:T(8,128)(2,1)S(1)}, bf16[4,1,48,512]{3,2,1,0:T(8,128)(2,1)S(1)}) fusion(bf16[4,2,48,512]{3,2,1,0:T(8,128)(2,1)} %bitcast.26, s32[]{:T(128)S(6)} %select_n.39, s32[]{:T(128)S(6)} %select_n.38), kind=kLoop, calls=%fused_computation.5 | loop fusion | bytes 786440 | tf_op jit(solution)/shard_map/jit(dynamic_index_in_dim)/dynamic_slice | solution.py:156
  2.2 0.2 collective-permute-start.5
  2.4 0.4 %collective-permute-start.1 = (s32[1,256]{1,0:T(1,128)}, s32[1,256]{1,0:T(1,128)S(1)}, u32[]{:S(2)}, u32[]{:S(2)}) collective-permute-start(s32[1,256]{1,0:T(1,128)} %bitcast.23), channel_id=1, source_target_pairs={{0,4},{4,0},{8,12},{12,8},{16,20},{20,16},{24,28},{28,24},{1,5},{5... | collective-permute-start | bytes 3080 | tf_op jit(solution)/shard_map/ppermute | solution.py:145
  2.8 2.7 %collective-permute-start.2 = (bf16[48,768]{1,0:T(8,128)(2,1)S(1)}, bf16[48,768]{1,0:T(8,128)(2,1)S(1)}, u32[]{:S(2)}, u32[]{:S(2)}) collective-permute-start(bf16[48,768]{1,0:T(8,128)(2,1)S(1)} %constant_dynamic-slice_fusion.3.refs_0_), channel_id=1, source_target_pairs={{0,1},{1,0},{2,3},{3,2},{4,5},{5,4},{6,7},{7,6},{8,9},{9,8},{10,11... | collective-permute-start | bytes 221192 | tf_op jit(solution)/shard_map/ppermute | solution.py:145
  5.6 2.6 %collective-permute-start.3 = (bf16[48,768]{1,0:T(8,128)(2,1)S(1)}, bf16[48,768]{1,0:T(8,128)(2,1)S(1)}, u32[]{:S(2)}, u32[]{:S(2)}) collective-permute-start(bf16[48,768]{1,0:T(8,128)(2,1)S(1)} %constant_dynamic-slice_fusion.3.refs_0_), channel_id=1, source_target_pairs={{0,2},{1,3},{2,0},{3,1},{4,6},{5,7},{6,4},{7,5},{8,10},{9,11},{10,... | collective-permute-start | bytes 221192 | tf_op jit(solution)/shard_map/ppermute | solution.py:145
  8.8 0.1 collective-permute-start.4
  8.9 0.0 collective-permute-done.5.met_ref
  9.0 1.7 %collective-permute-start.6 = (bf16[192,512]{1,0:T(8,128)(2,1)S(1)}, bf16[192,512]{1,0:T(8,128)(2,1)S(1)}, u32[]{:S(2)}, u32[]{:S(2)}) collective-permute-start(bf16[192,512]{1,0:T(8,128)(2,1)S(1)} %shard_map.71), channel_id=1, source_target_pairs={{0,8},{4,12},{8,0},{12,4},{16,24},{20,28},{24,16},{28,20},{1,9},{5... | collective-permute-start | bytes 589832 | tf_op jit(solution)/shard_map/ppermute | solution.py:145
  10.7 0.1 pad_add_fusion.place_ref
  10.8 1.1 %shard_map.68 = (bf16[2,512,768]{2,1,0:T(8,128)(2,1)S(1)}, bf16[512,64]{1,0:T(8,128)(2,1)S(1)}) custom-call(bf16[256,768]{1,0:T(8,128)(2,1)S(1)} %copy-done.1, s32[1,256]{1,0:T(1,128)S(1)} %bitcast.24, bf16[256,768]{1,0:T(8,128)(2,1)S(1)} %collective-permute-done.refs_2_.refs_0_, s32[1,256]{1,0:T(1,128)S(1)} %collective-permute-done.1.refs_3_.refs_1_), custom_call_target="tpu_custom_call" | custom-call | tf_op jit(solution)/shard_map/pallas_call | solution.py:130
  11.9 0.5 %collective-permute-done.3.refs_2_ = bf16[48,768]{1,0:T(8,128)(2,1)S(1)} collective-permute-done((bf16[48,768]{1,0:T(8,128)(2,1)S(1)}, bf16[48,768]{1,0:T(8,128)(2,1)S(1)}, u32[]{:S(2)}, u32[]{:S(2)}) %collective-permute-start.3) | collective-permute-done | bytes 73760 | tf_op jit(solution)/shard_map/ppermute | solution.py:145
  12.5 2.6 %collective-permute-done.4.refs_3_ = bf16[48,768]{1,0:T(8,128)(2,1)S(1)} collective-permute-done((bf16[48,768]{1,0:T(8,128)(2,1)S(1)}, bf16[48,768]{1,0:T(8,128)(2,1)S(1)}, u32[]{:S(2)}, u32[]{:S(2)}) %collective-permute-start.4) | collective-permute-done | bytes 73760 | tf_op jit(solution)/shard_map/ppermute | solution.py:145
  15.1 0.7 %shard_map.69 = (bf16[192,768]{1,0:T(8,128)(2,1)S(1)}, s32[1,512]{1,0:T(1,128)S(1)}) custom-call(s32[2]{0:T(128)S(1)} %pad_add_fusion.place_ref, bf16[512,64]{1,0:T(8,128)(2,1)S(1)} %get-tuple-element.9.after_ref.refs_1_, bf16[48,768]{1,0:T(8,128)(2,1)S(1)} %constant_dynamic-slice_fusion.3.refs_0_, bf16[48,768]{1,0:T(8,128)(2,1)S(1)} %collective-permute-done.2.refs_1_, ...), custom_call_target="tpu_custom_call" | custom-call | tf_op jit(solution)/shard_map/pallas_call | solution.py:130
  15.9 1.6 %collective-permute-start.7 = (bf16[192,512]{1,0:T(8,128)(2,1)S(1)}, bf16[192,512]{1,0:T(8,128)(2,1)S(1)}, u32[]{:S(2)}, u32[]{:S(2)}) collective-permute-start(bf16[192,512]{1,0:T(8,128)(2,1)S(1)} %broadcast_select_fusion), channel_id=1, source_target_pairs={{0,16},{4,20},{8,24},{12,28},{16,0},{20,4},{24,8},{28,12},{1,17},{... | collective-permute-start | bytes 589832 | tf_op jit(solution)/shard_map/ppermute | solution.py:145
  17.4 1.4 %shard_map.70 = bf16[8,2,64,256]{3,2,1,0:T(8,128)(2,1)} custom-call(bf16[2,512,768]{2,1,0:T(8,128)(2,1)S(1)} %get-tuple-element.8.refs_0_, bf16[512,64]{1,0:T(8,128)(2,1)S(1)} %get-tuple-element.9.after_ref.refs_1_, bf16[192,768]{1,0:T(8,128)(2,1)S(1)} %get-tuple-element.10.refs_2_), custom_call_target="tpu_custom_call" | custom-call | tf_op jit(solution)/shard_map/pallas_call | solution.py:130
  18.9 3.5 %all-to-all-start = ((bf16[8,128,256]{2,1,0:T(8,128)(2,1)}), bf16[8,128,256]{2,1,0:T(8,128)(2,1)S(1)}, u32[]{:S(2)}, u32[]{:S(2)}) async-start(bf16[8,128,256]{2,1,0:T(8,128)(2,1)} %bitcast.4), calls=%async_computation | async-start | bytes 1048576 | tf_op jit(solution)/shard_map/all_to_all | solution.py:165
  22.4 0.5 %collective-permute-start.8 = (bf16[96,512]{1,0:T(8,128)(2,1)S(1)}, bf16[96,512]{1,0:T(8,128)(2,1)S(1)}, u32[]{:S(2)}, u32[]{:S(2)}) collective-permute-start(bf16[96,512]{1,0:T(8,128)(2,1)S(1)} %get-tuple-element.21), channel_id=1, source_target_pairs={{0,4},{4,0},{8,12},{12,8},{16,20},{20,16},{24,28},{28,24},{1,5},{5... | collective-permute-start | bytes 294920 | tf_op jit(solution)/shard_map/ppermute | solution.py:145
  22.9 9.2 %all-to-all-done = bf16[8,128,256]{2,1,0:T(8,128)(2,1)S(1)} async-done(((bf16[8,128,256]{2,1,0:T(8,128)(2,1)}), bf16[8,128,256]{2,1,0:T(8,128)(2,1)S(1)}, u32[]{:S(2)}, u32[]{:S(2)}) %all-to-all-start) | async-done | bytes 524320 | tf_op jit(solution)/shard_map/all_to_all | solution.py:165
  32.1 0.1 collective-permute-start.9
  32.2 1.3 %collective-permute-done.9.refs_4_ = bf16[96,512]{1,0:T(8,128)(2,1)S(1)} collective-permute-done((bf16[96,512]{1,0:T(8,128)(2,1)S(1)}, bf16[96,512]{1,0:T(8,128)(2,1)S(1)}, u32[]{:S(2)}, u32[]{:S(2)}) %collective-permute-start.9) | collective-permute-done | bytes 98336 | tf_op jit(solution)/shard_map/ppermute | solution.py:145
  33.5 1.9 %shard_map.73 = (f32[512,512]{1,0:T(8,128)}, s32[1,512]{1,0:T(1,128)}) custom-call(bf16[512,256]{1,0:T(8,128)(2,1)S(1)} %bitcast.20, bf16[512,256]{1,0:T(8,128)(2,1)S(1)} %bitcast.21, bf16[192,512]{1,0:T(8,128)(2,1)S(1)} %broadcast_select_fusion.1.refs_2_, bf16[96,512]{1,0:T(8,128)(2,1)S(1)} %collective-permute-done.8.after_ref.refs_3_, ...), custom_call_target="tpu_custom_call" | custom-call | tf_op jit(solution)/shard_map/pallas_call | solution.py:130
  (20 shorter events, 0.2 us)
Async XLA Ops:
  0.6 2.2 %copy-start = (bf16[96,768]{1,0:T(8,128)(2,1)S(1)}, bf16[96,768]{1,0:T(8,128)(2,1)}, u32[]{:S(2)}) copy-start(bf16[96,768]{1,0:T(8,128)(2,1)} %param.6) | copy-start | bytes 442372
  0.6 10.1 %copy-start.1 = (bf16[256,768]{1,0:T(8,128)(2,1)S(1)}, bf16[256,768]{1,0:T(8,128)(2,1)}, u32[]{:S(2)}) copy-start(bf16[256,768]{1,0:T(8,128)(2,1)} %refs_0_.1) | copy-start | bytes 1179652
  0.7 10.1 %copy-start.2 = (s32[256]{0:T(256)S(1)}, s32[256]{0:T(256)}, u32[]{:S(2)}) copy-start(s32[256]{0:T(256)} %param.9) | copy-start | bytes 3076
  0.7 8.3 %collective-permute-start = (bf16[256,768]{1,0:T(8,128)(2,1)}, bf16[256,768]{1,0:T(8,128)(2,1)S(1)}, u32[]{:S(2)}, u32[]{:S(2)}) collective-permute-start(bf16[256,768]{1,0:T(8,128)(2,1)} %refs_0_.1), channel_id=1, source_target_pairs={{0,4},{4,0},{8,12},{12,8},{16,20},{20,16},{24,28},{28,24},{1,5},{5... | collective-permute-start | bytes 1179656 | tf_op jit(solution)/shard_map/ppermute | solution.py:145
  2.2 6.7 %collective-permute-start.5 = (bf16[192,512]{1,0:T(8,128)(2,1)S(1)}, bf16[192,512]{1,0:T(8,128)(2,1)S(1)}, u32[]{:S(2)}, u32[]{:S(2)}) collective-permute-start(bf16[192,512]{1,0:T(8,128)(2,1)S(1)} %bitcast.27), channel_id=1, source_target_pairs={{0,4},{4,0},{8,12},{12,8},{16,20},{20,16},{24,28},{28,24},{1,5},{5... | collective-permute-start | bytes 589832 | tf_op jit(solution)/shard_map/ppermute | solution.py:145
  2.4 6.4 %collective-permute-start.1 = (s32[1,256]{1,0:T(1,128)}, s32[1,256]{1,0:T(1,128)S(1)}, u32[]{:S(2)}, u32[]{:S(2)}) collective-permute-start(s32[1,256]{1,0:T(1,128)} %bitcast.23), channel_id=1, source_target_pairs={{0,4},{4,0},{8,12},{12,8},{16,20},{20,16},{24,28},{28,24},{1,5},{5... | collective-permute-start | bytes 3080 | tf_op jit(solution)/shard_map/ppermute | solution.py:145
  2.8 9.1 %collective-permute-start.2 = (bf16[48,768]{1,0:T(8,128)(2,1)S(1)}, bf16[48,768]{1,0:T(8,128)(2,1)S(1)}, u32[]{:S(2)}, u32[]{:S(2)}) collective-permute-start(bf16[48,768]{1,0:T(8,128)(2,1)S(1)} %constant_dynamic-slice_fusion.3.refs_0_), channel_id=1, source_target_pairs={{0,1},{1,0},{2,3},{3,2},{4,5},{5,4},{6,7},{7,6},{8,9},{9,8},{10,11... | collective-permute-start | bytes 221192 | tf_op jit(solution)/shard_map/ppermute | solution.py:145
  5.6 6.9 %collective-permute-start.3 = (bf16[48,768]{1,0:T(8,128)(2,1)S(1)}, bf16[48,768]{1,0:T(8,128)(2,1)S(1)}, u32[]{:S(2)}, u32[]{:S(2)}) collective-permute-start(bf16[48,768]{1,0:T(8,128)(2,1)S(1)} %constant_dynamic-slice_fusion.3.refs_0_), channel_id=1, source_target_pairs={{0,2},{1,3},{2,0},{3,1},{4,6},{5,7},{6,4},{7,5},{8,10},{9,11},{10,... | collective-permute-start | bytes 221192 | tf_op jit(solution)/shard_map/ppermute | solution.py:145
  8.8 6.3 %collective-permute-start.4 = (bf16[48,768]{1,0:T(8,128)(2,1)S(1)}, bf16[48,768]{1,0:T(8,128)(2,1)S(1)}, u32[]{:S(2)}, u32[]{:S(2)}) collective-permute-start(bf16[48,768]{1,0:T(8,128)(2,1)S(1)} %constant_dynamic-slice_fusion.3.refs_0_), channel_id=1, source_target_pairs={{0,3},{1,2},{2,1},{3,0},{4,7},{5,6},{6,5},{7,4},{8,11},{9,10},{10,... | collective-permute-start | bytes 221192 | tf_op jit(solution)/shard_map/ppermute | solution.py:145
  9.0 6.9 %collective-permute-start.6 = (bf16[192,512]{1,0:T(8,128)(2,1)S(1)}, bf16[192,512]{1,0:T(8,128)(2,1)S(1)}, u32[]{:S(2)}, u32[]{:S(2)}) collective-permute-start(bf16[192,512]{1,0:T(8,128)(2,1)S(1)} %shard_map.71), channel_id=1, source_target_pairs={{0,8},{4,12},{8,0},{12,4},{16,24},{20,28},{24,16},{28,20},{1,9},{5... | collective-permute-start | bytes 589832 | tf_op jit(solution)/shard_map/ppermute | solution.py:145
  15.9 6.5 %collective-permute-start.7 = (bf16[192,512]{1,0:T(8,128)(2,1)S(1)}, bf16[192,512]{1,0:T(8,128)(2,1)S(1)}, u32[]{:S(2)}, u32[]{:S(2)}) collective-permute-start(bf16[192,512]{1,0:T(8,128)(2,1)S(1)} %broadcast_select_fusion), channel_id=1, source_target_pairs={{0,16},{4,20},{8,24},{12,28},{16,0},{20,4},{24,8},{28,12},{1,17},{... | collective-permute-start | bytes 589832 | tf_op jit(solution)/shard_map/ppermute | solution.py:145
  18.9 13.2 %all-to-all-start = ((bf16[8,128,256]{2,1,0:T(8,128)(2,1)}), bf16[8,128,256]{2,1,0:T(8,128)(2,1)S(1)}, u32[]{:S(2)}, u32[]{:S(2)}) async-start(bf16[8,128,256]{2,1,0:T(8,128)(2,1)} %bitcast.4), calls=%async_computation | async-start | bytes 1048576 | tf_op jit(solution)/shard_map/all_to_all | solution.py:165
  22.4 9.7 %collective-permute-start.8 = (bf16[96,512]{1,0:T(8,128)(2,1)S(1)}, bf16[96,512]{1,0:T(8,128)(2,1)S(1)}, u32[]{:S(2)}, u32[]{:S(2)}) collective-permute-start(bf16[96,512]{1,0:T(8,128)(2,1)S(1)} %get-tuple-element.21), channel_id=1, source_target_pairs={{0,4},{4,0},{8,12},{12,8},{16,20},{20,16},{24,28},{28,24},{1,5},{5... | collective-permute-start | bytes 294920 | tf_op jit(solution)/shard_map/ppermute | solution.py:145
  32.1 1.4 %collective-permute-start.9 = (bf16[96,512]{1,0:T(8,128)(2,1)S(1)}, bf16[96,512]{1,0:T(8,128)(2,1)S(1)}, u32[]{:S(2)}, u32[]{:S(2)}) collective-permute-start(bf16[96,512]{1,0:T(8,128)(2,1)S(1)} %shard_map.72), channel_id=1, source_target_pairs={{0,4},{4,0},{8,12},{12,8},{16,20},{20,16},{24,28},{28,24},{1,5},{5... | collective-permute-start | bytes 294920 | tf_op jit(solution)/shard_map/ppermute | solution.py:145

commit v2 on v1

--- a/solution.py
+++ b/solution.py
@@ -95,7 +95,7 @@
 
 
 def sums_kernel(scale, even_ref, odd_ref, mine_ref, *refs):
-    others, (totals_ref, counts_ref, panel_ref) = refs[:-3], refs[-3:]
+    others, (totals_ref, counts_ref, panel_ref, sums_ref, sems) = refs[:-5], refs[-5:]
     slots, lanes = even_ref.shape
     owned, marks = totals_ref.shape[0], mine_ref.shape[0]
     panel_ref[0, :marks, :] = mine_ref[...]
@@ -118,20 +118,31 @@
         .astype(jnp.float32)
         .astype(jnp.bfloat16)
     )
-    totals_ref[...] = jnp.dot(member, features, preferred_element_type=jnp.float32) * scale
+    chunks = sums_ref.shape[0]
+    size = owned // chunks
+    copies = []
+    for at in range(chunks):
+        here = slice(at * size, (at + 1) * size)
+        sums_ref[at] = jnp.dot(member[here], features, preferred_element_type=jnp.float32) * scale
+        copies.append(pltpu.make_async_copy(sums_ref.at[at], totals_ref.at[here, :], sems.at[at]))
+        copies[-1].start()
     counts_ref[...] = lax.dot_general(
         jnp.ones((8, slots), jnp.bfloat16), member, NT, preferred_element_type=jnp.float32
     )[:1].astype(jnp.int32)
-
-
-def call(kernel, shapes, *operands, place=None, scratch=()):
-    held = pl.BlockSpec(memory_space=pltpu.VMEM)
+    for copy in copies:
+        copy.wait()
+
+
+def call(kernel, shapes, *operands, place=None, scratch=(), sent=()):
+    held, loose = pl.BlockSpec(memory_space=pltpu.VMEM), pl.BlockSpec(memory_space=pl.ANY)
     first = [] if place is None else [place]
     return pl.pallas_call(
         kernel,
         out_shape=shapes,
         in_specs=[pl.BlockSpec(memory_space=pltpu.SMEM)] * len(first) + [held] * len(operands),
-        out_specs=(held,) * len(shapes) if isinstance(shapes, tuple) else held,
+        out_specs=tuple(loose if at in sent else held for at in range(len(shapes)))
+        if isinstance(shapes, tuple)
+        else held,
         scratch_shapes=scratch,
         compiler_params=pltpu.CompilerParams(vmem_limit_bytes=VMEM_LIMIT),
     )(*first, *operands)
@@ -217,10 +228,11 @@
     panel = jnp.where(keep != 0, panel, panel_met)
     for mask in masks[1:]:
         panel = jnp.where((differs & mask) == 0, panel, swap(panel, "pts", mask))
-    cut = panel.shape[0] // 2
+    cut = min(16, panel.shape[0] // 2)
     others = [swap(panel[:cut], "pts", 1)]
-    others.append(swap(call(pass_kernel, array((cut, columns)), panel[cut:], others[0]), "pts", 1))
+    others.append(swap(call(pass_kernel, array((panel.shape[0] - cut, columns)), panel[cut:], others[0]), "pts", 1))
     even, odd = exchange(rows, groups, capacity)
+    chunks = max(1, owned // LANES)
     totals, counts = call(
         lambda *refs: sums_kernel(CLUSTERS / (point_rows * groups), *refs),
         (array((owned, columns), jnp.float32), array((1, owned), jnp.int32)),
@@ -228,7 +240,12 @@
         odd,
         panel,
         *others,
-        scratch=[pltpu.VMEM((2, lanes, columns), jnp.bfloat16)],
+        scratch=[
+            pltpu.VMEM((2, lanes, columns), jnp.bfloat16),
+            pltpu.VMEM((chunks, owned // chunks, columns), jnp.float32),
+            pltpu.SemaphoreType.DMA((chunks,)),
+        ],
+        sent=(0,),
     )
     return (totals, counts.reshape(owned))
 

time: 35.6 us -> 39.3 us (1.10)
  waiting for transfers between devices: 13.6 us -> 16.4 us
  starting transfers between devices: 13.8 us -> 14.4 us
    ppermute x10, waiting for transfers between devices: 4.46 us -> 16.4 us  [swap(): lax.ppermute(block, axis, [(i, i ^ mask) for i in range(lax.axis_size(axi...]
    all_to_all x1, waiting for transfers between devices: 9.15 us -> 0.01 us  [exchange(): lax.all_to_all(rows.reshape(groups, 2 * capacity, lanes), 'pts', split_ax...]
  transfers between devices with their start and end apart: 11 -> 11, of which waited for: 4 -> 5; matrix products, arithmetic and copies ran while one was open for 4% -> 3% of each run, Pallas kernels for 9% -> 8%
where the time goes in v2:
time: 39.3 us; the launch traced here: 39 us
  waiting for transfers between devices  16.4 us (42%)
  starting transfers between devices  14.4 us (37%)
  Pallas kernels  5.51 us (14%)
  between operations  1.45 us (4%)
  local copies, waits for them, and re-layouts  1.14 us (3%)
    ppermute x10, waiting for transfers between devices, swap(): lax.ppermute(block, axis, [(i, i ^ mask) for i in range(lax.axis_size(axi...  16.4 us
    ppermute x10, starting transfers between devices, swap(): lax.ppermute(block, axis, [(i, i ^ mask) for i in range(lax.axis_size(axi...  10.6 us
    pallas_call x6, Pallas kernels, call(): pl.pallas_call(kernel, out_shape=shapes, in_specs=[pl.BlockSpec(memory_sp...  5.51 us
    all_to_all x1, starting transfers between devices, exchange(): lax.all_to_all(rows.reshape(groups, 2 * capacity, lanes), 'pts', split_ax...  3.74 us
    dynamic_slice x1, local copies, waits for them, and re-layouts, sides_of(): lax.dynamic_index_in_dim(sides, side, 1, keepdims=False)  1.05 us
  transfers between devices with their start and end apart: 11, of which 5 were waited for; matrix products, arithmetic and copies ran while one was open for 3% of the time, Pallas kernels for 8%

profile of v2, /device:TPU:0, one launch (start us, length us, event | category | flops | bytes accessed | tf_op | source)
XLA Modules:
  0.0 39.0 jit_solution(1275408499034385494)
XLA Ops:
  0.6 0.0 copy-start
  0.7 0.0 copy-start.2
  0.7 0.5 %collective-permute-start = (bf16[256,768]{1,0:T(8,128)(2,1)}, bf16[256,768]{1,0:T(8,128)(2,1)S(1)}, u32[]{:S(2)}, u32[]{:S(2)}) collective-permute-start(bf16[256,768]{1,0:T(8,128)(2,1)} %refs_0_.1), channel_id=1, source_target_pairs={{0,4},{4,0},{8,12},{12,8},{16,20},{20,16},{24,28},{28,24},{1,5},{5... | collective-permute-start | bytes 1179656 | tf_op jit(solution)/shard_map/ppermute | solution.py:156
  1.2 1.0 %constant_dynamic-slice_fusion = (bf16[4,1,48,512]{3,2,1,0:T(8,128)(2,1)S(1)}, bf16[4,1,48,512]{3,2,1,0:T(8,128)(2,1)S(1)}) fusion(bf16[4,2,48,512]{3,2,1,0:T(8,128)(2,1)} %bitcast.26, s32[]{:T(128)S(6)} %select_n.39, s32[]{:T(128)S(6)} %select_n.38), kind=kLoop, calls=%fused_computation.5 | loop fusion | bytes 786440 | tf_op jit(solution)/shard_map/jit(dynamic_index_in_dim)/dynamic_slice | solution.py:167
  2.2 0.2 collective-permute-start.5
  2.4 0.4 %collective-permute-start.1 = (s32[1,256]{1,0:T(1,128)}, s32[1,256]{1,0:T(1,128)S(1)}, u32[]{:S(2)}, u32[]{:S(2)}) collective-permute-start(s32[1,256]{1,0:T(1,128)} %bitcast.23), channel_id=1, source_target_pairs={{0,4},{4,0},{8,12},{12,8},{16,20},{20,16},{24,28},{28,24},{1,5},{5... | collective-permute-start | bytes 3080 | tf_op jit(solution)/shard_map/ppermute | solution.py:156
  2.8 2.7 %collective-permute-start.2 = (bf16[48,768]{1,0:T(8,128)(2,1)S(1)}, bf16[48,768]{1,0:T(8,128)(2,1)S(1)}, u32[]{:S(2)}, u32[]{:S(2)}) collective-permute-start(bf16[48,768]{1,0:T(8,128)(2,1)S(1)} %constant_dynamic-slice_fusion.3.refs_0_), channel_id=1, source_target_pairs={{0,1},{1,0},{2,3},{3,2},{4,5},{5,4},{6,7},{7,6},{8,9},{9,8},{10,11... | collective-permute-start | bytes 221192 | tf_op jit(solution)/shard_map/ppermute | solution.py:156
  5.6 2.6 %collective-permute-start.3 = (bf16[48,768]{1,0:T(8,128)(2,1)S(1)}, bf16[48,768]{1,0:T(8,128)(2,1)S(1)}, u32[]{:S(2)}, u32[]{:S(2)}) collective-permute-start(bf16[48,768]{1,0:T(8,128)(2,1)S(1)} %constant_dynamic-slice_fusion.3.refs_0_), channel_id=1, source_target_pairs={{0,2},{1,3},{2,0},{3,1},{4,6},{5,7},{6,4},{7,5},{8,10},{9,11},{10,... | collective-permute-start | bytes 221192 | tf_op jit(solution)/shard_map/ppermute | solution.py:156
  8.8 0.1 collective-permute-start.4
  9.0 1.7 %collective-permute-start.6 = (bf16[192,512]{1,0:T(8,128)(2,1)S(1)}, bf16[192,512]{1,0:T(8,128)(2,1)S(1)}, u32[]{:S(2)}, u32[]{:S(2)}) collective-permute-start(bf16[192,512]{1,0:T(8,128)(2,1)S(1)} %shard_map.71), channel_id=1, source_target_pairs={{0,8},{4,12},{8,0},{12,4},{16,24},{20,28},{24,16},{28,20},{1,9},{5... | collective-permute-start | bytes 589832 | tf_op jit(solution)/shard_map/ppermute | solution.py:156
  10.7 0.1 pad_add_fusion.place_ref
  10.8 1.1 %shard_map.68 = (bf16[2,512,768]{2,1,0:T(8,128)(2,1)S(1)}, bf16[512,64]{1,0:T(8,128)(2,1)S(1)}) custom-call(bf16[256,768]{1,0:T(8,128)(2,1)S(1)} %copy-done.1, s32[1,256]{1,0:T(1,128)S(1)} %bitcast.24, bf16[256,768]{1,0:T(8,128)(2,1)S(1)} %collective-permute-done.refs_2_.refs_0_, s32[1,256]{1,0:T(1,128)S(1)} %collective-permute-done.1.refs_3_.refs_1_), custom_call_target="tpu_custom_call" | custom-call | tf_op jit(solution)/shard_map/pallas_call | solution.py:139
  11.9 0.5 %collective-permute-done.3.refs_2_ = bf16[48,768]{1,0:T(8,128)(2,1)S(1)} collective-permute-done((bf16[48,768]{1,0:T(8,128)(2,1)S(1)}, bf16[48,768]{1,0:T(8,128)(2,1)S(1)}, u32[]{:S(2)}, u32[]{:S(2)}) %collective-permute-start.3) | collective-permute-done | bytes 73760 | tf_op jit(solution)/shard_map/ppermute | solution.py:156
  12.5 2.6 %collective-permute-done.4.refs_3_ = bf16[48,768]{1,0:T(8,128)(2,1)S(1)} collective-permute-done((bf16[48,768]{1,0:T(8,128)(2,1)S(1)}, bf16[48,768]{1,0:T(8,128)(2,1)S(1)}, u32[]{:S(2)}, u32[]{:S(2)}) %collective-permute-start.4) | collective-permute-done | bytes 73760 | tf_op jit(solution)/shard_map/ppermute | solution.py:156
  15.1 0.7 %shard_map.69 = (bf16[192,768]{1,0:T(8,128)(2,1)S(1)}, s32[1,512]{1,0:T(1,128)S(1)}) custom-call(s32[2]{0:T(128)S(1)} %pad_add_fusion.place_ref, bf16[512,64]{1,0:T(8,128)(2,1)S(1)} %get-tuple-element.9.after_ref.refs_1_, bf16[48,768]{1,0:T(8,128)(2,1)S(1)} %constant_dynamic-slice_fusion.3.refs_0_, bf16[48,768]{1,0:T(8,128)(2,1)S(1)} %collective-permute-done.2.refs_1_, ...), custom_call_target="tpu_custom_call" | custom-call | tf_op jit(solution)/shard_map/pallas_call | solution.py:139
  15.8 1.4 %shard_map.70 = bf16[8,2,64,256]{3,2,1,0:T(8,128)(2,1)} custom-call(bf16[2,512,768]{2,1,0:T(8,128)(2,1)S(1)} %get-tuple-element.8.refs_0_, bf16[512,64]{1,0:T(8,128)(2,1)S(1)} %get-tuple-element.9.after_ref.refs_1_, bf16[192,768]{1,0:T(8,128)(2,1)S(1)} %get-tuple-element.10.refs_2_), custom_call_target="tpu_custom_call" | custom-call | tf_op jit(solution)/shard_map/pallas_call | solution.py:139
  17.2 3.7 %all-to-all-start = ((bf16[8,128,256]{2,1,0:T(8,128)(2,1)}), bf16[8,128,256]{2,1,0:T(8,128)(2,1)S(1)}, u32[]{:S(2)}, u32[]{:S(2)}) async-start(bf16[8,128,256]{2,1,0:T(8,128)(2,1)} %bitcast.4), calls=%async_computation | async-start | bytes 1048576 | tf_op jit(solution)/shard_map/all_to_all | solution.py:176
  21.0 2.1 %collective-permute-start.7 = (bf16[192,512]{1,0:T(8,128)(2,1)S(1)}, bf16[192,512]{1,0:T(8,128)(2,1)S(1)}, u32[]{:S(2)}, u32[]{:S(2)}) collective-permute-start(bf16[192,512]{1,0:T(8,128)(2,1)S(1)} %broadcast_select_fusion), channel_id=1, source_target_pairs={{0,16},{4,20},{8,24},{12,28},{16,0},{20,4},{24,8},{28,12},{1,17},{... | collective-permute-start | bytes 589832 | tf_op jit(solution)/shard_map/ppermute | solution.py:156
  23.1 10.9 %collective-permute-done.7 = bf16[192,512]{1,0:T(8,128)(2,1)S(1)} collective-permute-done((bf16[192,512]{1,0:T(8,128)(2,1)S(1)}, bf16[192,512]{1,0:T(8,128)(2,1)S(1)}, u32[]{:S(2)}, u32[]{:S(2)}) %collective-permute-start.7) | collective-permute-done | bytes 196640 | tf_op jit(solution)/shard_map/ppermute | solution.py:156
  34.0 0.1 collective-permute-start.8
  34.1 1.1 %collective-permute-done.8.after_ref.refs_3_ = bf16[16,512]{1,0:T(8,128)(2,1)S(1)} collective-permute-done((bf16[16,512]{1,0:T(8,128)(2,1)S(1)}, bf16[16,512]{1,0:T(8,128)(2,1)S(1)}, u32[]{:S(2)}, u32[]{:S(2)}) %collective-permute-start.8) | collective-permute-done | bytes 16416 | tf_op jit(solution)/shard_map/ppermute | solution.py:156
  35.3 0.2 collective-permute-start.9
  35.6 1.2 %collective-permute-done.9.refs_4_ = bf16[176,512]{1,0:T(8,128)(2,1)S(1)} collective-permute-done((bf16[176,512]{1,0:T(8,128)(2,1)S(1)}, bf16[176,512]{1,0:T(8,128)(2,1)S(1)}, u32[]{:S(2)}, u32[]{:S(2)}) %collective-permute-start.9) | collective-permute-done | bytes 180256 | tf_op jit(solution)/shard_map/ppermute | solution.py:156
  36.8 2.3 %shard_map.73 = (f32[512,512]{1,0:T(8,128)}, s32[1,512]{1,0:T(1,128)}) custom-call(bf16[512,256]{1,0:T(8,128)(2,1)S(1)} %bitcast.20, bf16[512,256]{1,0:T(8,128)(2,1)S(1)} %bitcast.21, bf16[192,512]{1,0:T(8,128)(2,1)S(1)} %broadcast_select_fusion.1.refs_2_, bf16[16,512]{1,0:T(8,128)(2,1)S(1)} %collective-permute-done.8.after_ref.refs_3_, ...), custom_call_target="tpu_custom_call" | custom-call | tf_op jit(solution)/shard_map/pallas_call | solution.py:139
  (21 shorter events, 0.2 us)
Async XLA Ops:
  0.6 2.2 %copy-start = (bf16[96,768]{1,0:T(8,128)(2,1)S(1)}, bf16[96,768]{1,0:T(8,128)(2,1)}, u32[]{:S(2)}) copy-start(bf16[96,768]{1,0:T(8,128)(2,1)} %param.6) | copy-start | bytes 442372
  0.6 10.1 %copy-start.1 = (bf16[256,768]{1,0:T(8,128)(2,1)S(1)}, bf16[256,768]{1,0:T(8,128)(2,1)}, u32[]{:S(2)}) copy-start(bf16[256,768]{1,0:T(8,128)(2,1)} %refs_0_.1) | copy-start | bytes 1179652
  0.7 10.1 %copy-start.2 = (s32[256]{0:T(256)S(1)}, s32[256]{0:T(256)}, u32[]{:S(2)}) copy-start(s32[256]{0:T(256)} %param.9) | copy-start | bytes 3076
  0.7 8.3 %collective-permute-start = (bf16[256,768]{1,0:T(8,128)(2,1)}, bf16[256,768]{1,0:T(8,128)(2,1)S(1)}, u32[]{:S(2)}, u32[]{:S(2)}) collective-permute-start(bf16[256,768]{1,0:T(8,128)(2,1)} %refs_0_.1), channel_id=1, source_target_pairs={{0,4},{4,0},{8,12},{12,8},{16,20},{20,16},{24,28},{28,24},{1,5},{5... | collective-permute-start | bytes 1179656 | tf_op jit(solution)/shard_map/ppermute | solution.py:156
  2.2 6.7 %collective-permute-start.5 = (bf16[192,512]{1,0:T(8,128)(2,1)S(1)}, bf16[192,512]{1,0:T(8,128)(2,1)S(1)}, u32[]{:S(2)}, u32[]{:S(2)}) collective-permute-start(bf16[192,512]{1,0:T(8,128)(2,1)S(1)} %bitcast.27), channel_id=1, source_target_pairs={{0,4},{4,0},{8,12},{12,8},{16,20},{20,16},{24,28},{28,24},{1,5},{5... | collective-permute-start | bytes 589832 | tf_op jit(solution)/shard_map/ppermute | solution.py:156
  2.4 6.4 %collective-permute-start.1 = (s32[1,256]{1,0:T(1,128)}, s32[1,256]{1,0:T(1,128)S(1)}, u32[]{:S(2)}, u32[]{:S(2)}) collective-permute-start(s32[1,256]{1,0:T(1,128)} %bitcast.23), channel_id=1, source_target_pairs={{0,4},{4,0},{8,12},{12,8},{16,20},{20,16},{24,28},{28,24},{1,5},{5... | collective-permute-start | bytes 3080 | tf_op jit(solution)/shard_map/ppermute | solution.py:156
  2.8 9.1 %collective-permute-start.2 = (bf16[48,768]{1,0:T(8,128)(2,1)S(1)}, bf16[48,768]{1,0:T(8,128)(2,1)S(1)}, u32[]{:S(2)}, u32[]{:S(2)}) collective-permute-start(bf16[48,768]{1,0:T(8,128)(2,1)S(1)} %constant_dynamic-slice_fusion.3.refs_0_), channel_id=1, source_target_pairs={{0,1},{1,0},{2,3},{3,2},{4,5},{5,4},{6,7},{7,6},{8,9},{9,8},{10,11... | collective-permute-start | bytes 221192 | tf_op jit(solution)/shard_map/ppermute | solution.py:156
  5.6 6.9 %collective-permute-start.3 = (bf16[48,768]{1,0:T(8,128)(2,1)S(1)}, bf16[48,768]{1,0:T(8,128)(2,1)S(1)}, u32[]{:S(2)}, u32[]{:S(2)}) collective-permute-start(bf16[48,768]{1,0:T(8,128)(2,1)S(1)} %constant_dynamic-slice_fusion.3.refs_0_), channel_id=1, source_target_pairs={{0,2},{1,3},{2,0},{3,1},{4,6},{5,7},{6,4},{7,5},{8,10},{9,11},{10,... | collective-permute-start | bytes 221192 | tf_op jit(solution)/shard_map/ppermute | solution.py:156
  8.8 6.3 %collective-permute-start.4 = (bf16[48,768]{1,0:T(8,128)(2,1)S(1)}, bf16[48,768]{1,0:T(8,128)(2,1)S(1)}, u32[]{:S(2)}, u32[]{:S(2)}) collective-permute-start(bf16[48,768]{1,0:T(8,128)(2,1)S(1)} %constant_dynamic-slice_fusion.3.refs_0_), channel_id=1, source_target_pairs={{0,3},{1,2},{2,1},{3,0},{4,7},{5,6},{6,5},{7,4},{8,11},{9,10},{10,... | collective-permute-start | bytes 221192 | tf_op jit(solution)/shard_map/ppermute | solution.py:156
  9.0 12.0 %collective-permute-start.6 = (bf16[192,512]{1,0:T(8,128)(2,1)S(1)}, bf16[192,512]{1,0:T(8,128)(2,1)S(1)}, u32[]{:S(2)}, u32[]{:S(2)}) collective-permute-start(bf16[192,512]{1,0:T(8,128)(2,1)S(1)} %shard_map.71), channel_id=1, source_target_pairs={{0,8},{4,12},{8,0},{12,4},{16,24},{20,28},{24,16},{28,20},{1,9},{5... | collective-permute-start | bytes 589832 | tf_op jit(solution)/shard_map/ppermute | solution.py:156
  17.2 18.3 %all-to-all-start = ((bf16[8,128,256]{2,1,0:T(8,128)(2,1)}), bf16[8,128,256]{2,1,0:T(8,128)(2,1)S(1)}, u32[]{:S(2)}, u32[]{:S(2)}) async-start(bf16[8,128,256]{2,1,0:T(8,128)(2,1)} %bitcast.4), calls=%async_computation | async-start | bytes 1048576 | tf_op jit(solution)/shard_map/all_to_all | solution.py:176
  21.0 13.0 %collective-permute-start.7 = (bf16[192,512]{1,0:T(8,128)(2,1)S(1)}, bf16[192,512]{1,0:T(8,128)(2,1)S(1)}, u32[]{:S(2)}, u32[]{:S(2)}) collective-permute-start(bf16[192,512]{1,0:T(8,128)(2,1)S(1)} %broadcast_select_fusion), channel_id=1, source_target_pairs={{0,16},{4,20},{8,24},{12,28},{16,0},{20,4},{24,8},{28,12},{1,17},{... | collective-permute-start | bytes 589832 | tf_op jit(solution)/shard_map/ppermute | solution.py:156
  34.0 1.2 %collective-permute-start.8 = (bf16[16,512]{1,0:T(8,128)(2,1)S(1)}, bf16[16,512]{1,0:T(8,128)(2,1)S(1)}, u32[]{:S(2)}, u32[]{:S(2)}) collective-permute-start(bf16[16,512]{1,0:T(8,128)(2,1)S(1)} %slice.18), channel_id=1, source_target_pairs={{0,4},{4,0},{8,12},{12,8},{16,20},{20,16},{24,28},{28,24},{1,5},{5... | collective-permute-start | bytes 49160 | tf_op jit(solution)/shard_map/ppermute | solution.py:156
  35.3 1.5 %collective-permute-start.9 = (bf16[176,512]{1,0:T(8,128)(2,1)S(1)}, bf16[176,512]{1,0:T(8,128)(2,1)S(1)}, u32[]{:S(2)}, u32[]{:S(2)}) collective-permute-start(bf16[176,512]{1,0:T(8,128)(2,1)S(1)} %shard_map.72), channel_id=1, source_target_pairs={{0,4},{4,0},{8,12},{12,8},{16,20},{20,16},{24,28},{28,24},{1,5},{5... | collective-permute-start | bytes 540680 | tf_op jit(solution)/shard_map/ppermute | solution.py:156

commit v3 on v1

--- a/solution.py
+++ b/solution.py
@@ -68,8 +68,12 @@
     keep_ref[...] = jnp.full(keep_ref.shape, place_ref[1], jnp.int32)
 
 
-def pick_kernel(keep_ref, mine_ref, met_ref, *refs):
-    refs[-1][...] = jnp.where(keep_ref[0] != 0, mine_ref[...], met_ref[...])
+def pick_kernel(place_ref, mine_ref, met_ref, *refs):
+    out_ref, half = refs[-1], mine_ref.shape[2]
+    for part in range(mine_ref.shape[0]):
+        out_ref[part * half : (part + 1) * half, :] = jnp.where(
+            place_ref[0] != 0, mine_ref[part, place_ref[1]], met_ref[part, place_ref[1]]
+        )
 
 
 def pass_kernel(block_ref, after_ref, out_ref):
@@ -145,19 +149,6 @@
     return lax.ppermute(block, axis, [(i, i ^ mask) for i in range(lax.axis_size(axis))])
 
 
-def pick(keep, mine, met, *after):
-    keep = keep.astype(jnp.int32).reshape(1)
-    return call(pick_kernel, array(mine.shape), mine, met, *after, place=keep)
-
-
-def sides_of(panel, parts, core):
-    sides = panel.reshape(parts, 2, -1, panel.shape[1])
-    return (
-        lax.dynamic_index_in_dim(sides, side, 1, keepdims=False).reshape(-1, panel.shape[1])
-        for side in (core, 1 - core)
-    )
-
-
 def exchange(rows, groups, capacity):
     slots, lanes = groups * capacity, rows.shape[-1]
     if rows.ndim == 3:
@@ -187,8 +178,16 @@
     assignment = assignment.reshape(1, point_rows)
     points_met, assignment_met = swap(points, "pts", 1), swap(assignment, "pts", 1)
     differs = panel_index[0] ^ me
-    mine, other = sides_of(panels[0], parts, me % 2)
-    panel = pick((differs & 1) == 0, mine, swap(other, "pts", 1), points_met, assignment_met)
+    panel_met = swap(panels[0], "pts", 1)
+    panel = call(
+        pick_kernel,
+        array((depth // 2, columns)),
+        panels.reshape(parts, 2, half, columns),
+        panel_met.reshape(parts, 2, half, columns),
+        points_met,
+        assignment_met,
+        place=jnp.stack([(differs & 1) == 0, me % 2]).astype(jnp.int32),
+    )
     masks = [1 << bit for bit in range(1, groups.bit_length() - 1)]
     panel_met = swap(panel, "pts", masks[0])
     place = jnp.stack([lax.axis_index("lmk"), (differs & masks[0]) == 0]).astype(jnp.int32)

time: 35.6 us -> 36.9 us (1.037)
  local copies, waits for them, and re-layouts: 1.14 us -> 2.05 us
  Pallas kernels: 5.13 us -> 5.65 us
    unnamed x6 -> x8, local copies, waits for them, and re-layouts: 0.02 us -> 1.98 us
    dynamic_slice x1 -> x0, local copies, waits for them, and re-layouts: 1.05 us -> none  [sides_of(): lax.dynamic_index_in_dim(sides, side, 1, keepdims=False)]
    pallas_call x6, Pallas kernels: 5.13 us -> 5.65 us  [call(): pl.pallas_call(kernel, out_shape=shapes, in_specs=[pl.BlockSpec(memory_sp...]
  transfers between devices with their start and end apart: 11 -> 11, of which waited for: 4 -> 4; matrix products, arithmetic and copies ran while one was open for 4% -> 1% of each run, Pallas kernels for 9% -> 10%
where the time goes in v3:
time: 36.9 us; the launch traced here: 36.6 us
  starting transfers between devices  13.7 us (37%)
  waiting for transfers between devices  13.5 us (37%)
  Pallas kernels  5.65 us (15%)
  local copies, waits for them, and re-layouts  2.05 us (6%)
  between operations  1.44 us (4%)
    ppermute x10, starting transfers between devices, swap(): lax.ppermute(block, axis, [(i, i ^ mask) for i in range(lax.axis_size(axi...  10.2 us
    all_to_all x1, waiting for transfers between devices, exchange(): lax.all_to_all(rows.reshape(groups, 2 * capacity, lanes), 'pts', split_ax...  9.15 us
    pallas_call x6, Pallas kernels, call(): pl.pallas_call(kernel, out_shape=shapes, in_specs=[pl.BlockSpec(memory_sp...  5.65 us
    ppermute x10, waiting for transfers between devices, swap(): lax.ppermute(block, axis, [(i, i ^ mask) for i in range(lax.axis_size(axi...  4.34 us
    all_to_all x1, starting transfers between devices, exchange(): lax.all_to_all(rows.reshape(groups, 2 * capacity, lanes), 'pts', split_ax...  3.49 us
    unnamed x8, local copies, waits for them, and re-layouts  1.98 us
  transfers between devices with their start and end apart: 11, of which 4 were waited for; matrix products, arithmetic and copies ran while one was open for 1% of the time, Pallas kernels for 10%

profile of v3, /device:TPU:0, one launch (start us, length us, event | category | flops | bytes accessed | tf_op | source)
XLA Modules:
  0.0 36.6 jit_solution(9261380561400902434)
XLA Ops:
  0.6 0.0 copy-start
  0.7 0.5 %collective-permute-start.5 = (bf16[384,512]{1,0:T(8,128)(2,1)}, bf16[384,512]{1,0:T(8,128)(2,1)S(1)}, u32[]{:S(2)}, u32[]{:S(2)}) collective-permute-start(bf16[384,512]{1,0:T(8,128)(2,1)} %bitcast.19), channel_id=1, source_target_pairs={{0,4},{4,0},{8,12},{12,8},{16,20},{20,16},{24,28},{28,24},{1,5},{5... | collective-permute-start | bytes 1179656 | tf_op jit(solution)/shard_map/ppermute | solution.py:149
  1.2 0.1 collective-permute-start
  1.3 0.3 copy-done
  1.6 5.0 %collective-permute-start.4 = (bf16[48,768]{1,0:T(8,128)(2,1)S(1)}, bf16[48,768]{1,0:T(8,128)(2,1)S(1)}, u32[]{:S(2)}, u32[]{:S(2)}) collective-permute-start(bf16[48,768]{1,0:T(8,128)(2,1)S(1)} %constant_dynamic-slice_fusion.1.refs_0_), channel_id=1, source_target_pairs={{0,3},{1,2},{2,1},{3,0},{4,7},{5,6},{6,5},{7,4},{8,11},{9,10},{10,... | collective-permute-start | bytes 221192 | tf_op jit(solution)/shard_map/ppermute | solution.py:149
  7.3 0.1 pad_add_fusion.1.place_ref
  7.3 0.6 %collective-permute-done.1.refs_3_.refs_1_ = s32[1,256]{1,0:T(1,128)S(1)} collective-permute-done((s32[1,256]{1,0:T(1,128)}, s32[1,256]{1,0:T(1,128)S(1)}, u32[]{:S(2)}, u32[]{:S(2)}) %collective-permute-start.1) | collective-permute-done | bytes 1056 | tf_op jit(solution)/shard_map/ppermute | solution.py:149
  8.0 0.6 %collective-permute-start.2 = (bf16[48,768]{1,0:T(8,128)(2,1)S(1)}, bf16[48,768]{1,0:T(8,128)(2,1)S(1)}, u32[]{:S(2)}, u32[]{:S(2)}) collective-permute-start(bf16[48,768]{1,0:T(8,128)(2,1)S(1)} %constant_dynamic-slice_fusion.1.refs_0_), channel_id=1, source_target_pairs={{0,1},{1,0},{2,3},{3,2},{4,5},{5,4},{6,7},{7,6},{8,9},{9,8},{10,11... | collective-permute-start | bytes 221192 | tf_op jit(solution)/shard_map/ppermute | solution.py:149
  8.6 1.0 %copy-done.2 = bf16[1,384,512]{2,1,0:T(8,128)(2,1)S(1)} copy-done((bf16[1,384,512]{2,1,0:T(8,128)(2,1)S(1)}, bf16[1,384,512]{2,1,0:T(8,128)(2,1)}, u32[]{:S(2)}) %copy-start.2) | copy-done | bytes 393240
  9.6 0.6 %shard_map.71 = bf16[192,512]{1,0:T(8,128)(2,1)S(1)} custom-call(s32[2]{0:T(128)S(1)} %pad_add_fusion.1.place_ref, bf16[4,2,48,512]{3,2,1,0:T(8,128)(2,1)S(1)} %bitcast.20, bf16[4,2,48,512]{3,2,1,0:T(8,128)(2,1)S(1)} %bitcast.21, bf16[256,768]{1,0:T(8,128)(2,1)S(1)} %collective-permute-done.refs_2_.refs_0_, s32[1,256]{1,0:T(1,128)S(1)} %collective-permute-done.1.refs_3_.refs_1_), custom_call_target="tpu_custom_call" | custom-call | tf_op jit(solution)/shard_map/pallas_call | solution.py:134
  10.2 1.7 %collective-permute-start.6 = (bf16[192,512]{1,0:T(8,128)(2,1)S(1)}, bf16[192,512]{1,0:T(8,128)(2,1)S(1)}, u32[]{:S(2)}, u32[]{:S(2)}) collective-permute-start(bf16[192,512]{1,0:T(8,128)(2,1)S(1)} %shard_map.71), channel_id=1, source_target_pairs={{0,8},{4,12},{8,0},{12,4},{16,24},{20,28},{24,16},{28,20},{1,9},{5... | collective-permute-start | bytes 589832 | tf_op jit(solution)/shard_map/ppermute | solution.py:149
  11.9 0.1 pad_add_fusion.place_ref
  12.0 0.7 %copy-done.3 = s32[256]{0:T(256)S(1)} copy-done((s32[256]{0:T(256)S(1)}, s32[256]{0:T(256)}, u32[]{:S(2)}) %copy-start.3) | copy-done | bytes 1048
  12.6 1.1 %shard_map.68 = (bf16[2,512,768]{2,1,0:T(8,128)(2,1)S(1)}, bf16[512,64]{1,0:T(8,128)(2,1)S(1)}) custom-call(bf16[256,768]{1,0:T(8,128)(2,1)S(1)} %copy-done.1, s32[1,256]{1,0:T(1,128)S(1)} %bitcast.23, bf16[256,768]{1,0:T(8,128)(2,1)S(1)} %collective-permute-done.refs_2_.refs_0_, s32[1,256]{1,0:T(1,128)S(1)} %collective-permute-done.1.refs_3_.refs_1_), custom_call_target="tpu_custom_call" | custom-call | tf_op jit(solution)/shard_map/pallas_call | solution.py:134
  13.8 0.7 %shard_map.69 = (bf16[192,768]{1,0:T(8,128)(2,1)S(1)}, s32[1,512]{1,0:T(1,128)S(1)}) custom-call(s32[2]{0:T(128)S(1)} %pad_add_fusion.place_ref, bf16[512,64]{1,0:T(8,128)(2,1)S(1)} %get-tuple-element.9.after_ref.refs_1_, bf16[48,768]{1,0:T(8,128)(2,1)S(1)} %constant_dynamic-slice_fusion.1.refs_0_, bf16[48,768]{1,0:T(8,128)(2,1)S(1)} %collective-permute-done.2.refs_1_, ...), custom_call_target="tpu_custom_call" | custom-call | tf_op jit(solution)/shard_map/pallas_call | solution.py:134
  14.5 2.5 %collective-permute-done.6 = bf16[192,512]{1,0:T(8,128)(2,1)S(1)} collective-permute-done((bf16[192,512]{1,0:T(8,128)(2,1)S(1)}, bf16[192,512]{1,0:T(8,128)(2,1)S(1)}, u32[]{:S(2)}, u32[]{:S(2)}) %collective-permute-start.6) | collective-permute-done | bytes 196640 | tf_op jit(solution)/shard_map/ppermute | solution.py:149
  17.0 1.7 %collective-permute-start.7 = (bf16[192,512]{1,0:T(8,128)(2,1)S(1)}, bf16[192,512]{1,0:T(8,128)(2,1)S(1)}, u32[]{:S(2)}, u32[]{:S(2)}) collective-permute-start(bf16[192,512]{1,0:T(8,128)(2,1)S(1)} %broadcast_select_fusion), channel_id=1, source_target_pairs={{0,16},{4,20},{8,24},{12,28},{16,0},{20,4},{24,8},{28,12},{1,17},{... | collective-permute-start | bytes 589832 | tf_op jit(solution)/shard_map/ppermute | solution.py:149
  18.7 1.4 %shard_map.70 = bf16[8,2,64,256]{3,2,1,0:T(8,128)(2,1)} custom-call(bf16[2,512,768]{2,1,0:T(8,128)(2,1)S(1)} %get-tuple-element.8.refs_0_, bf16[512,64]{1,0:T(8,128)(2,1)S(1)} %get-tuple-element.9.after_ref.refs_1_, bf16[192,768]{1,0:T(8,128)(2,1)S(1)} %get-tuple-element.10.refs_2_), custom_call_target="tpu_custom_call" | custom-call | tf_op jit(solution)/shard_map/pallas_call | solution.py:134
  20.1 3.5 %all-to-all-start = ((bf16[8,128,256]{2,1,0:T(8,128)(2,1)}), bf16[8,128,256]{2,1,0:T(8,128)(2,1)S(1)}, u32[]{:S(2)}, u32[]{:S(2)}) async-start(bf16[8,128,256]{2,1,0:T(8,128)(2,1)} %bitcast.4), calls=%async_computation | async-start | bytes 1048576 | tf_op jit(solution)/shard_map/all_to_all | solution.py:156
  23.7 0.5 %collective-permute-start.8 = (bf16[96,512]{1,0:T(8,128)(2,1)S(1)}, bf16[96,512]{1,0:T(8,128)(2,1)S(1)}, u32[]{:S(2)}, u32[]{:S(2)}) collective-permute-start(bf16[96,512]{1,0:T(8,128)(2,1)S(1)} %get-tuple-element.19), channel_id=1, source_target_pairs={{0,4},{4,0},{8,12},{12,8},{16,20},{20,16},{24,28},{28,24},{1,5},{5... | collective-permute-start | bytes 294920 | tf_op jit(solution)/shard_map/ppermute | solution.py:149
  24.1 9.2 %all-to-all-done = bf16[8,128,256]{2,1,0:T(8,128)(2,1)S(1)} async-done(((bf16[8,128,256]{2,1,0:T(8,128)(2,1)}), bf16[8,128,256]{2,1,0:T(8,128)(2,1)S(1)}, u32[]{:S(2)}, u32[]{:S(2)}) %all-to-all-start) | async-done | bytes 524320 | tf_op jit(solution)/shard_map/all_to_all | solution.py:156
  33.4 0.1 collective-permute-start.9
  33.5 1.3 %collective-permute-done.9.refs_4_ = bf16[96,512]{1,0:T(8,128)(2,1)S(1)} collective-permute-done((bf16[96,512]{1,0:T(8,128)(2,1)S(1)}, bf16[96,512]{1,0:T(8,128)(2,1)S(1)}, u32[]{:S(2)}, u32[]{:S(2)}) %collective-permute-start.9) | collective-permute-done | bytes 98336 | tf_op jit(solution)/shard_map/ppermute | solution.py:149
  34.8 1.9 %shard_map.73 = (f32[512,512]{1,0:T(8,128)}, s32[1,512]{1,0:T(1,128)}) custom-call(bf16[512,256]{1,0:T(8,128)(2,1)S(1)} %bitcast.17, bf16[512,256]{1,0:T(8,128)(2,1)S(1)} %bitcast.18, bf16[192,512]{1,0:T(8,128)(2,1)S(1)} %broadcast_select_fusion.1.refs_2_, bf16[96,512]{1,0:T(8,128)(2,1)S(1)} %collective-permute-done.8.after_ref.refs_3_, ...), custom_call_target="tpu_custom_call" | custom-call | tf_op jit(solution)/shard_map/pallas_call | solution.py:134
  (22 shorter events, 0.2 us)
Async XLA Ops:
  0.6 0.9 %copy-start = (bf16[96,768]{1,0:T(8,128)(2,1)S(1)}, bf16[96,768]{1,0:T(8,128)(2,1)}, u32[]{:S(2)}) copy-start(bf16[96,768]{1,0:T(8,128)(2,1)} %param.6) | copy-start | bytes 442372
  0.6 11.3 %copy-start.1 = (bf16[256,768]{1,0:T(8,128)(2,1)S(1)}, bf16[256,768]{1,0:T(8,128)(2,1)}, u32[]{:S(2)}) copy-start(bf16[256,768]{1,0:T(8,128)(2,1)} %refs_0_.1) | copy-start | bytes 1179652
  0.7 7.9 %collective-permute-start.5 = (bf16[384,512]{1,0:T(8,128)(2,1)}, bf16[384,512]{1,0:T(8,128)(2,1)S(1)}, u32[]{:S(2)}, u32[]{:S(2)}) collective-permute-start(bf16[384,512]{1,0:T(8,128)(2,1)} %bitcast.19), channel_id=1, source_target_pairs={{0,4},{4,0},{8,12},{12,8},{16,20},{20,16},{24,28},{28,24},{1,5},{5... | collective-permute-start | bytes 1179656 | tf_op jit(solution)/shard_map/ppermute | solution.py:149
  1.2 7.4 %collective-permute-start = (bf16[256,768]{1,0:T(8,128)(2,1)}, bf16[256,768]{1,0:T(8,128)(2,1)S(1)}, u32[]{:S(2)}, u32[]{:S(2)}) collective-permute-start(bf16[256,768]{1,0:T(8,128)(2,1)} %refs_0_.1), channel_id=1, source_target_pairs={{0,4},{4,0},{8,12},{12,8},{16,20},{20,16},{24,28},{28,24},{1,5},{5... | collective-permute-start | bytes 1179656 | tf_op jit(solution)/shard_map/ppermute | solution.py:149
  1.6 12.2 %collective-permute-start.4 = (bf16[48,768]{1,0:T(8,128)(2,1)S(1)}, bf16[48,768]{1,0:T(8,128)(2,1)S(1)}, u32[]{:S(2)}, u32[]{:S(2)}) collective-permute-start(bf16[48,768]{1,0:T(8,128)(2,1)S(1)} %constant_dynamic-slice_fusion.1.refs_0_), channel_id=1, source_target_pairs={{0,3},{1,2},{2,1},{3,0},{4,7},{5,6},{6,5},{7,4},{8,11},{9,10},{10,... | collective-permute-start | bytes 221192 | tf_op jit(solution)/shard_map/ppermute | solution.py:149
  6.6 7.2 %collective-permute-start.3 = (bf16[48,768]{1,0:T(8,128)(2,1)S(1)}, bf16[48,768]{1,0:T(8,128)(2,1)S(1)}, u32[]{:S(2)}, u32[]{:S(2)}) collective-permute-start(bf16[48,768]{1,0:T(8,128)(2,1)S(1)} %constant_dynamic-slice_fusion.1.refs_0_), channel_id=1, source_target_pairs={{0,2},{1,3},{2,0},{3,1},{4,6},{5,7},{6,4},{7,5},{8,10},{9,11},{10,... | collective-permute-start | bytes 221192 | tf_op jit(solution)/shard_map/ppermute | solution.py:149
  6.6 1.4 %collective-permute-start.1 = (s32[1,256]{1,0:T(1,128)}, s32[1,256]{1,0:T(1,128)S(1)}, u32[]{:S(2)}, u32[]{:S(2)}) collective-permute-start(s32[1,256]{1,0:T(1,128)} %bitcast.22), channel_id=1, source_target_pairs={{0,4},{4,0},{8,12},{12,8},{16,20},{20,16},{24,28},{28,24},{1,5},{5... | collective-permute-start | bytes 3080 | tf_op jit(solution)/shard_map/ppermute | solution.py:149
  8.0 5.8 %collective-permute-start.2 = (bf16[48,768]{1,0:T(8,128)(2,1)S(1)}, bf16[48,768]{1,0:T(8,128)(2,1)S(1)}, u32[]{:S(2)}, u32[]{:S(2)}) collective-permute-start(bf16[48,768]{1,0:T(8,128)(2,1)S(1)} %constant_dynamic-slice_fusion.1.refs_0_), channel_id=1, source_target_pairs={{0,1},{1,0},{2,3},{3,2},{4,5},{5,4},{6,7},{7,6},{8,9},{9,8},{10,11... | collective-permute-start | bytes 221192 | tf_op jit(solution)/shard_map/ppermute | solution.py:149
  8.6 1.0 %copy-start.2 = (bf16[1,384,512]{2,1,0:T(8,128)(2,1)S(1)}, bf16[1,384,512]{2,1,0:T(8,128)(2,1)}, u32[]{:S(2)}) copy-start(bf16[1,384,512]{2,1,0:T(8,128)(2,1)} %param.7) | copy-start | bytes 1179652
  10.2 6.8 %collective-permute-start.6 = (bf16[192,512]{1,0:T(8,128)(2,1)S(1)}, bf16[192,512]{1,0:T(8,128)(2,1)S(1)}, u32[]{:S(2)}, u32[]{:S(2)}) collective-permute-start(bf16[192,512]{1,0:T(8,128)(2,1)S(1)} %shard_map.71), channel_id=1, source_target_pairs={{0,8},{4,12},{8,0},{12,4},{16,24},{20,28},{24,16},{28,20},{1,9},{5... | collective-permute-start | bytes 589832 | tf_op jit(solution)/shard_map/ppermute | solution.py:149
  12.0 0.7 %copy-start.3 = (s32[256]{0:T(256)S(1)}, s32[256]{0:T(256)}, u32[]{:S(2)}) copy-start(s32[256]{0:T(256)} %param.9) | copy-start | bytes 3076
  17.0 6.6 %collective-permute-start.7 = (bf16[192,512]{1,0:T(8,128)(2,1)S(1)}, bf16[192,512]{1,0:T(8,128)(2,1)S(1)}, u32[]{:S(2)}, u32[]{:S(2)}) collective-permute-start(bf16[192,512]{1,0:T(8,128)(2,1)S(1)} %broadcast_select_fusion), channel_id=1, source_target_pairs={{0,16},{4,20},{8,24},{12,28},{16,0},{20,4},{24,8},{28,12},{1,17},{... | collective-permute-start | bytes 589832 | tf_op jit(solution)/shard_map/ppermute | solution.py:149
  20.1 13.2 %all-to-all-start = ((bf16[8,128,256]{2,1,0:T(8,128)(2,1)}), bf16[8,128,256]{2,1,0:T(8,128)(2,1)S(1)}, u32[]{:S(2)}, u32[]{:S(2)}) async-start(bf16[8,128,256]{2,1,0:T(8,128)(2,1)} %bitcast.4), calls=%async_computation | async-start | bytes 1048576 | tf_op jit(solution)/shard_map/all_to_all | solution.py:156
  23.7 9.7 %collective-permute-start.8 = (bf16[96,512]{1,0:T(8,128)(2,1)S(1)}, bf16[96,512]{1,0:T(8,128)(2,1)S(1)}, u32[]{:S(2)}, u32[]{:S(2)}) collective-permute-start(bf16[96,512]{1,0:T(8,128)(2,1)S(1)} %get-tuple-element.19), channel_id=1, source_target_pairs={{0,4},{4,0},{8,12},{12,8},{16,20},{20,16},{24,28},{28,24},{1,5},{5... | collective-permute-start | bytes 294920 | tf_op jit(solution)/shard_map/ppermute | solution.py:149
  33.4 1.4 %collective-permute-start.9 = (bf16[96,512]{1,0:T(8,128)(2,1)S(1)}, bf16[96,512]{1,0:T(8,128)(2,1)S(1)}, u32[]{:S(2)}, u32[]{:S(2)}) collective-permute-start(bf16[96,512]{1,0:T(8,128)(2,1)S(1)} %shard_map.72), channel_id=1, source_target_pairs={{0,4},{4,0},{8,12},{12,8},{16,20},{20,16},{24,28},{28,24},{1,5},{5... | collective-permute-start | bytes 294920 | tf_op jit(solution)/shard_map/ppermute | solution.py:149

commit v4 on v1

--- a/solution.py
+++ b/solution.py
@@ -94,10 +94,19 @@
             out_ref[core, :, marks:] = tags
 
 
-def sums_kernel(scale, even_ref, odd_ref, mine_ref, *refs):
-    others, (totals_ref, counts_ref, panel_ref) = refs[:-3], refs[-3:]
-    slots, lanes = even_ref.shape
+def sums_kernel(scale, core_ref, arrived_ref, mine_ref, *refs):
+    others, (totals_ref, counts_ref, panel_ref, rows_ref) = refs[:-4], refs[-4:]
+    slots, lanes = rows_ref.shape[1:]
     owned, marks = totals_ref.shape[0], mine_ref.shape[0]
+    if len(arrived_ref.shape) == 3:
+        rows_ref[...] = arrived_ref[...]
+    else:
+        part = arrived_ref.shape[2] // 2
+        for chip in range(arrived_ref.shape[0]):
+            first, middle, last = 2 * chip * part, (2 * chip + 1) * part, (2 * chip + 2) * part
+            rows_ref[0, first:last, :] = arrived_ref[chip, core_ref[0]]
+            rows_ref[1, first:middle, :] = arrived_ref[chip, 1 - core_ref[0], part:, :]
+            rows_ref[1, middle:last, :] = arrived_ref[chip, 1 - core_ref[0], :part, :]
     panel_ref[0, :marks, :] = mine_ref[...]
     first = 0
     for other in others:
@@ -105,13 +114,13 @@
         first += other.shape[0]
     panel_ref[:, marks:, :] = jnp.zeros((2, lanes - marks, mine_ref.shape[1]), jnp.bfloat16)
     features = (
-        jnp.dot(even_ref[...], panel_ref[0], preferred_element_type=jnp.float32)
-        + jnp.dot(odd_ref[...], panel_ref[1], preferred_element_type=jnp.float32)
+        jnp.dot(rows_ref[0], panel_ref[0], preferred_element_type=jnp.float32)
+        + jnp.dot(rows_ref[1], panel_ref[1], preferred_element_type=jnp.float32)
     ).astype(jnp.bfloat16)
     which = lax.broadcasted_iota(jnp.int32, (8, lanes - marks), 1)
     weights = jnp.where(which == 0, 256.0, jnp.where(which == 1, 1.0, 0.0)).astype(jnp.bfloat16)
-    tags = lax.dot_general(weights, even_ref[:, marks:], NT, preferred_element_type=jnp.float32)
-    tags += lax.dot_general(weights, odd_ref[:, marks:], NT, preferred_element_type=jnp.float32)
+    tags = lax.dot_general(weights, rows_ref[0, :, marks:], NT, preferred_element_type=jnp.float32)
+    tags += lax.dot_general(weights, rows_ref[1, :, marks:], NT, preferred_element_type=jnp.float32)
     tags = tags[:1].astype(jnp.int32)
     member = (
         (lax.broadcasted_iota(jnp.int32, (owned, slots), 0) + 1 == tags)
@@ -158,18 +167,20 @@
     )
 
 
-def exchange(rows, groups, capacity):
+def exchange(rows, groups, capacity, core):
     slots, lanes = groups * capacity, rows.shape[-1]
-    if rows.ndim == 3:
+    whole_tiles = rows.ndim == 4
+    if not whole_tiles:
         rows = rows.reshape(2, groups, capacity, lanes).swapaxes(0, 1)
     arrived = lax.all_to_all(
         rows.reshape(groups, 2 * capacity, lanes), "pts", split_axis=0, concat_axis=0, tiled=True
     ).reshape(groups // 2, 2, 2 * capacity, lanes)
-    core = lax.axis_index("pts") % 2
+    if whole_tiles:
+        return arrived
     even = lax.dynamic_index_in_dim(arrived, core, 1, keepdims=False)
     odd = lax.dynamic_index_in_dim(arrived, 1 - core, 1, keepdims=False)
     odd = jnp.concatenate([odd[:, capacity:], odd[:, :capacity]], axis=1)
-    return even.reshape(slots, lanes), odd.reshape(slots, lanes)
+    return jnp.stack([even.reshape(slots, lanes), odd.reshape(slots, lanes)])
 
 
 def body(points, landmarks, panels, panel_index, assignment):
@@ -220,15 +231,18 @@
     cut = panel.shape[0] // 2
     others = [swap(panel[:cut], "pts", 1)]
     others.append(swap(call(pass_kernel, array((cut, columns)), panel[cut:], others[0]), "pts", 1))
-    even, odd = exchange(rows, groups, capacity)
+    arrived = exchange(rows, groups, capacity, me % 2)
     totals, counts = call(
         lambda *refs: sums_kernel(CLUSTERS / (point_rows * groups), *refs),
         (array((owned, columns), jnp.float32), array((1, owned), jnp.int32)),
-        even,
-        odd,
+        arrived,
         panel,
         *others,
-        scratch=[pltpu.VMEM((2, lanes, columns), jnp.bfloat16)],
+        place=(me % 2).astype(jnp.int32).reshape(1),
+        scratch=[
+            pltpu.VMEM((2, lanes, columns), jnp.bfloat16),
+            pltpu.VMEM((2, slots, lanes), jnp.bfloat16),
+        ],
     )
     return (totals, counts.reshape(owned))
 

time: 35.6 us -> 34.1 us (0.958)
  waiting for transfers between devices: 13.6 us -> 11.8 us
  starting transfers between devices: 13.8 us -> 14.2 us
    all_to_all x1, waiting for transfers between devices: 9.15 us -> 7.77 us  [exchange(): lax.all_to_all(rows.reshape(groups, 2 * capacity, lanes), 'pts', split_ax...]
    ppermute x10, waiting for transfers between devices: 4.46 us -> 4.07 us  [swap(): lax.ppermute(block, axis, [(i, i ^ mask) for i in range(lax.axis_size(axi...]
  transfers between devices with their start and end apart: 11 -> 11, of which waited for: 4 -> 4; matrix products, arithmetic and copies ran while one was open for 4% -> 4% of each run, Pallas kernels for 9% -> 10%
where the time goes in v4:
time: 34.1 us; the launch traced here: 33.8 us
  starting transfers between devices  14.2 us (42%)
  waiting for transfers between devices  11.8 us (35%)
  Pallas kernels  5.13 us (15%)
  between operations  1.4 us (4%)
  local copies, waits for them, and re-layouts  1.09 us (3%)
    ppermute x10, starting transfers between devices, swap(): lax.ppermute(block, axis, [(i, i ^ mask) for i in range(lax.axis_size(axi...  10.7 us
    all_to_all x1, waiting for transfers between devices, exchange(): lax.all_to_all(rows.reshape(groups, 2 * capacity, lanes), 'pts', split_ax...  7.77 us
    pallas_call x6, Pallas kernels, call(): pl.pallas_call(kernel, out_shape=shapes, in_specs=[pl.BlockSpec(memory_sp...  5.13 us
    ppermute x10, waiting for transfers between devices, swap(): lax.ppermute(block, axis, [(i, i ^ mask) for i in range(lax.axis_size(axi...  4.07 us
    all_to_all x1, starting transfers between devices, exchange(): lax.all_to_all(rows.reshape(groups, 2 * capacity, lanes), 'pts', split_ax...  3.49 us
    dynamic_slice x1, local copies, waits for them, and re-layouts, sides_of(): lax.dynamic_index_in_dim(sides, side, 1, keepdims=False)  1.05 us
  transfers between devices with their start and end apart: 11, of which 4 were waited for; matrix products, arithmetic and copies ran while one was open for 4% of the time, Pallas kernels for 10%

profile of v4, /device:TPU:0, one launch (start us, length us, event | category | flops | bytes accessed | tf_op | source)
XLA Modules:
  0.0 33.8 jit_solution(17011212766426272090)
XLA Ops:
  0.6 0.0 copy-start
  0.7 0.0 copy-start.2
  0.7 0.5 %collective-permute-start = (bf16[256,768]{1,0:T(8,128)(2,1)}, bf16[256,768]{1,0:T(8,128)(2,1)S(1)}, u32[]{:S(2)}, u32[]{:S(2)}) collective-permute-start(bf16[256,768]{1,0:T(8,128)(2,1)} %refs_0_.1), channel_id=1, source_target_pairs={{0,4},{4,0},{8,12},{12,8},{16,20},{20,16},{24,28},{28,24},{1,5},{5... | collective-permute-start | bytes 1179656 | tf_op jit(solution)/shard_map/ppermute | solution.py:154
  1.2 1.0 %constant_dynamic-slice_fusion = (bf16[4,1,48,512]{3,2,1,0:T(8,128)(2,1)S(1)}, bf16[4,1,48,512]{3,2,1,0:T(8,128)(2,1)S(1)}) fusion(bf16[4,2,48,512]{3,2,1,0:T(8,128)(2,1)} %bitcast.21, s32[]{:T(128)S(6)} %select_n.37, s32[]{:T(128)S(6)} %select_n.36), kind=kLoop, calls=%fused_computation.3 | loop fusion | bytes 786440 | tf_op jit(solution)/shard_map/jit(dynamic_index_in_dim)/dynamic_slice | solution.py:165
  2.2 0.2 collective-permute-start.5
  2.4 0.4 %collective-permute-start.1 = (s32[1,256]{1,0:T(1,128)}, s32[1,256]{1,0:T(1,128)S(1)}, u32[]{:S(2)}, u32[]{:S(2)}) collective-permute-start(s32[1,256]{1,0:T(1,128)} %bitcast.19), channel_id=1, source_target_pairs={{0,4},{4,0},{8,12},{12,8},{16,20},{20,16},{24,28},{28,24},{1,5},{5... | collective-permute-start | bytes 3080 | tf_op jit(solution)/shard_map/ppermute | solution.py:154
  2.8 4.8 %collective-permute-start.4 = (bf16[48,768]{1,0:T(8,128)(2,1)S(1)}, bf16[48,768]{1,0:T(8,128)(2,1)S(1)}, u32[]{:S(2)}, u32[]{:S(2)}) collective-permute-start(bf16[48,768]{1,0:T(8,128)(2,1)S(1)} %constant_dynamic-slice_fusion.2.refs_0_), channel_id=1, source_target_pairs={{0,3},{1,2},{2,1},{3,0},{4,7},{5,6},{6,5},{7,4},{8,11},{9,10},{10,... | collective-permute-start | bytes 221192 | tf_op jit(solution)/shard_map/ppermute | solution.py:154
  7.6 0.0 collective-permute-start.3
  8.3 0.7 %collective-permute-start.2 = (bf16[48,768]{1,0:T(8,128)(2,1)S(1)}, bf16[48,768]{1,0:T(8,128)(2,1)S(1)}, u32[]{:S(2)}, u32[]{:S(2)}) collective-permute-start(bf16[48,768]{1,0:T(8,128)(2,1)S(1)} %constant_dynamic-slice_fusion.2.refs_0_), channel_id=1, source_target_pairs={{0,1},{1,0},{2,3},{3,2},{4,5},{5,4},{6,7},{7,6},{8,9},{9,8},{10,11... | collective-permute-start | bytes 221192 | tf_op jit(solution)/shard_map/ppermute | solution.py:154
  9.0 0.0 collective-permute-done.5.met_ref
  9.0 1.7 %collective-permute-start.6 = (bf16[192,512]{1,0:T(8,128)(2,1)S(1)}, bf16[192,512]{1,0:T(8,128)(2,1)S(1)}, u32[]{:S(2)}, u32[]{:S(2)}) collective-permute-start(bf16[192,512]{1,0:T(8,128)(2,1)S(1)} %shard_map.71), channel_id=1, source_target_pairs={{0,8},{4,12},{8,0},{12,4},{16,24},{20,28},{24,16},{28,20},{1,9},{5... | collective-permute-start | bytes 589832 | tf_op jit(solution)/shard_map/ppermute | solution.py:154
  10.7 0.1 pad_add_fusion.place_ref
  10.8 1.1 %shard_map.68 = (bf16[2,512,768]{2,1,0:T(8,128)(2,1)S(1)}, bf16[512,64]{1,0:T(8,128)(2,1)S(1)}) custom-call(bf16[256,768]{1,0:T(8,128)(2,1)S(1)} %copy-done.1, s32[1,256]{1,0:T(1,128)S(1)} %bitcast.20, bf16[256,768]{1,0:T(8,128)(2,1)S(1)} %collective-permute-done.refs_2_.refs_0_, s32[1,256]{1,0:T(1,128)S(1)} %collective-permute-done.1.refs_3_.refs_1_), custom_call_target="tpu_custom_call" | custom-call | tf_op jit(solution)/shard_map/pallas_call | solution.py:139
  11.9 2.4 %collective-permute-done.3.refs_2_ = bf16[48,768]{1,0:T(8,128)(2,1)S(1)} collective-permute-done((bf16[48,768]{1,0:T(8,128)(2,1)S(1)}, bf16[48,768]{1,0:T(8,128)(2,1)S(1)}, u32[]{:S(2)}, u32[]{:S(2)}) %collective-permute-start.3) | collective-permute-done | bytes 73760 | tf_op jit(solution)/shard_map/ppermute | solution.py:154
  14.3 0.7 %shard_map.69 = (bf16[192,768]{1,0:T(8,128)(2,1)S(1)}, s32[1,512]{1,0:T(1,128)S(1)}) custom-call(s32[2]{0:T(128)S(1)} %pad_add_fusion.place_ref, bf16[512,64]{1,0:T(8,128)(2,1)S(1)} %get-tuple-element.9.after_ref.refs_1_, bf16[48,768]{1,0:T(8,128)(2,1)S(1)} %constant_dynamic-slice_fusion.2.refs_0_, bf16[48,768]{1,0:T(8,128)(2,1)S(1)} %collective-permute-done.2.refs_1_, ...), custom_call_target="tpu_custom_call" | custom-call | tf_op jit(solution)/shard_map/pallas_call | solution.py:139
  15.1 0.7 %collective-permute-done.6 = bf16[192,512]{1,0:T(8,128)(2,1)S(1)} collective-permute-done((bf16[192,512]{1,0:T(8,128)(2,1)S(1)}, bf16[192,512]{1,0:T(8,128)(2,1)S(1)}, u32[]{:S(2)}, u32[]{:S(2)}) %collective-permute-start.6) | collective-permute-done | bytes 196640 | tf_op jit(solution)/shard_map/ppermute | solution.py:154
  15.8 1.6 %collective-permute-start.7 = (bf16[192,512]{1,0:T(8,128)(2,1)S(1)}, bf16[192,512]{1,0:T(8,128)(2,1)S(1)}, u32[]{:S(2)}, u32[]{:S(2)}) collective-permute-start(bf16[192,512]{1,0:T(8,128)(2,1)S(1)} %broadcast_select_fusion), channel_id=1, source_target_pairs={{0,16},{4,20},{8,24},{12,28},{16,0},{20,4},{24,8},{28,12},{1,17},{... | collective-permute-start | bytes 589832 | tf_op jit(solution)/shard_map/ppermute | solution.py:154
  17.3 1.4 %shard_map.70 = bf16[8,2,64,256]{3,2,1,0:T(8,128)(2,1)} custom-call(bf16[2,512,768]{2,1,0:T(8,128)(2,1)S(1)} %get-tuple-element.8.refs_0_, bf16[512,64]{1,0:T(8,128)(2,1)S(1)} %get-tuple-element.9.after_ref.refs_1_, bf16[192,768]{1,0:T(8,128)(2,1)S(1)} %get-tuple-element.10.refs_2_), custom_call_target="tpu_custom_call" | custom-call | tf_op jit(solution)/shard_map/pallas_call | solution.py:139
  18.7 3.5 %all-to-all-start = ((bf16[8,128,256]{2,1,0:T(8,128)(2,1)}), bf16[8,128,256]{2,1,0:T(8,128)(2,1)S(1)}, u32[]{:S(2)}, u32[]{:S(2)}) async-start(bf16[8,128,256]{2,1,0:T(8,128)(2,1)} %bitcast.5), calls=%async_computation | async-start | bytes 1048576 | tf_op jit(solution)/shard_map/all_to_all | solution.py:175
  22.3 0.5 %collective-permute-start.8 = (bf16[96,512]{1,0:T(8,128)(2,1)S(1)}, bf16[96,512]{1,0:T(8,128)(2,1)S(1)}, u32[]{:S(2)}, u32[]{:S(2)}) collective-permute-start(bf16[96,512]{1,0:T(8,128)(2,1)S(1)} %get-tuple-element.17), channel_id=1, source_target_pairs={{0,4},{4,0},{8,12},{12,8},{16,20},{20,16},{24,28},{28,24},{1,5},{5... | collective-permute-start | bytes 294920 | tf_op jit(solution)/shard_map/ppermute | solution.py:154
  22.8 0.9 %collective-permute-done.8.after_ref.refs_3_ = bf16[96,512]{1,0:T(8,128)(2,1)S(1)} collective-permute-done((bf16[96,512]{1,0:T(8,128)(2,1)S(1)}, bf16[96,512]{1,0:T(8,128)(2,1)S(1)}, u32[]{:S(2)}, u32[]{:S(2)}) %collective-permute-start.8) | collective-permute-done | bytes 98336 | tf_op jit(solution)/shard_map/ppermute | solution.py:154
  23.7 0.4 %collective-permute-start.9 = (bf16[96,512]{1,0:T(8,128)(2,1)S(1)}, bf16[96,512]{1,0:T(8,128)(2,1)S(1)}, u32[]{:S(2)}, u32[]{:S(2)}) collective-permute-start(bf16[96,512]{1,0:T(8,128)(2,1)S(1)} %shard_map.72), channel_id=1, source_target_pairs={{0,4},{4,0},{8,12},{12,8},{16,20},{20,16},{24,28},{28,24},{1,5},{5... | collective-permute-start | bytes 294920 | tf_op jit(solution)/shard_map/ppermute | solution.py:154
  24.1 7.8 %all-to-all-done = bf16[8,128,256]{2,1,0:T(8,128)(2,1)S(1)} async-done(((bf16[8,128,256]{2,1,0:T(8,128)(2,1)}), bf16[8,128,256]{2,1,0:T(8,128)(2,1)S(1)}, u32[]{:S(2)}, u32[]{:S(2)}) %all-to-all-start) | async-done | bytes 524320 | tf_op jit(solution)/shard_map/all_to_all | solution.py:175
  31.9 1.9 %shard_map.73 = (f32[512,512]{1,0:T(8,128)}, s32[1,512]{1,0:T(1,128)}) custom-call(s32[1]{0:T(128)} %bitcast.refs_0_, bf16[4,2,128,256]{3,2,1,0:T(8,128)(2,1)S(1)} %bitcast.17, bf16[192,512]{1,0:T(8,128)(2,1)S(1)} %broadcast_select_fusion.1.refs_2_, bf16[96,512]{1,0:T(8,128)(2,1)S(1)} %collective-permute-done.8.after_ref.refs_3_, ...), custom_call_target="tpu_custom_call" | custom-call | tf_op jit(solution)/shard_map/pallas_call | solution.py:139
  (17 shorter events, 0.2 us)
Async XLA Ops:
  0.6 2.2 %copy-start = (bf16[96,768]{1,0:T(8,128)(2,1)S(1)}, bf16[96,768]{1,0:T(8,128)(2,1)}, u32[]{:S(2)}) copy-start(bf16[96,768]{1,0:T(8,128)(2,1)} %param.6) | copy-start | bytes 442372
  0.6 10.1 %copy-start.1 = (bf16[256,768]{1,0:T(8,128)(2,1)S(1)}, bf16[256,768]{1,0:T(8,128)(2,1)}, u32[]{:S(2)}) copy-start(bf16[256,768]{1,0:T(8,128)(2,1)} %refs_0_.1) | copy-start | bytes 1179652
  0.7 10.1 %copy-start.2 = (s32[256]{0:T(256)S(1)}, s32[256]{0:T(256)}, u32[]{:S(2)}) copy-start(s32[256]{0:T(256)} %param.9) | copy-start | bytes 3076
  0.7 8.3 %collective-permute-start = (bf16[256,768]{1,0:T(8,128)(2,1)}, bf16[256,768]{1,0:T(8,128)(2,1)S(1)}, u32[]{:S(2)}, u32[]{:S(2)}) collective-permute-start(bf16[256,768]{1,0:T(8,128)(2,1)} %refs_0_.1), channel_id=1, source_target_pairs={{0,4},{4,0},{8,12},{12,8},{16,20},{20,16},{24,28},{28,24},{1,5},{5... | collective-permute-start | bytes 1179656 | tf_op jit(solution)/shard_map/ppermute | solution.py:154
  2.2 6.7 %collective-permute-start.5 = (bf16[192,512]{1,0:T(8,128)(2,1)S(1)}, bf16[192,512]{1,0:T(8,128)(2,1)S(1)}, u32[]{:S(2)}, u32[]{:S(2)}) collective-permute-start(bf16[192,512]{1,0:T(8,128)(2,1)S(1)} %bitcast.22), channel_id=1, source_target_pairs={{0,4},{4,0},{8,12},{12,8},{16,20},{20,16},{24,28},{28,24},{1,5},{5... | collective-permute-start | bytes 589832 | tf_op jit(solution)/shard_map/ppermute | solution.py:154
  2.4 5.9 %collective-permute-start.1 = (s32[1,256]{1,0:T(1,128)}, s32[1,256]{1,0:T(1,128)S(1)}, u32[]{:S(2)}, u32[]{:S(2)}) collective-permute-start(s32[1,256]{1,0:T(1,128)} %bitcast.19), channel_id=1, source_target_pairs={{0,4},{4,0},{8,12},{12,8},{16,20},{20,16},{24,28},{28,24},{1,5},{5... | collective-permute-start | bytes 3080 | tf_op jit(solution)/shard_map/ppermute | solution.py:154
  2.8 9.1 %collective-permute-start.4 = (bf16[48,768]{1,0:T(8,128)(2,1)S(1)}, bf16[48,768]{1,0:T(8,128)(2,1)S(1)}, u32[]{:S(2)}, u32[]{:S(2)}) collective-permute-start(bf16[48,768]{1,0:T(8,128)(2,1)S(1)} %constant_dynamic-slice_fusion.2.refs_0_), channel_id=1, source_target_pairs={{0,3},{1,2},{2,1},{3,0},{4,7},{5,6},{6,5},{7,4},{8,11},{9,10},{10,... | collective-permute-start | bytes 221192 | tf_op jit(solution)/shard_map/ppermute | solution.py:154
  7.6 6.8 %collective-permute-start.3 = (bf16[48,768]{1,0:T(8,128)(2,1)S(1)}, bf16[48,768]{1,0:T(8,128)(2,1)S(1)}, u32[]{:S(2)}, u32[]{:S(2)}) collective-permute-start(bf16[48,768]{1,0:T(8,128)(2,1)S(1)} %constant_dynamic-slice_fusion.2.refs_0_), channel_id=1, source_target_pairs={{0,2},{1,3},{2,0},{3,1},{4,6},{5,7},{6,4},{7,5},{8,10},{9,11},{10,... | collective-permute-start | bytes 221192 | tf_op jit(solution)/shard_map/ppermute | solution.py:154
  8.3 6.1 %collective-permute-start.2 = (bf16[48,768]{1,0:T(8,128)(2,1)S(1)}, bf16[48,768]{1,0:T(8,128)(2,1)S(1)}, u32[]{:S(2)}, u32[]{:S(2)}) collective-permute-start(bf16[48,768]{1,0:T(8,128)(2,1)S(1)} %constant_dynamic-slice_fusion.2.refs_0_), channel_id=1, source_target_pairs={{0,1},{1,0},{2,3},{3,2},{4,5},{5,4},{6,7},{7,6},{8,9},{9,8},{10,11... | collective-permute-start | bytes 221192 | tf_op jit(solution)/shard_map/ppermute | solution.py:154
  9.0 6.7 %collective-permute-start.6 = (bf16[192,512]{1,0:T(8,128)(2,1)S(1)}, bf16[192,512]{1,0:T(8,128)(2,1)S(1)}, u32[]{:S(2)}, u32[]{:S(2)}) collective-permute-start(bf16[192,512]{1,0:T(8,128)(2,1)S(1)} %shard_map.71), channel_id=1, source_target_pairs={{0,8},{4,12},{8,0},{12,4},{16,24},{20,28},{24,16},{28,20},{1,9},{5... | collective-permute-start | bytes 589832 | tf_op jit(solution)/shard_map/ppermute | solution.py:154
  15.8 6.5 %collective-permute-start.7 = (bf16[192,512]{1,0:T(8,128)(2,1)S(1)}, bf16[192,512]{1,0:T(8,128)(2,1)S(1)}, u32[]{:S(2)}, u32[]{:S(2)}) collective-permute-start(bf16[192,512]{1,0:T(8,128)(2,1)S(1)} %broadcast_select_fusion), channel_id=1, source_target_pairs={{0,16},{4,20},{8,24},{12,28},{16,0},{20,4},{24,8},{28,12},{1,17},{... | collective-permute-start | bytes 589832 | tf_op jit(solution)/shard_map/ppermute | solution.py:154
  18.7 13.2 %all-to-all-start = ((bf16[8,128,256]{2,1,0:T(8,128)(2,1)}), bf16[8,128,256]{2,1,0:T(8,128)(2,1)S(1)}, u32[]{:S(2)}, u32[]{:S(2)}) async-start(bf16[8,128,256]{2,1,0:T(8,128)(2,1)} %bitcast.5), calls=%async_computation | async-start | bytes 1048576 | tf_op jit(solution)/shard_map/all_to_all | solution.py:175
  22.3 1.4 %collective-permute-start.8 = (bf16[96,512]{1,0:T(8,128)(2,1)S(1)}, bf16[96,512]{1,0:T(8,128)(2,1)S(1)}, u32[]{:S(2)}, u32[]{:S(2)}) collective-permute-start(bf16[96,512]{1,0:T(8,128)(2,1)S(1)} %get-tuple-element.17), channel_id=1, source_target_pairs={{0,4},{4,0},{8,12},{12,8},{16,20},{20,16},{24,28},{28,24},{1,5},{5... | collective-permute-start | bytes 294920 | tf_op jit(solution)/shard_map/ppermute | solution.py:154
  23.7 8.2 %collective-permute-start.9 = (bf16[96,512]{1,0:T(8,128)(2,1)S(1)}, bf16[96,512]{1,0:T(8,128)(2,1)S(1)}, u32[]{:S(2)}, u32[]{:S(2)}) collective-permute-start(bf16[96,512]{1,0:T(8,128)(2,1)S(1)} %shard_map.72), channel_id=1, source_target_pairs={{0,4},{4,0},{8,12},{12,8},{16,20},{20,16},{24,28},{28,24},{1,5},{5... | collective-permute-start | bytes 294920 | tf_op jit(solution)/shard_map/ppermute | solution.py:154

commit v5 on v4

--- a/solution.py
+++ b/solution.py
@@ -84,11 +84,12 @@
             points_ref[core], marks_ref[...], NT, preferred_element_type=jnp.float32
         )
         rows = jnp.exp(scores * (0.5 / math.sqrt(points_ref.shape[2]))).astype(jnp.bfloat16)
-        if len(out_ref.shape) == 4:
+        if len(out_ref.shape) == 2:
             for group in range(groups):
                 here = slice(group * capacity, (group + 1) * capacity)
-                out_ref[group, core, :, :marks] = rows[here]
-                out_ref[group, core, :, marks:] = tags[here]
+                first = (2 * group + core) * capacity
+                out_ref[first : first + capacity, :marks] = rows[here]
+                out_ref[first : first + capacity, marks:] = tags[here]
         else:
             out_ref[core, :, :marks] = rows
             out_ref[core, :, marks:] = tags
@@ -169,7 +170,7 @@
 
 def exchange(rows, groups, capacity, core):
     slots, lanes = groups * capacity, rows.shape[-1]
-    whole_tiles = rows.ndim == 4
+    whole_tiles = rows.ndim == 2
     if not whole_tiles:
         rows = rows.reshape(2, groups, capacity, lanes).swapaxes(0, 1)
     arrived = lax.all_to_all(
@@ -194,12 +195,15 @@
     lanes = -(-(depth // 2 + 2) // LANES) * LANES
     me = lax.axis_index("pts")
     marks = lax.dynamic_slice_in_dim(landmarks, (me % 2) * half, half, 0)
-    halves = [marks] + [swap(marks, "lmk", mask) for mask in range(1, parts)]
     assignment = assignment.reshape(1, point_rows)
     points_met, assignment_met = swap(points, "pts", 1), swap(assignment, "pts", 1)
     differs = panel_index[0] ^ me
     mine, other = sides_of(panels[0], parts, me % 2)
     panel = pick((differs & 1) == 0, mine, swap(other, "pts", 1), points_met, assignment_met)
+    near = call(pass_kernel, array(marks.shape), marks, panel)
+    halves = [marks] + [
+        swap(near if mask == 1 else marks, "lmk", mask) for mask in range(1, parts)
+    ]
     masks = [1 << bit for bit in range(1, groups.bit_length() - 1)]
     panel_met = swap(panel, "pts", masks[0])
     place = jnp.stack([lax.axis_index("lmk"), (differs & masks[0]) == 0]).astype(jnp.int32)
@@ -220,7 +224,7 @@
     )
     rows = call(
         lambda *refs: rows_kernel(groups, capacity, *refs),
-        array((groups, 2, capacity, lanes) if capacity % 16 == 0 else (2, slots, lanes)),
+        array((2 * slots, lanes) if capacity % 16 == 0 else (2, slots, lanes)),
         placed,
         tags,
         marks,

time: 34.1 us -> 33.7 us (0.988)
    pallas_call x6 -> x7, Pallas kernels: 5.13 us -> 5.14 us  [call(): pl.pallas_call(kernel, out_shape=shapes, in_specs=[pl.BlockSpec(memory_sp...]
  transfers between devices with their start and end apart: 11 -> 11, of which waited for: 4 -> 5; matrix products, arithmetic and copies ran while one was open for 4% -> 4% of each run, Pallas kernels for 10% -> 10%
where the time goes in v5:
time: 33.7 us; the launch traced here: 33.5 us
  starting transfers between devices  13.9 us (41%)
  waiting for transfers between devices  11.8 us (35%)
  Pallas kernels  5.14 us (15%)
  between operations  1.42 us (4%)
  local copies, waits for them, and re-layouts  1.09 us (3%)
    ppermute x10, starting transfers between devices, swap(): lax.ppermute(block, axis, [(i, i ^ mask) for i in range(lax.axis_size(axi...  10.4 us
    all_to_all x1, waiting for transfers between devices, exchange(): lax.all_to_all(rows.reshape(groups, 2 * capacity, lanes), 'pts', split_ax...  7.77 us
    pallas_call x7, Pallas kernels, call(): pl.pallas_call(kernel, out_shape=shapes, in_specs=[pl.BlockSpec(memory_sp...  5.14 us
    ppermute x10, waiting for transfers between devices, swap(): lax.ppermute(block, axis, [(i, i ^ mask) for i in range(lax.axis_size(axi...  4 us
    all_to_all x1, starting transfers between devices, exchange(): lax.all_to_all(rows.reshape(groups, 2 * capacity, lanes), 'pts', split_ax...  3.49 us
    dynamic_slice x1, local copies, waits for them, and re-layouts, sides_of(): lax.dynamic_index_in_dim(sides, side, 1, keepdims=False)  1.05 us
  transfers between devices with their start and end apart: 11, of which 5 were waited for; matrix products, arithmetic and copies ran while one was open for 4% of the time, Pallas kernels for 10%

profile of v5, /device:TPU:0, one launch (start us, length us, event | category | flops | bytes accessed | tf_op | source)
XLA Modules:
  0.0 33.5 jit_solution(10161968694966558494)
XLA Ops:
  0.6 0.0 copy-start
  0.7 0.0 copy-start.2
  0.7 0.5 %collective-permute-start = (bf16[256,768]{1,0:T(8,128)(2,1)}, bf16[256,768]{1,0:T(8,128)(2,1)S(1)}, u32[]{:S(2)}, u32[]{:S(2)}) collective-permute-start(bf16[256,768]{1,0:T(8,128)(2,1)} %refs_0_.1), channel_id=1, source_target_pairs={{0,4},{4,0},{8,12},{12,8},{16,20},{20,16},{24,28},{28,24},{1,5},{5... | collective-permute-start | bytes 1179656 | tf_op jit(solution)/shard_map/ppermute | solution.py:155
  1.2 1.0 %constant_dynamic-slice_fusion = (bf16[4,1,48,512]{3,2,1,0:T(8,128)(2,1)S(1)}, bf16[4,1,48,512]{3,2,1,0:T(8,128)(2,1)S(1)}) fusion(bf16[4,2,48,512]{3,2,1,0:T(8,128)(2,1)} %bitcast.21, s32[]{:T(128)S(6)} %select_n.36, s32[]{:T(128)S(6)} %select_n.35), kind=kLoop, calls=%fused_computation.3 | loop fusion | bytes 786440 | tf_op jit(solution)/shard_map/jit(dynamic_index_in_dim)/dynamic_slice | solution.py:166
  2.2 0.2 collective-permute-start.2
  2.4 0.4 %collective-permute-start.1 = (s32[1,256]{1,0:T(1,128)}, s32[1,256]{1,0:T(1,128)S(1)}, u32[]{:S(2)}, u32[]{:S(2)}) collective-permute-start(s32[1,256]{1,0:T(1,128)} %bitcast.19), channel_id=1, source_target_pairs={{0,4},{4,0},{8,12},{12,8},{16,20},{20,16},{24,28},{28,24},{1,5},{5... | collective-permute-start | bytes 3080 | tf_op jit(solution)/shard_map/ppermute | solution.py:155
  2.8 3.8 %collective-permute-start.4 = (bf16[48,768]{1,0:T(8,128)(2,1)S(1)}, bf16[48,768]{1,0:T(8,128)(2,1)S(1)}, u32[]{:S(2)}, u32[]{:S(2)}) collective-permute-start(bf16[48,768]{1,0:T(8,128)(2,1)S(1)} %constant_dynamic-slice_fusion.2.block_ref.refs_0_), channel_id=1, source_target_pairs={{0,2},{1,3},{2,0},{3,1},{4,6},{5,7},{6,4},{7,5},{8,10},{9,11},{10,... | collective-permute-start | bytes 221192 | tf_op jit(solution)/shard_map/ppermute | solution.py:155
  6.6 1.3 %collective-permute-start.5 = (bf16[48,768]{1,0:T(8,128)(2,1)S(1)}, bf16[48,768]{1,0:T(8,128)(2,1)S(1)}, u32[]{:S(2)}, u32[]{:S(2)}) collective-permute-start(bf16[48,768]{1,0:T(8,128)(2,1)S(1)} %constant_dynamic-slice_fusion.2.block_ref.refs_0_), channel_id=1, source_target_pairs={{0,3},{1,2},{2,1},{3,0},{4,7},{5,6},{6,5},{7,4},{8,11},{9,10},{10,... | collective-permute-start | bytes 221192 | tf_op jit(solution)/shard_map/ppermute | solution.py:155
  8.7 1.6 %collective-permute-start.6 = (bf16[192,512]{1,0:T(8,128)(2,1)S(1)}, bf16[192,512]{1,0:T(8,128)(2,1)S(1)}, u32[]{:S(2)}, u32[]{:S(2)}) collective-permute-start(bf16[192,512]{1,0:T(8,128)(2,1)S(1)} %shard_map.69.after_ref), channel_id=1, source_target_pairs={{0,8},{4,12},{8,0},{12,4},{16,24},{20,28},{24,16},{28,20},{1,9},{5... | collective-permute-start | bytes 589832 | tf_op jit(solution)/shard_map/ppermute | solution.py:155
  10.2 0.2 collective-permute-start.3
  10.5 0.1 pad_add_fusion.place_ref
  10.5 1.1 %shard_map.68 = (bf16[2,512,768]{2,1,0:T(8,128)(2,1)S(1)}, bf16[512,64]{1,0:T(8,128)(2,1)S(1)}) custom-call(bf16[256,768]{1,0:T(8,128)(2,1)S(1)} %copy-done.1, s32[1,256]{1,0:T(1,128)S(1)} %bitcast.20, bf16[256,768]{1,0:T(8,128)(2,1)S(1)} %collective-permute-done.refs_2_.refs_0_, s32[1,256]{1,0:T(1,128)S(1)} %collective-permute-done.1.refs_3_.refs_1_), custom_call_target="tpu_custom_call" | custom-call | tf_op jit(solution)/shard_map/pallas_call | solution.py:140
  11.7 1.2 %collective-permute-done.4.refs_2_ = bf16[48,768]{1,0:T(8,128)(2,1)S(1)} collective-permute-done((bf16[48,768]{1,0:T(8,128)(2,1)S(1)}, bf16[48,768]{1,0:T(8,128)(2,1)S(1)}, u32[]{:S(2)}, u32[]{:S(2)}) %collective-permute-start.4) | collective-permute-done | bytes 73760 | tf_op jit(solution)/shard_map/ppermute | solution.py:155
  12.9 1.7 %collective-permute-done.3.refs_1_ = bf16[48,768]{1,0:T(8,128)(2,1)S(1)} collective-permute-done((bf16[48,768]{1,0:T(8,128)(2,1)S(1)}, bf16[48,768]{1,0:T(8,128)(2,1)S(1)}, u32[]{:S(2)}, u32[]{:S(2)}) %collective-permute-start.3) | collective-permute-done | bytes 73760 | tf_op jit(solution)/shard_map/ppermute | solution.py:155
  14.6 0.7 %shard_map.71 = (bf16[192,768]{1,0:T(8,128)(2,1)S(1)}, s32[1,512]{1,0:T(1,128)S(1)}) custom-call(s32[2]{0:T(128)S(1)} %pad_add_fusion.place_ref, bf16[512,64]{1,0:T(8,128)(2,1)S(1)} %get-tuple-element.9.after_ref.refs_1_, bf16[48,768]{1,0:T(8,128)(2,1)S(1)} %constant_dynamic-slice_fusion.2.block_ref.refs_0_, ...), custom_call_target="tpu_custom_call" | custom-call | tf_op jit(solution)/shard_map/pallas_call | solution.py:140
  15.3 0.1 collective-permute-done.6
  15.5 1.6 %collective-permute-start.7 = (bf16[192,512]{1,0:T(8,128)(2,1)S(1)}, bf16[192,512]{1,0:T(8,128)(2,1)S(1)}, u32[]{:S(2)}, u32[]{:S(2)}) collective-permute-start(bf16[192,512]{1,0:T(8,128)(2,1)S(1)} %broadcast_select_fusion), channel_id=1, source_target_pairs={{0,16},{4,20},{8,24},{12,28},{16,0},{20,4},{24,8},{28,12},{1,17},{... | collective-permute-start | bytes 589832 | tf_op jit(solution)/shard_map/ppermute | solution.py:155
  17.0 1.4 %shard_map.72 = bf16[1024,256]{1,0:T(8,128)(2,1)} custom-call(bf16[2,512,768]{2,1,0:T(8,128)(2,1)S(1)} %get-tuple-element.8.refs_0_, bf16[512,64]{1,0:T(8,128)(2,1)S(1)} %get-tuple-element.9.after_ref.refs_1_, bf16[192,768]{1,0:T(8,128)(2,1)S(1)} %get-tuple-element.10.refs_2_), custom_call_target="tpu_custom_call" | custom-call | tf_op jit(solution)/shard_map/pallas_call | solution.py:140
  18.4 3.5 %all-to-all-start = ((bf16[8,128,256]{2,1,0:T(8,128)(2,1)}), bf16[8,128,256]{2,1,0:T(8,128)(2,1)S(1)}, u32[]{:S(2)}, u32[]{:S(2)}) async-start(bf16[8,128,256]{2,1,0:T(8,128)(2,1)} %bitcast.9), calls=%async_computation | async-start | bytes 1048576 | tf_op jit(solution)/shard_map/all_to_all | solution.py:176
  22.0 0.5 %collective-permute-start.8 = (bf16[96,512]{1,0:T(8,128)(2,1)S(1)}, bf16[96,512]{1,0:T(8,128)(2,1)S(1)}, u32[]{:S(2)}, u32[]{:S(2)}) collective-permute-start(bf16[96,512]{1,0:T(8,128)(2,1)S(1)} %get-tuple-element.17), channel_id=1, source_target_pairs={{0,4},{4,0},{8,12},{12,8},{16,20},{20,16},{24,28},{28,24},{1,5},{5... | collective-permute-start | bytes 294920 | tf_op jit(solution)/shard_map/ppermute | solution.py:155
  22.5 0.9 %collective-permute-done.8.after_ref.refs_3_ = bf16[96,512]{1,0:T(8,128)(2,1)S(1)} collective-permute-done((bf16[96,512]{1,0:T(8,128)(2,1)S(1)}, bf16[96,512]{1,0:T(8,128)(2,1)S(1)}, u32[]{:S(2)}, u32[]{:S(2)}) %collective-permute-start.8) | collective-permute-done | bytes 98336 | tf_op jit(solution)/shard_map/ppermute | solution.py:155
  23.4 0.4 %collective-permute-start.9 = (bf16[96,512]{1,0:T(8,128)(2,1)S(1)}, bf16[96,512]{1,0:T(8,128)(2,1)S(1)}, u32[]{:S(2)}, u32[]{:S(2)}) collective-permute-start(bf16[96,512]{1,0:T(8,128)(2,1)S(1)} %shard_map.73), channel_id=1, source_target_pairs={{0,4},{4,0},{8,12},{12,8},{16,20},{20,16},{24,28},{28,24},{1,5},{5... | collective-permute-start | bytes 294920 | tf_op jit(solution)/shard_map/ppermute | solution.py:155
  23.8 7.8 %all-to-all-done = bf16[8,128,256]{2,1,0:T(8,128)(2,1)S(1)} async-done(((bf16[8,128,256]{2,1,0:T(8,128)(2,1)}), bf16[8,128,256]{2,1,0:T(8,128)(2,1)S(1)}, u32[]{:S(2)}, u32[]{:S(2)}) %all-to-all-start) | async-done | bytes 524320 | tf_op jit(solution)/shard_map/all_to_all | solution.py:176
  31.6 1.9 %shard_map.74 = (f32[512,512]{1,0:T(8,128)}, s32[1,512]{1,0:T(1,128)}) custom-call(s32[1]{0:T(128)} %bitcast.refs_0_, bf16[4,2,128,256]{3,2,1,0:T(8,128)(2,1)S(1)} %bitcast.17, bf16[192,512]{1,0:T(8,128)(2,1)S(1)} %broadcast_select_fusion.1.refs_2_, bf16[96,512]{1,0:T(8,128)(2,1)S(1)} %collective-permute-done.8.after_ref.refs_3_, ...), custom_call_target="tpu_custom_call" | custom-call | tf_op jit(solution)/shard_map/pallas_call | solution.py:140
  (18 shorter events, 0.2 us)
Async XLA Ops:
  0.6 2.2 %copy-start = (bf16[96,768]{1,0:T(8,128)(2,1)S(1)}, bf16[96,768]{1,0:T(8,128)(2,1)}, u32[]{:S(2)}) copy-start(bf16[96,768]{1,0:T(8,128)(2,1)} %param.6) | copy-start | bytes 442372
  0.6 9.9 %copy-start.1 = (bf16[256,768]{1,0:T(8,128)(2,1)S(1)}, bf16[256,768]{1,0:T(8,128)(2,1)}, u32[]{:S(2)}) copy-start(bf16[256,768]{1,0:T(8,128)(2,1)} %refs_0_.1) | copy-start | bytes 1179652
  0.7 9.9 %copy-start.2 = (s32[256]{0:T(256)S(1)}, s32[256]{0:T(256)}, u32[]{:S(2)}) copy-start(s32[256]{0:T(256)} %param.9) | copy-start | bytes 3076
  0.7 7.9 %collective-permute-start = (bf16[256,768]{1,0:T(8,128)(2,1)}, bf16[256,768]{1,0:T(8,128)(2,1)S(1)}, u32[]{:S(2)}, u32[]{:S(2)}) collective-permute-start(bf16[256,768]{1,0:T(8,128)(2,1)} %refs_0_.1), channel_id=1, source_target_pairs={{0,4},{4,0},{8,12},{12,8},{16,20},{20,16},{24,28},{28,24},{1,5},{5... | collective-permute-start | bytes 1179656 | tf_op jit(solution)/shard_map/ppermute | solution.py:155
  2.2 6.4 %collective-permute-start.2 = (bf16[192,512]{1,0:T(8,128)(2,1)S(1)}, bf16[192,512]{1,0:T(8,128)(2,1)S(1)}, u32[]{:S(2)}, u32[]{:S(2)}) collective-permute-start(bf16[192,512]{1,0:T(8,128)(2,1)S(1)} %bitcast.22), channel_id=1, source_target_pairs={{0,4},{4,0},{8,12},{12,8},{16,20},{20,16},{24,28},{28,24},{1,5},{5... | collective-permute-start | bytes 589832 | tf_op jit(solution)/shard_map/ppermute | solution.py:155
  2.4 6.2 %collective-permute-start.1 = (s32[1,256]{1,0:T(1,128)}, s32[1,256]{1,0:T(1,128)S(1)}, u32[]{:S(2)}, u32[]{:S(2)}) collective-permute-start(s32[1,256]{1,0:T(1,128)} %bitcast.19), channel_id=1, source_target_pairs={{0,4},{4,0},{8,12},{12,8},{16,20},{20,16},{24,28},{28,24},{1,5},{5... | collective-permute-start | bytes 3080 | tf_op jit(solution)/shard_map/ppermute | solution.py:155
  2.8 10.1 %collective-permute-start.4 = (bf16[48,768]{1,0:T(8,128)(2,1)S(1)}, bf16[48,768]{1,0:T(8,128)(2,1)S(1)}, u32[]{:S(2)}, u32[]{:S(2)}) collective-permute-start(bf16[48,768]{1,0:T(8,128)(2,1)S(1)} %constant_dynamic-slice_fusion.2.block_ref.refs_0_), channel_id=1, source_target_pairs={{0,2},{1,3},{2,0},{3,1},{4,6},{5,7},{6,4},{7,5},{8,10},{9,11},{10,... | collective-permute-start | bytes 221192 | tf_op jit(solution)/shard_map/ppermute | solution.py:155
  6.6 6.3 %collective-permute-start.5 = (bf16[48,768]{1,0:T(8,128)(2,1)S(1)}, bf16[48,768]{1,0:T(8,128)(2,1)S(1)}, u32[]{:S(2)}, u32[]{:S(2)}) collective-permute-start(bf16[48,768]{1,0:T(8,128)(2,1)S(1)} %constant_dynamic-slice_fusion.2.block_ref.refs_0_), channel_id=1, source_target_pairs={{0,3},{1,2},{2,1},{3,0},{4,7},{5,6},{6,5},{7,4},{8,11},{9,10},{10,... | collective-permute-start | bytes 221192 | tf_op jit(solution)/shard_map/ppermute | solution.py:155
  8.7 6.7 %collective-permute-start.6 = (bf16[192,512]{1,0:T(8,128)(2,1)S(1)}, bf16[192,512]{1,0:T(8,128)(2,1)S(1)}, u32[]{:S(2)}, u32[]{:S(2)}) collective-permute-start(bf16[192,512]{1,0:T(8,128)(2,1)S(1)} %shard_map.69.after_ref), channel_id=1, source_target_pairs={{0,8},{4,12},{8,0},{12,4},{16,24},{20,28},{24,16},{28,20},{1,9},{5... | collective-permute-start | bytes 589832 | tf_op jit(solution)/shard_map/ppermute | solution.py:155
  10.2 4.4 %collective-permute-start.3 = (bf16[48,768]{1,0:T(8,128)(2,1)S(1)}, bf16[48,768]{1,0:T(8,128)(2,1)S(1)}, u32[]{:S(2)}, u32[]{:S(2)}) collective-permute-start(bf16[48,768]{1,0:T(8,128)(2,1)S(1)} %shard_map.70), channel_id=1, source_target_pairs={{0,1},{1,0},{2,3},{3,2},{4,5},{5,4},{6,7},{7,6},{8,9},{9,8},{10,11... | collective-permute-start | bytes 221192 | tf_op jit(solution)/shard_map/ppermute | solution.py:155
  15.5 6.5 %collective-permute-start.7 = (bf16[192,512]{1,0:T(8,128)(2,1)S(1)}, bf16[192,512]{1,0:T(8,128)(2,1)S(1)}, u32[]{:S(2)}, u32[]{:S(2)}) collective-permute-start(bf16[192,512]{1,0:T(8,128)(2,1)S(1)} %broadcast_select_fusion), channel_id=1, source_target_pairs={{0,16},{4,20},{8,24},{12,28},{16,0},{20,4},{24,8},{28,12},{1,17},{... | collective-permute-start | bytes 589832 | tf_op jit(solution)/shard_map/ppermute | solution.py:155
  18.4 13.2 %all-to-all-start = ((bf16[8,128,256]{2,1,0:T(8,128)(2,1)}), bf16[8,128,256]{2,1,0:T(8,128)(2,1)S(1)}, u32[]{:S(2)}, u32[]{:S(2)}) async-start(bf16[8,128,256]{2,1,0:T(8,128)(2,1)} %bitcast.9), calls=%async_computation | async-start | bytes 1048576 | tf_op jit(solution)/shard_map/all_to_all | solution.py:176
  22.0 1.4 %collective-permute-start.8 = (bf16[96,512]{1,0:T(8,128)(2,1)S(1)}, bf16[96,512]{1,0:T(8,128)(2,1)S(1)}, u32[]{:S(2)}, u32[]{:S(2)}) collective-permute-start(bf16[96,512]{1,0:T(8,128)(2,1)S(1)} %get-tuple-element.17), channel_id=1, source_target_pairs={{0,4},{4,0},{8,12},{12,8},{16,20},{20,16},{24,28},{28,24},{1,5},{5... | collective-permute-start | bytes 294920 | tf_op jit(solution)/shard_map/ppermute | solution.py:155
  23.4 8.2 %collective-permute-start.9 = (bf16[96,512]{1,0:T(8,128)(2,1)S(1)}, bf16[96,512]{1,0:T(8,128)(2,1)S(1)}, u32[]{:S(2)}, u32[]{:S(2)}) collective-permute-start(bf16[96,512]{1,0:T(8,128)(2,1)S(1)} %shard_map.73), channel_id=1, source_target_pairs={{0,4},{4,0},{8,12},{12,8},{16,20},{20,16},{24,28},{28,24},{1,5},{5... | collective-permute-start | bytes 294920 | tf_op jit(solution)/shard_map/ppermute | solution.py:155

commit v6 on v5

--- a/solution.py
+++ b/solution.py
@@ -59,25 +59,25 @@
             ).astype(jnp.bfloat16)
 
 
-def marks_kernel(place_ref, after_ref, *refs):
-    halves, marks_ref, keep_ref = refs[:-2], refs[-2], refs[-1]
-    half = halves[0].shape[0]
+def keep_kernel(place_ref, *refs):
+    refs[-1][...] = jnp.full(refs[-1].shape, place_ref[1], jnp.int32)
+
+
+def pick_kernel(keep_ref, mine_ref, met_ref, *refs):
+    refs[-1][...] = jnp.where(keep_ref[0] != 0, mine_ref[...], met_ref[...])
+
+
+def pass_kernel(block_ref, after_ref, out_ref):
+    out_ref[...] = block_ref[...]
+
+
+def rows_kernel(groups, capacity, place_ref, points_ref, tags_ref, *refs):
+    halves, (out_ref, marks_ref, blocks_ref, sems) = refs[:-4], refs[-4:]
+    half, marks = halves[0].shape[0], marks_ref.shape[0]
     for away, block in enumerate(halves):
         first = pl.multiple_of(lax.bitwise_xor(place_ref[0], away) * half, 16)
         marks_ref[pl.ds(first, half), :] = unit_rows(block[...])
-    keep_ref[...] = jnp.full(keep_ref.shape, place_ref[1], jnp.int32)
-
-
-def pick_kernel(keep_ref, mine_ref, met_ref, *refs):
-    refs[-1][...] = jnp.where(keep_ref[0] != 0, mine_ref[...], met_ref[...])
-
-
-def pass_kernel(block_ref, after_ref, out_ref):
-    out_ref[...] = block_ref[...]
-
-
-def rows_kernel(groups, capacity, points_ref, tags_ref, marks_ref, out_ref):
-    marks = marks_ref.shape[0]
+    copies = []
     no_tags = jnp.zeros(tags_ref.shape, jnp.bfloat16)
     for core, tags in enumerate((tags_ref[...], no_tags)):
         scores = lax.dot_general(
@@ -87,12 +87,20 @@
         if len(out_ref.shape) == 2:
             for group in range(groups):
                 here = slice(group * capacity, (group + 1) * capacity)
-                first = (2 * group + core) * capacity
-                out_ref[first : first + capacity, :marks] = rows[here]
-                out_ref[first : first + capacity, marks:] = tags[here]
+                there = slice(core * capacity, (core + 1) * capacity)
+                blocks_ref[group, there, :marks] = rows[here]
+                blocks_ref[group, there, marks:] = tags[here]
+                if core == 1:
+                    block = slice(2 * group * capacity, 2 * (group + 1) * capacity)
+                    copies.append(
+                        pltpu.make_async_copy(blocks_ref.at[group], out_ref.at[block, :], sems.at[group])
+                    )
+                    copies[-1].start()
         else:
             out_ref[core, :, :marks] = rows
             out_ref[core, :, marks:] = tags
+    for copy in copies:
+        copy.wait()
 
 
 def sums_kernel(scale, core_ref, arrived_ref, mine_ref, *refs):
@@ -134,14 +142,16 @@
     )[:1].astype(jnp.int32)
 
 
-def call(kernel, shapes, *operands, place=None, scratch=()):
-    held = pl.BlockSpec(memory_space=pltpu.VMEM)
+def call(kernel, shapes, *operands, place=None, scratch=(), sent=()):
+    held, loose = pl.BlockSpec(memory_space=pltpu.VMEM), pl.BlockSpec(memory_space=pl.ANY)
     first = [] if place is None else [place]
     return pl.pallas_call(
         kernel,
         out_shape=shapes,
         in_specs=[pl.BlockSpec(memory_space=pltpu.SMEM)] * len(first) + [held] * len(operands),
-        out_specs=(held,) * len(shapes) if isinstance(shapes, tuple) else held,
+        out_specs=tuple(loose if at in sent else held for at in range(len(shapes)))
+        if isinstance(shapes, tuple)
+        else held,
         scratch_shapes=scratch,
         compiler_params=pltpu.CompilerParams(vmem_limit_bytes=VMEM_LIMIT),
     )(*first, *operands)
@@ -215,19 +225,21 @@
         points_met,
         assignment_met,
     )
-    marks, keep = call(
-        marks_kernel,
-        (array((depth // 2, width)), array((1, columns), jnp.int32)),
+    keep = call(keep_kernel, array((1, columns), jnp.int32), tags, *halves, place=place)
+    whole_tiles = capacity % 16 == 0
+    (rows,) = call(
+        lambda *refs: rows_kernel(groups, capacity, *refs),
+        (array((2 * slots, lanes) if whole_tiles else (2, slots, lanes)),),
+        placed,
         tags,
         *halves,
         place=place,
-    )
-    rows = call(
-        lambda *refs: rows_kernel(groups, capacity, *refs),
-        array((2 * slots, lanes) if capacity % 16 == 0 else (2, slots, lanes)),
-        placed,
-        tags,
-        marks,
+        scratch=[
+            pltpu.VMEM((depth // 2, width), jnp.bfloat16),
+            pltpu.VMEM((groups, 2 * capacity, lanes), jnp.bfloat16),
+            pltpu.SemaphoreType.DMA((groups,)),
+        ],
+        sent=(0,) if whole_tiles else (),
     )
     panel = jnp.where(keep != 0, panel, panel_met)
     for mask in masks[1:]:

time: 33.7 us -> 34.5 us (1.024)
  Pallas kernels: 5.14 us -> 5.75 us
    pallas_call x7, Pallas kernels: 5.14 us -> 5.75 us  [call(): pl.pallas_call(kernel, out_shape=shapes, in_specs=[pl.BlockSpec(memory_sp...]
  transfers between devices with their start and end apart: 11 -> 11, of which waited for: 5 -> 5; matrix products, arithmetic and copies ran while one was open for 4% -> 3% of each run, Pallas kernels for 10% -> 11%
where the time goes in v6:
time: 34.5 us; the launch traced here: 34.3 us
  starting transfers between devices  14 us (41%)
  waiting for transfers between devices  11.9 us (34%)
  Pallas kernels  5.75 us (17%)
  between operations  1.43 us (4%)
  local copies, waits for them, and re-layouts  1.09 us (3%)
    ppermute x10, starting transfers between devices, swap(): lax.ppermute(block, axis, [(i, i ^ mask) for i in range(lax.axis_size(axi...  10.4 us
    all_to_all x1, waiting for transfers between devices, exchange(): lax.all_to_all(rows.reshape(groups, 2 * capacity, lanes), 'pts', split_ax...  7.77 us
    pallas_call x7, Pallas kernels, call(): pl.pallas_call(kernel, out_shape=shapes, in_specs=[pl.BlockSpec(memory_sp...  5.75 us
    ppermute x10, waiting for transfers between devices, swap(): lax.ppermute(block, axis, [(i, i ^ mask) for i in range(lax.axis_size(axi...  4.13 us
    all_to_all x1, starting transfers between devices, exchange(): lax.all_to_all(rows.reshape(groups, 2 * capacity, lanes), 'pts', split_ax...  3.51 us
    dynamic_slice x1, local copies, waits for them, and re-layouts, sides_of(): lax.dynamic_index_in_dim(sides, side, 1, keepdims=False)  1.05 us
  transfers between devices with their start and end apart: 11, of which 5 were waited for; matrix products, arithmetic and copies ran while one was open for 3% of the time, Pallas kernels for 11%

profile of v6, /device:TPU:0, one launch (start us, length us, event | category | flops | bytes accessed | tf_op | source)
XLA Modules:
  0.0 34.3 jit_solution(1638269878006633775)
XLA Ops:
  0.6 0.0 copy-start
  0.7 0.0 copy-start.2
  0.7 0.5 %collective-permute-start = (bf16[256,768]{1,0:T(8,128)(2,1)}, bf16[256,768]{1,0:T(8,128)(2,1)S(1)}, u32[]{:S(2)}, u32[]{:S(2)}) collective-permute-start(bf16[256,768]{1,0:T(8,128)(2,1)} %refs_0_.1), channel_id=1, source_target_pairs={{0,4},{4,0},{8,12},{12,8},{16,20},{20,16},{24,28},{28,24},{1,5},{5... | collective-permute-start | bytes 1179656 | tf_op jit(solution)/shard_map/ppermute | solution.py:165
  1.2 1.0 %constant_dynamic-slice_fusion = (bf16[4,1,48,512]{3,2,1,0:T(8,128)(2,1)S(1)}, bf16[4,1,48,512]{3,2,1,0:T(8,128)(2,1)S(1)}) fusion(bf16[4,2,48,512]{3,2,1,0:T(8,128)(2,1)} %bitcast.21, s32[]{:T(128)S(6)} %select_n.36, s32[]{:T(128)S(6)} %select_n.35), kind=kLoop, calls=%fused_computation.3 | loop fusion | bytes 786440 | tf_op jit(solution)/shard_map/jit(dynamic_index_in_dim)/dynamic_slice | solution.py:176
  2.2 0.2 collective-permute-start.2
  2.4 0.4 %collective-permute-start.1 = (s32[1,256]{1,0:T(1,128)}, s32[1,256]{1,0:T(1,128)S(1)}, u32[]{:S(2)}, u32[]{:S(2)}) collective-permute-start(s32[1,256]{1,0:T(1,128)} %bitcast.19), channel_id=1, source_target_pairs={{0,4},{4,0},{8,12},{12,8},{16,20},{20,16},{24,28},{28,24},{1,5},{5... | collective-permute-start | bytes 3080 | tf_op jit(solution)/shard_map/ppermute | solution.py:165
  2.8 3.8 %collective-permute-start.4 = (bf16[48,768]{1,0:T(8,128)(2,1)S(1)}, bf16[48,768]{1,0:T(8,128)(2,1)S(1)}, u32[]{:S(2)}, u32[]{:S(2)}) collective-permute-start(bf16[48,768]{1,0:T(8,128)(2,1)S(1)} %constant_dynamic-slice_fusion.2.block_ref.refs_3_.refs_1_), channel_id=1, source_target_pairs={{0,2},{1,3},{2,0},{3,1},{4,6},{5,7},{6,4},{7,5},{8,10},{9,11},{10,... | collective-permute-start | bytes 221192 | tf_op jit(solution)/shard_map/ppermute | solution.py:165
  6.6 1.3 %collective-permute-start.5 = (bf16[48,768]{1,0:T(8,128)(2,1)S(1)}, bf16[48,768]{1,0:T(8,128)(2,1)S(1)}, u32[]{:S(2)}, u32[]{:S(2)}) collective-permute-start(bf16[48,768]{1,0:T(8,128)(2,1)S(1)} %constant_dynamic-slice_fusion.2.block_ref.refs_3_.refs_1_), channel_id=1, source_target_pairs={{0,3},{1,2},{2,1},{3,0},{4,7},{5,6},{6,5},{7,4},{8,11},{9,10},{10,... | collective-permute-start | bytes 221192 | tf_op jit(solution)/shard_map/ppermute | solution.py:165
  8.7 1.6 %collective-permute-start.6 = (bf16[192,512]{1,0:T(8,128)(2,1)S(1)}, bf16[192,512]{1,0:T(8,128)(2,1)S(1)}, u32[]{:S(2)}, u32[]{:S(2)}) collective-permute-start(bf16[192,512]{1,0:T(8,128)(2,1)S(1)} %shard_map.69.after_ref), channel_id=1, source_target_pairs={{0,8},{4,12},{8,0},{12,4},{16,24},{20,28},{24,16},{28,20},{1,9},{5... | collective-permute-start | bytes 589832 | tf_op jit(solution)/shard_map/ppermute | solution.py:165
  10.2 0.2 collective-permute-start.3
  10.5 0.1 pad_add_fusion.refs_0_.place_ref
  10.5 1.1 %shard_map.68 = (bf16[2,512,768]{2,1,0:T(8,128)(2,1)S(1)}, bf16[512,64]{1,0:T(8,128)(2,1)S(1)}) custom-call(bf16[256,768]{1,0:T(8,128)(2,1)S(1)} %copy-done.1, s32[1,256]{1,0:T(1,128)S(1)} %bitcast.20, bf16[256,768]{1,0:T(8,128)(2,1)S(1)} %collective-permute-done.refs_2_.refs_0_, s32[1,256]{1,0:T(1,128)S(1)} %collective-permute-done.1.refs_3_.refs_1_), custom_call_target="tpu_custom_call" | custom-call | tf_op jit(solution)/shard_map/pallas_call | solution.py:148
  11.7 1.2 %collective-permute-done.4.refs_5_.refs_3_ = bf16[48,768]{1,0:T(8,128)(2,1)S(1)} collective-permute-done((bf16[48,768]{1,0:T(8,128)(2,1)S(1)}, bf16[48,768]{1,0:T(8,128)(2,1)S(1)}, u32[]{:S(2)}, u32[]{:S(2)}) %collective-permute-start.4) | collective-permute-done | bytes 73760 | tf_op jit(solution)/shard_map/ppermute | solution.py:165
  12.9 1.7 %collective-permute-done.3.refs_4_.refs_2_ = bf16[48,768]{1,0:T(8,128)(2,1)S(1)} collective-permute-done((bf16[48,768]{1,0:T(8,128)(2,1)S(1)}, bf16[48,768]{1,0:T(8,128)(2,1)S(1)}, u32[]{:S(2)}, u32[]{:S(2)}) %collective-permute-start.3) | collective-permute-done | bytes 73760 | tf_op jit(solution)/shard_map/ppermute | solution.py:165
  14.6 0.5 %shard_map.72 = s32[1,512]{1,0:T(1,128)S(1)} custom-call(s32[2]{0:T(128)S(1)} %pad_add_fusion.refs_0_.place_ref, bf16[512,64]{1,0:T(8,128)(2,1)S(1)} %get-tuple-element.7.refs_2_.refs_0_, bf16[48,768]{1,0:T(8,128)(2,1)S(1)} %constant_dynamic-slice_fusion.2.block_ref.refs_3_.refs_1_, bf16[48,768]{1,0:T(8,128)(2,1)S(1)} %collective-permute-done.3.refs_4_.refs_2_, ...), custom_call_target="tpu_custom_call" | custom-call | tf_op jit(solution)/shard_map/pallas_call | solution.py:148
  15.2 0.3 collective-permute-done.6
  15.4 1.6 %collective-permute-start.7 = (bf16[192,512]{1,0:T(8,128)(2,1)S(1)}, bf16[192,512]{1,0:T(8,128)(2,1)S(1)}, u32[]{:S(2)}, u32[]{:S(2)}) collective-permute-start(bf16[192,512]{1,0:T(8,128)(2,1)S(1)} %broadcast_select_fusion), channel_id=1, source_target_pairs={{0,16},{4,20},{8,24},{12,28},{16,0},{20,4},{24,8},{28,12},{1,17},{... | collective-permute-start | bytes 589832 | tf_op jit(solution)/shard_map/ppermute | solution.py:165
  17.0 2.1 %shard_map.71 = bf16[1024,256]{1,0:T(8,128)(2,1)} custom-call(s32[2]{0:T(128)S(1)} %pad_add_fusion.refs_0_.place_ref, bf16[2,512,768]{2,1,0:T(8,128)(2,1)S(1)} %get-tuple-element.6.refs_1_, bf16[512,64]{1,0:T(8,128)(2,1)S(1)} %get-tuple-element.7.refs_2_.refs_0_, bf16[48,768]{1,0:T(8,128)(2,1)S(1)} %constant_dynamic-slice_fusion.2.block_ref.refs_3_.refs_1_, ...), custom_call_target="tpu_custom_call" | custom-call | tf_op jit(solution)/shard_map/pallas_call | solution.py:148
  19.2 3.5 %all-to-all-start = ((bf16[8,128,256]{2,1,0:T(8,128)(2,1)}), bf16[8,128,256]{2,1,0:T(8,128)(2,1)S(1)}, u32[]{:S(2)}, u32[]{:S(2)}) async-start(bf16[8,128,256]{2,1,0:T(8,128)(2,1)} %bitcast.9), calls=%async_computation | async-start | bytes 1048576 | tf_op jit(solution)/shard_map/all_to_all | solution.py:186
  22.8 0.5 %collective-permute-start.8 = (bf16[96,512]{1,0:T(8,128)(2,1)S(1)}, bf16[96,512]{1,0:T(8,128)(2,1)S(1)}, u32[]{:S(2)}, u32[]{:S(2)}) collective-permute-start(bf16[96,512]{1,0:T(8,128)(2,1)S(1)} %get-tuple-element.13), channel_id=1, source_target_pairs={{0,4},{4,0},{8,12},{12,8},{16,20},{20,16},{24,28},{28,24},{1,5},{5... | collective-permute-start | bytes 294920 | tf_op jit(solution)/shard_map/ppermute | solution.py:165
  23.2 0.9 %collective-permute-done.8.after_ref.refs_3_ = bf16[96,512]{1,0:T(8,128)(2,1)S(1)} collective-permute-done((bf16[96,512]{1,0:T(8,128)(2,1)S(1)}, bf16[96,512]{1,0:T(8,128)(2,1)S(1)}, u32[]{:S(2)}, u32[]{:S(2)}) %collective-permute-start.8) | collective-permute-done | bytes 98336 | tf_op jit(solution)/shard_map/ppermute | solution.py:165
  24.2 0.4 %collective-permute-start.9 = (bf16[96,512]{1,0:T(8,128)(2,1)S(1)}, bf16[96,512]{1,0:T(8,128)(2,1)S(1)}, u32[]{:S(2)}, u32[]{:S(2)}) collective-permute-start(bf16[96,512]{1,0:T(8,128)(2,1)S(1)} %shard_map.73), channel_id=1, source_target_pairs={{0,4},{4,0},{8,12},{12,8},{16,20},{20,16},{24,28},{28,24},{1,5},{5... | collective-permute-start | bytes 294920 | tf_op jit(solution)/shard_map/ppermute | solution.py:165
  24.6 7.8 %all-to-all-done = bf16[8,128,256]{2,1,0:T(8,128)(2,1)S(1)} async-done(((bf16[8,128,256]{2,1,0:T(8,128)(2,1)}), bf16[8,128,256]{2,1,0:T(8,128)(2,1)S(1)}, u32[]{:S(2)}, u32[]{:S(2)}) %all-to-all-start) | async-done | bytes 524320 | tf_op jit(solution)/shard_map/all_to_all | solution.py:186
  32.4 1.9 %shard_map.74 = (f32[512,512]{1,0:T(8,128)}, s32[1,512]{1,0:T(1,128)}) custom-call(s32[1]{0:T(128)} %bitcast.refs_0_, bf16[4,2,128,256]{3,2,1,0:T(8,128)(2,1)S(1)} %bitcast.17, bf16[192,512]{1,0:T(8,128)(2,1)S(1)} %broadcast_select_fusion.1.refs_2_, bf16[96,512]{1,0:T(8,128)(2,1)S(1)} %collective-permute-done.8.after_ref.refs_3_, ...), custom_call_target="tpu_custom_call" | custom-call | tf_op jit(solution)/shard_map/pallas_call | solution.py:148
  (18 shorter events, 0.2 us)
Async XLA Ops:
  0.6 2.2 %copy-start = (bf16[96,768]{1,0:T(8,128)(2,1)S(1)}, bf16[96,768]{1,0:T(8,128)(2,1)}, u32[]{:S(2)}) copy-start(bf16[96,768]{1,0:T(8,128)(2,1)} %param.6) | copy-start | bytes 442372
  0.6 9.9 %copy-start.1 = (bf16[256,768]{1,0:T(8,128)(2,1)S(1)}, bf16[256,768]{1,0:T(8,128)(2,1)}, u32[]{:S(2)}) copy-start(bf16[256,768]{1,0:T(8,128)(2,1)} %refs_0_.1) | copy-start | bytes 1179652
  0.7 9.9 %copy-start.2 = (s32[256]{0:T(256)S(1)}, s32[256]{0:T(256)}, u32[]{:S(2)}) copy-start(s32[256]{0:T(256)} %param.9) | copy-start | bytes 3076
  0.7 7.9 %collective-permute-start = (bf16[256,768]{1,0:T(8,128)(2,1)}, bf16[256,768]{1,0:T(8,128)(2,1)S(1)}, u32[]{:S(2)}, u32[]{:S(2)}) collective-permute-start(bf16[256,768]{1,0:T(8,128)(2,1)} %refs_0_.1), channel_id=1, source_target_pairs={{0,4},{4,0},{8,12},{12,8},{16,20},{20,16},{24,28},{28,24},{1,5},{5... | collective-permute-start | bytes 1179656 | tf_op jit(solution)/shard_map/ppermute | solution.py:165
  2.2 6.4 %collective-permute-start.2 = (bf16[192,512]{1,0:T(8,128)(2,1)S(1)}, bf16[192,512]{1,0:T(8,128)(2,1)S(1)}, u32[]{:S(2)}, u32[]{:S(2)}) collective-permute-start(bf16[192,512]{1,0:T(8,128)(2,1)S(1)} %bitcast.22), channel_id=1, source_target_pairs={{0,4},{4,0},{8,12},{12,8},{16,20},{20,16},{24,28},{28,24},{1,5},{5... | collective-permute-start | bytes 589832 | tf_op jit(solution)/shard_map/ppermute | solution.py:165
  2.4 6.2 %collective-permute-start.1 = (s32[1,256]{1,0:T(1,128)}, s32[1,256]{1,0:T(1,128)S(1)}, u32[]{:S(2)}, u32[]{:S(2)}) collective-permute-start(s32[1,256]{1,0:T(1,128)} %bitcast.19), channel_id=1, source_target_pairs={{0,4},{4,0},{8,12},{12,8},{16,20},{20,16},{24,28},{28,24},{1,5},{5... | collective-permute-start | bytes 3080 | tf_op jit(solution)/shard_map/ppermute | solution.py:165
  2.8 10.1 %collective-permute-start.4 = (bf16[48,768]{1,0:T(8,128)(2,1)S(1)}, bf16[48,768]{1,0:T(8,128)(2,1)S(1)}, u32[]{:S(2)}, u32[]{:S(2)}) collective-permute-start(bf16[48,768]{1,0:T(8,128)(2,1)S(1)} %constant_dynamic-slice_fusion.2.block_ref.refs_3_.refs_1_), channel_id=1, source_target_pairs={{0,2},{1,3},{2,0},{3,1},{4,6},{5,7},{6,4},{7,5},{8,10},{9,11},{10,... | collective-permute-start | bytes 221192 | tf_op jit(solution)/shard_map/ppermute | solution.py:165
  6.6 6.3 %collective-permute-start.5 = (bf16[48,768]{1,0:T(8,128)(2,1)S(1)}, bf16[48,768]{1,0:T(8,128)(2,1)S(1)}, u32[]{:S(2)}, u32[]{:S(2)}) collective-permute-start(bf16[48,768]{1,0:T(8,128)(2,1)S(1)} %constant_dynamic-slice_fusion.2.block_ref.refs_3_.refs_1_), channel_id=1, source_target_pairs={{0,3},{1,2},{2,1},{3,0},{4,7},{5,6},{6,5},{7,4},{8,11},{9,10},{10,... | collective-permute-start | bytes 221192 | tf_op jit(solution)/shard_map/ppermute | solution.py:165
  8.7 6.7 %collective-permute-start.6 = (bf16[192,512]{1,0:T(8,128)(2,1)S(1)}, bf16[192,512]{1,0:T(8,128)(2,1)S(1)}, u32[]{:S(2)}, u32[]{:S(2)}) collective-permute-start(bf16[192,512]{1,0:T(8,128)(2,1)S(1)} %shard_map.69.after_ref), channel_id=1, source_target_pairs={{0,8},{4,12},{8,0},{12,4},{16,24},{20,28},{24,16},{28,20},{1,9},{5... | collective-permute-start | bytes 589832 | tf_op jit(solution)/shard_map/ppermute | solution.py:165
  10.2 4.4 %collective-permute-start.3 = (bf16[48,768]{1,0:T(8,128)(2,1)S(1)}, bf16[48,768]{1,0:T(8,128)(2,1)S(1)}, u32[]{:S(2)}, u32[]{:S(2)}) collective-permute-start(bf16[48,768]{1,0:T(8,128)(2,1)S(1)} %shard_map.70), channel_id=1, source_target_pairs={{0,1},{1,0},{2,3},{3,2},{4,5},{5,4},{6,7},{7,6},{8,9},{9,8},{10,11... | collective-permute-start | bytes 221192 | tf_op jit(solution)/shard_map/ppermute | solution.py:165
  15.4 7.3 %collective-permute-start.7 = (bf16[192,512]{1,0:T(8,128)(2,1)S(1)}, bf16[192,512]{1,0:T(8,128)(2,1)S(1)}, u32[]{:S(2)}, u32[]{:S(2)}) collective-permute-start(bf16[192,512]{1,0:T(8,128)(2,1)S(1)} %broadcast_select_fusion), channel_id=1, source_target_pairs={{0,16},{4,20},{8,24},{12,28},{16,0},{20,4},{24,8},{28,12},{1,17},{... | collective-permute-start | bytes 589832 | tf_op jit(solution)/shard_map/ppermute | solution.py:165
  19.2 13.2 %all-to-all-start = ((bf16[8,128,256]{2,1,0:T(8,128)(2,1)}), bf16[8,128,256]{2,1,0:T(8,128)(2,1)S(1)}, u32[]{:S(2)}, u32[]{:S(2)}) async-start(bf16[8,128,256]{2,1,0:T(8,128)(2,1)} %bitcast.9), calls=%async_computation | async-start | bytes 1048576 | tf_op jit(solution)/shard_map/all_to_all | solution.py:186
  22.8 1.4 %collective-permute-start.8 = (bf16[96,512]{1,0:T(8,128)(2,1)S(1)}, bf16[96,512]{1,0:T(8,128)(2,1)S(1)}, u32[]{:S(2)}, u32[]{:S(2)}) collective-permute-start(bf16[96,512]{1,0:T(8,128)(2,1)S(1)} %get-tuple-element.13), channel_id=1, source_target_pairs={{0,4},{4,0},{8,12},{12,8},{16,20},{20,16},{24,28},{28,24},{1,5},{5... | collective-permute-start | bytes 294920 | tf_op jit(solution)/shard_map/ppermute | solution.py:165
  24.2 8.2 %collective-permute-start.9 = (bf16[96,512]{1,0:T(8,128)(2,1)S(1)}, bf16[96,512]{1,0:T(8,128)(2,1)S(1)}, u32[]{:S(2)}, u32[]{:S(2)}) collective-permute-start(bf16[96,512]{1,0:T(8,128)(2,1)S(1)} %shard_map.73), channel_id=1, source_target_pairs={{0,4},{4,0},{8,12},{12,8},{16,20},{20,16},{24,28},{28,24},{1,5},{5... | collective-permute-start | bytes 294920 | tf_op jit(solution)/shard_map/ppermute | solution.py:165

commit v7 on v5

--- a/solution.py
+++ b/solution.py
@@ -59,13 +59,13 @@
             ).astype(jnp.bfloat16)
 
 
-def marks_kernel(place_ref, after_ref, *refs):
+def marks_kernel(line_ref, choice_ref, after_ref, *refs):
     halves, marks_ref, keep_ref = refs[:-2], refs[-2], refs[-1]
     half = halves[0].shape[0]
     for away, block in enumerate(halves):
-        first = pl.multiple_of(lax.bitwise_xor(place_ref[0], away) * half, 16)
+        first = pl.multiple_of(lax.bitwise_xor(line_ref[0], away) * half, 16)
         marks_ref[pl.ds(first, half), :] = unit_rows(block[...])
-    keep_ref[...] = jnp.full(keep_ref.shape, place_ref[1], jnp.int32)
+    keep_ref[...] = jnp.full(keep_ref.shape, choice_ref[0], jnp.int32)
 
 
 def pick_kernel(keep_ref, mine_ref, met_ref, *refs):
@@ -134,9 +134,9 @@
     )[:1].astype(jnp.int32)
 
 
-def call(kernel, shapes, *operands, place=None, scratch=()):
+def call(kernel, shapes, *operands, place=(), scratch=()):
     held = pl.BlockSpec(memory_space=pltpu.VMEM)
-    first = [] if place is None else [place]
+    first = [scalar.astype(jnp.int32).reshape(1) for scalar in place]
     return pl.pallas_call(
         kernel,
         out_shape=shapes,
@@ -156,8 +156,7 @@
 
 
 def pick(keep, mine, met, *after):
-    keep = keep.astype(jnp.int32).reshape(1)
-    return call(pick_kernel, array(mine.shape), mine, met, *after, place=keep)
+    return call(pick_kernel, array(mine.shape), mine, met, *after, place=(keep,))
 
 
 def sides_of(panel, parts, core):
@@ -206,7 +205,6 @@
     ]
     masks = [1 << bit for bit in range(1, groups.bit_length() - 1)]
     panel_met = swap(panel, "pts", masks[0])
-    place = jnp.stack([lax.axis_index("lmk"), (differs & masks[0]) == 0]).astype(jnp.int32)
     placed, tags = call(
         lambda *refs: place_kernel(groups, capacity, *refs),
         (array((2, slots, width)), array((slots, lanes - depth // 2))),
@@ -220,7 +218,7 @@
         (array((depth // 2, width)), array((1, columns), jnp.int32)),
         tags,
         *halves,
-        place=place,
+        place=(lax.axis_index("lmk"), (differs & masks[0]) == 0),
     )
     rows = call(
         lambda *refs: rows_kernel(groups, capacity, *refs),
@@ -242,7 +240,7 @@
         arrived,
         panel,
         *others,
-        place=(me % 2).astype(jnp.int32).reshape(1),
+        place=(me % 2,),
         scratch=[
             pltpu.VMEM((2, lanes, columns), jnp.bfloat16),
             pltpu.VMEM((2, slots, lanes), jnp.bfloat16),

time: 33.7 us -> 35.1 us (1.042)
  waiting for transfers between devices: 11.8 us -> 13.5 us
  Pallas kernels: 5.14 us -> 4.61 us
    ppermute x10, waiting for transfers between devices: 4 us -> 5.77 us  [swap(): lax.ppermute(block, axis, [(i, i ^ mask) for i in range(lax.axis_size(axi...]
    pallas_call x7, Pallas kernels: 5.14 us -> 4.61 us  [call(): pl.pallas_call(kernel, out_shape=shapes, in_specs=[pl.BlockSpec(memory_sp...]
  transfers between devices with their start and end apart: 11 -> 11, of which waited for: 5 -> 6; matrix products, arithmetic and copies ran while one was open for 4% -> 3% of each run, Pallas kernels for 10% -> 8%
where the time goes in v7:
time: 35.1 us; the launch traced here: 34.9 us
  starting transfers between devices  14.1 us (40%)
  waiting for transfers between devices  13.5 us (38%)
  Pallas kernels  4.61 us (13%)
  between operations  1.4 us (4%)
  local copies, waits for them, and re-layouts  1.09 us (3%)
    ppermute x10, starting transfers between devices, swap(): lax.ppermute(block, axis, [(i, i ^ mask) for i in range(lax.axis_size(axi...  10.6 us
    all_to_all x1, waiting for transfers between devices, exchange(): lax.all_to_all(rows.reshape(groups, 2 * capacity, lanes), 'pts', split_ax...  7.77 us
    ppermute x10, waiting for transfers between devices, swap(): lax.ppermute(block, axis, [(i, i ^ mask) for i in range(lax.axis_size(axi...  5.77 us
    pallas_call x7, Pallas kernels, call(): pl.pallas_call(kernel, out_shape=shapes, in_specs=[pl.BlockSpec(memory_sp...  4.61 us
    all_to_all x1, starting transfers between devices, exchange(): lax.all_to_all(rows.reshape(groups, 2 * capacity, lanes), 'pts', split_ax...  3.49 us
    dynamic_slice x1, local copies, waits for them, and re-layouts, sides_of(): lax.dynamic_index_in_dim(sides, side, 1, keepdims=False)  1.05 us
  transfers between devices with their start and end apart: 11, of which 6 were waited for; matrix products, arithmetic and copies ran while one was open for 3% of the time, Pallas kernels for 8%

profile of v7, /device:TPU:0, one launch (start us, length us, event | category | flops | bytes accessed | tf_op | source)
XLA Modules:
  0.0 34.9 jit_solution(10379196230284245079)
XLA Ops:
  0.6 0.0 copy-start
  0.7 0.0 copy-start.2
  0.7 0.5 %collective-permute-start = (bf16[256,768]{1,0:T(8,128)(2,1)}, bf16[256,768]{1,0:T(8,128)(2,1)S(1)}, u32[]{:S(2)}, u32[]{:S(2)}) collective-permute-start(bf16[256,768]{1,0:T(8,128)(2,1)} %refs_0_.1), channel_id=1, source_target_pairs={{0,4},{4,0},{8,12},{12,8},{16,20},{20,16},{24,28},{28,24},{1,5},{5... | collective-permute-start | bytes 1179656 | tf_op jit(solution)/shard_map/ppermute | solution.py:155
  1.2 1.0 %constant_dynamic-slice_fusion = (bf16[4,1,48,512]{3,2,1,0:T(8,128)(2,1)S(1)}, bf16[4,1,48,512]{3,2,1,0:T(8,128)(2,1)S(1)}) fusion(bf16[4,2,48,512]{3,2,1,0:T(8,128)(2,1)} %bitcast.21, s32[]{:T(128)S(6)} %select_n.36, s32[]{:T(128)S(6)} %select_n.35), kind=kLoop, calls=%fused_computation.3 | loop fusion | bytes 786440 | tf_op jit(solution)/shard_map/jit(dynamic_index_in_dim)/dynamic_slice | solution.py:165
  2.2 0.2 collective-permute-start.2
  2.4 0.4 %collective-permute-start.1 = (s32[1,256]{1,0:T(1,128)}, s32[1,256]{1,0:T(1,128)S(1)}, u32[]{:S(2)}, u32[]{:S(2)}) collective-permute-start(s32[1,256]{1,0:T(1,128)} %bitcast.19), channel_id=1, source_target_pairs={{0,4},{4,0},{8,12},{12,8},{16,20},{20,16},{24,28},{28,24},{1,5},{5... | collective-permute-start | bytes 3080 | tf_op jit(solution)/shard_map/ppermute | solution.py:155
  3.5 0.5 %collective-permute-done.1.refs_3_.refs_1_ = s32[1,256]{1,0:T(1,128)S(1)} collective-permute-done((s32[1,256]{1,0:T(1,128)}, s32[1,256]{1,0:T(1,128)S(1)}, u32[]{:S(2)}, u32[]{:S(2)}) %collective-permute-start.1) | collective-permute-done | bytes 1056 | tf_op jit(solution)/shard_map/ppermute | solution.py:155
  4.0 2.8 %collective-permute-start.6 = (bf16[192,512]{1,0:T(8,128)(2,1)S(1)}, bf16[192,512]{1,0:T(8,128)(2,1)S(1)}, u32[]{:S(2)}, u32[]{:S(2)}) collective-permute-start(bf16[192,512]{1,0:T(8,128)(2,1)S(1)} %shard_map.69.after_ref), channel_id=1, source_target_pairs={{0,8},{4,12},{8,0},{12,4},{16,24},{20,28},{24,16},{28,20},{1,9},{5... | collective-permute-start | bytes 589832 | tf_op jit(solution)/shard_map/ppermute | solution.py:155
  6.8 2.7 %collective-permute-start.4 = (bf16[48,768]{1,0:T(8,128)(2,1)S(1)}, bf16[48,768]{1,0:T(8,128)(2,1)S(1)}, u32[]{:S(2)}, u32[]{:S(2)}) collective-permute-start(bf16[48,768]{1,0:T(8,128)(2,1)S(1)} %constant_dynamic-slice_fusion.2.block_ref.refs_0_), channel_id=1, source_target_pairs={{0,2},{1,3},{2,0},{3,1},{4,6},{5,7},{6,4},{7,5},{8,10},{9,11},{10,... | collective-permute-start | bytes 221192 | tf_op jit(solution)/shard_map/ppermute | solution.py:155
  9.4 1.3 %collective-permute-start.5 = (bf16[48,768]{1,0:T(8,128)(2,1)S(1)}, bf16[48,768]{1,0:T(8,128)(2,1)S(1)}, u32[]{:S(2)}, u32[]{:S(2)}) collective-permute-start(bf16[48,768]{1,0:T(8,128)(2,1)S(1)} %constant_dynamic-slice_fusion.2.block_ref.refs_0_), channel_id=1, source_target_pairs={{0,3},{1,2},{2,1},{3,0},{4,7},{5,6},{6,5},{7,4},{8,11},{9,10},{10,... | collective-permute-start | bytes 221192 | tf_op jit(solution)/shard_map/ppermute | solution.py:155
  10.8 0.3 collective-permute-start.3
  11.1 1.1 %shard_map.68 = (bf16[2,512,768]{2,1,0:T(8,128)(2,1)S(1)}, bf16[512,64]{1,0:T(8,128)(2,1)S(1)}) custom-call(bf16[256,768]{1,0:T(8,128)(2,1)S(1)} %copy-done.1, s32[1,256]{1,0:T(1,128)S(1)} %bitcast.20, bf16[256,768]{1,0:T(8,128)(2,1)S(1)} %collective-permute-done.refs_2_.refs_0_, s32[1,256]{1,0:T(1,128)S(1)} %collective-permute-done.1.refs_3_.refs_1_), custom_call_target="tpu_custom_call" | custom-call | tf_op jit(solution)/shard_map/pallas_call | solution.py:140
  12.2 3.0 %collective-permute-done.4.refs_2_ = bf16[48,768]{1,0:T(8,128)(2,1)S(1)} collective-permute-done((bf16[48,768]{1,0:T(8,128)(2,1)S(1)}, bf16[48,768]{1,0:T(8,128)(2,1)S(1)}, u32[]{:S(2)}, u32[]{:S(2)}) %collective-permute-start.4) | collective-permute-done | bytes 73760 | tf_op jit(solution)/shard_map/ppermute | solution.py:155
  15.2 0.8 %collective-permute-done.5.refs_3_ = bf16[48,768]{1,0:T(8,128)(2,1)S(1)} collective-permute-done((bf16[48,768]{1,0:T(8,128)(2,1)S(1)}, bf16[48,768]{1,0:T(8,128)(2,1)S(1)}, u32[]{:S(2)}, u32[]{:S(2)}) %collective-permute-start.5) | collective-permute-done | bytes 73760 | tf_op jit(solution)/shard_map/ppermute | solution.py:155
  16.1 0.5 %collective-permute-done.3.refs_1_ = bf16[48,768]{1,0:T(8,128)(2,1)S(1)} collective-permute-done((bf16[48,768]{1,0:T(8,128)(2,1)S(1)}, bf16[48,768]{1,0:T(8,128)(2,1)S(1)}, u32[]{:S(2)}, u32[]{:S(2)}) %collective-permute-start.3) | collective-permute-done | bytes 73760 | tf_op jit(solution)/shard_map/ppermute | solution.py:155
  16.6 0.1 shard_map.71
  16.8 1.6 %collective-permute-start.7 = (bf16[192,512]{1,0:T(8,128)(2,1)S(1)}, bf16[192,512]{1,0:T(8,128)(2,1)S(1)}, u32[]{:S(2)}, u32[]{:S(2)}) collective-permute-start(bf16[192,512]{1,0:T(8,128)(2,1)S(1)} %broadcast_select_fusion), channel_id=1, source_target_pairs={{0,16},{4,20},{8,24},{12,28},{16,0},{20,4},{24,8},{28,12},{1,17},{... | collective-permute-start | bytes 589832 | tf_op jit(solution)/shard_map/ppermute | solution.py:155
  18.4 1.4 %shard_map.72 = bf16[1024,256]{1,0:T(8,128)(2,1)} custom-call(bf16[2,512,768]{2,1,0:T(8,128)(2,1)S(1)} %get-tuple-element.8.refs_0_, bf16[512,64]{1,0:T(8,128)(2,1)S(1)} %get-tuple-element.9.after_ref.refs_1_, bf16[192,768]{1,0:T(8,128)(2,1)S(1)} %get-tuple-element.10.refs_2_), custom_call_target="tpu_custom_call" | custom-call | tf_op jit(solution)/shard_map/pallas_call | solution.py:140
  19.8 3.5 %all-to-all-start = ((bf16[8,128,256]{2,1,0:T(8,128)(2,1)}), bf16[8,128,256]{2,1,0:T(8,128)(2,1)S(1)}, u32[]{:S(2)}, u32[]{:S(2)}) async-start(bf16[8,128,256]{2,1,0:T(8,128)(2,1)} %bitcast.9), calls=%async_computation | async-start | bytes 1048576 | tf_op jit(solution)/shard_map/all_to_all | solution.py:175
  23.3 0.5 %collective-permute-start.8 = (bf16[96,512]{1,0:T(8,128)(2,1)S(1)}, bf16[96,512]{1,0:T(8,128)(2,1)S(1)}, u32[]{:S(2)}, u32[]{:S(2)}) collective-permute-start(bf16[96,512]{1,0:T(8,128)(2,1)S(1)} %get-tuple-element.17), channel_id=1, source_target_pairs={{0,4},{4,0},{8,12},{12,8},{16,20},{20,16},{24,28},{28,24},{1,5},{5... | collective-permute-start | bytes 294920 | tf_op jit(solution)/shard_map/ppermute | solution.py:155
  23.8 0.9 %collective-permute-done.8.after_ref.refs_3_ = bf16[96,512]{1,0:T(8,128)(2,1)S(1)} collective-permute-done((bf16[96,512]{1,0:T(8,128)(2,1)S(1)}, bf16[96,512]{1,0:T(8,128)(2,1)S(1)}, u32[]{:S(2)}, u32[]{:S(2)}) %collective-permute-start.8) | collective-permute-done | bytes 98336 | tf_op jit(solution)/shard_map/ppermute | solution.py:155
  24.7 0.4 %collective-permute-start.9 = (bf16[96,512]{1,0:T(8,128)(2,1)S(1)}, bf16[96,512]{1,0:T(8,128)(2,1)S(1)}, u32[]{:S(2)}, u32[]{:S(2)}) collective-permute-start(bf16[96,512]{1,0:T(8,128)(2,1)S(1)} %shard_map.73), channel_id=1, source_target_pairs={{0,4},{4,0},{8,12},{12,8},{16,20},{20,16},{24,28},{28,24},{1,5},{5... | collective-permute-start | bytes 294920 | tf_op jit(solution)/shard_map/ppermute | solution.py:155
  25.2 7.8 %all-to-all-done = bf16[8,128,256]{2,1,0:T(8,128)(2,1)S(1)} async-done(((bf16[8,128,256]{2,1,0:T(8,128)(2,1)}), bf16[8,128,256]{2,1,0:T(8,128)(2,1)S(1)}, u32[]{:S(2)}, u32[]{:S(2)}) %all-to-all-start) | async-done | bytes 524320 | tf_op jit(solution)/shard_map/all_to_all | solution.py:175
  32.9 1.9 %shard_map.74 = (f32[512,512]{1,0:T(8,128)}, s32[1,512]{1,0:T(1,128)}) custom-call(s32[1]{0:T(128)} %bitcast.refs_0_, bf16[4,2,128,256]{3,2,1,0:T(8,128)(2,1)S(1)} %bitcast.17, bf16[192,512]{1,0:T(8,128)(2,1)S(1)} %broadcast_select_fusion.1.refs_2_, bf16[96,512]{1,0:T(8,128)(2,1)S(1)} %collective-permute-done.8.after_ref.refs_3_, ...), custom_call_target="tpu_custom_call" | custom-call | tf_op jit(solution)/shard_map/pallas_call | solution.py:140
  (17 shorter events, 0.2 us)
Async XLA Ops:
  0.6 6.1 %copy-start = (bf16[96,768]{1,0:T(8,128)(2,1)S(1)}, bf16[96,768]{1,0:T(8,128)(2,1)}, u32[]{:S(2)}) copy-start(bf16[96,768]{1,0:T(8,128)(2,1)} %param.6) | copy-start | bytes 442372
  0.6 10.4 %copy-start.1 = (bf16[256,768]{1,0:T(8,128)(2,1)S(1)}, bf16[256,768]{1,0:T(8,128)(2,1)}, u32[]{:S(2)}) copy-start(bf16[256,768]{1,0:T(8,128)(2,1)} %refs_0_.1) | copy-start | bytes 1179652
  0.7 10.4 %copy-start.2 = (s32[256]{0:T(256)S(1)}, s32[256]{0:T(256)}, u32[]{:S(2)}) copy-start(s32[256]{0:T(256)} %param.9) | copy-start | bytes 3076
  0.7 3.3 %collective-permute-start = (bf16[256,768]{1,0:T(8,128)(2,1)}, bf16[256,768]{1,0:T(8,128)(2,1)S(1)}, u32[]{:S(2)}, u32[]{:S(2)}) collective-permute-start(bf16[256,768]{1,0:T(8,128)(2,1)} %refs_0_.1), channel_id=1, source_target_pairs={{0,4},{4,0},{8,12},{12,8},{16,20},{20,16},{24,28},{28,24},{1,5},{5... | collective-permute-start | bytes 1179656 | tf_op jit(solution)/shard_map/ppermute | solution.py:155
  2.2 1.7 %collective-permute-start.2 = (bf16[192,512]{1,0:T(8,128)(2,1)S(1)}, bf16[192,512]{1,0:T(8,128)(2,1)S(1)}, u32[]{:S(2)}, u32[]{:S(2)}) collective-permute-start(bf16[192,512]{1,0:T(8,128)(2,1)S(1)} %bitcast.22), channel_id=1, source_target_pairs={{0,4},{4,0},{8,12},{12,8},{16,20},{20,16},{24,28},{28,24},{1,5},{5... | collective-permute-start | bytes 589832 | tf_op jit(solution)/shard_map/ppermute | solution.py:155
  2.4 1.5 %collective-permute-start.1 = (s32[1,256]{1,0:T(1,128)}, s32[1,256]{1,0:T(1,128)S(1)}, u32[]{:S(2)}, u32[]{:S(2)}) collective-permute-start(s32[1,256]{1,0:T(1,128)} %bitcast.19), channel_id=1, source_target_pairs={{0,4},{4,0},{8,12},{12,8},{16,20},{20,16},{24,28},{28,24},{1,5},{5... | collective-permute-start | bytes 3080 | tf_op jit(solution)/shard_map/ppermute | solution.py:155
  4.0 12.8 %collective-permute-start.6 = (bf16[192,512]{1,0:T(8,128)(2,1)S(1)}, bf16[192,512]{1,0:T(8,128)(2,1)S(1)}, u32[]{:S(2)}, u32[]{:S(2)}) collective-permute-start(bf16[192,512]{1,0:T(8,128)(2,1)S(1)} %shard_map.69.after_ref), channel_id=1, source_target_pairs={{0,8},{4,12},{8,0},{12,4},{16,24},{20,28},{24,16},{28,20},{1,9},{5... | collective-permute-start | bytes 589832 | tf_op jit(solution)/shard_map/ppermute | solution.py:155
  6.8 8.5 %collective-permute-start.4 = (bf16[48,768]{1,0:T(8,128)(2,1)S(1)}, bf16[48,768]{1,0:T(8,128)(2,1)S(1)}, u32[]{:S(2)}, u32[]{:S(2)}) collective-permute-start(bf16[48,768]{1,0:T(8,128)(2,1)S(1)} %constant_dynamic-slice_fusion.2.block_ref.refs_0_), channel_id=1, source_target_pairs={{0,2},{1,3},{2,0},{3,1},{4,6},{5,7},{6,4},{7,5},{8,10},{9,11},{10,... | collective-permute-start | bytes 221192 | tf_op jit(solution)/shard_map/ppermute | solution.py:155
  9.4 6.6 %collective-permute-start.5 = (bf16[48,768]{1,0:T(8,128)(2,1)S(1)}, bf16[48,768]{1,0:T(8,128)(2,1)S(1)}, u32[]{:S(2)}, u32[]{:S(2)}) collective-permute-start(bf16[48,768]{1,0:T(8,128)(2,1)S(1)} %constant_dynamic-slice_fusion.2.block_ref.refs_0_), channel_id=1, source_target_pairs={{0,3},{1,2},{2,1},{3,0},{4,7},{5,6},{6,5},{7,4},{8,11},{9,10},{10,... | collective-permute-start | bytes 221192 | tf_op jit(solution)/shard_map/ppermute | solution.py:155
  10.8 5.8 %collective-permute-start.3 = (bf16[48,768]{1,0:T(8,128)(2,1)S(1)}, bf16[48,768]{1,0:T(8,128)(2,1)S(1)}, u32[]{:S(2)}, u32[]{:S(2)}) collective-permute-start(bf16[48,768]{1,0:T(8,128)(2,1)S(1)} %shard_map.70), channel_id=1, source_target_pairs={{0,1},{1,0},{2,3},{3,2},{4,5},{5,4},{6,7},{7,6},{8,9},{9,8},{10,11... | collective-permute-start | bytes 221192 | tf_op jit(solution)/shard_map/ppermute | solution.py:155
  16.8 6.5 %collective-permute-start.7 = (bf16[192,512]{1,0:T(8,128)(2,1)S(1)}, bf16[192,512]{1,0:T(8,128)(2,1)S(1)}, u32[]{:S(2)}, u32[]{:S(2)}) collective-permute-start(bf16[192,512]{1,0:T(8,128)(2,1)S(1)} %broadcast_select_fusion), channel_id=1, source_target_pairs={{0,16},{4,20},{8,24},{12,28},{16,0},{20,4},{24,8},{28,12},{1,17},{... | collective-permute-start | bytes 589832 | tf_op jit(solution)/shard_map/ppermute | solution.py:155
  19.8 13.2 %all-to-all-start = ((bf16[8,128,256]{2,1,0:T(8,128)(2,1)}), bf16[8,128,256]{2,1,0:T(8,128)(2,1)S(1)}, u32[]{:S(2)}, u32[]{:S(2)}) async-start(bf16[8,128,256]{2,1,0:T(8,128)(2,1)} %bitcast.9), calls=%async_computation | async-start | bytes 1048576 | tf_op jit(solution)/shard_map/all_to_all | solution.py:175
  23.3 1.4 %collective-permute-start.8 = (bf16[96,512]{1,0:T(8,128)(2,1)S(1)}, bf16[96,512]{1,0:T(8,128)(2,1)S(1)}, u32[]{:S(2)}, u32[]{:S(2)}) collective-permute-start(bf16[96,512]{1,0:T(8,128)(2,1)S(1)} %get-tuple-element.17), channel_id=1, source_target_pairs={{0,4},{4,0},{8,12},{12,8},{16,20},{20,16},{24,28},{28,24},{1,5},{5... | collective-permute-start | bytes 294920 | tf_op jit(solution)/shard_map/ppermute | solution.py:155
  24.7 8.2 %collective-permute-start.9 = (bf16[96,512]{1,0:T(8,128)(2,1)S(1)}, bf16[96,512]{1,0:T(8,128)(2,1)S(1)}, u32[]{:S(2)}, u32[]{:S(2)}) collective-permute-start(bf16[96,512]{1,0:T(8,128)(2,1)S(1)} %shard_map.73), channel_id=1, source_target_pairs={{0,4},{4,0},{8,12},{12,8},{16,20},{20,16},{24,28},{28,24},{1,5},{5... | collective-permute-start | bytes 294920 | tf_op jit(solution)/shard_map/ppermute | solution.py:155

commit v8 on v7

--- a/solution.py
+++ b/solution.py
@@ -19,7 +19,7 @@
     return (widened * scale).astype(jnp.bfloat16)
 
 
-def place_kernel(groups, capacity, *refs):
+def place_kernel(groups, capacity, after_ref, *refs):
     points_out, tags_out = refs[-2:]
     for core in range(2):
         points_ref, assignment_ref = refs[2 * core : 2 * core + 2]
@@ -136,7 +136,7 @@
 
 def call(kernel, shapes, *operands, place=(), scratch=()):
     held = pl.BlockSpec(memory_space=pltpu.VMEM)
-    first = [scalar.astype(jnp.int32).reshape(1) for scalar in place]
+    first = [scalar.astype(jnp.int32).reshape(-1) for scalar in place]
     return pl.pallas_call(
         kernel,
         out_shape=shapes,
@@ -212,6 +212,7 @@
         assignment,
         points_met,
         assignment_met,
+        place=(jnp.stack([lax.axis_index("lmk"), (differs & masks[0]) == 0]).astype(jnp.int32),),
     )
     marks, keep = call(
         marks_kernel,

time: 35.1 us -> 33.7 us (0.960)
  waiting for transfers between devices: 13.5 us -> 11.8 us
  Pallas kernels: 4.61 us -> 5.14 us
    ppermute x10, waiting for transfers between devices: 5.77 us -> 3.99 us  [swap(): lax.ppermute(block, axis, [(i, i ^ mask) for i in range(lax.axis_size(axi...]
    pallas_call x7, Pallas kernels: 4.61 us -> 5.14 us  [call(): pl.pallas_call(kernel, out_shape=shapes, in_specs=[pl.BlockSpec(memory_sp...]
  transfers between devices with their start and end apart: 11 -> 11, of which waited for: 6 -> 5; matrix products, arithmetic and copies ran while one was open for 3% -> 4% of each run, Pallas kernels for 8% -> 10%
where the time goes in v8:
time: 33.7 us; the launch traced here: 33.5 us
  starting transfers between devices  13.9 us (41%)
  waiting for transfers between devices  11.8 us (35%)
  Pallas kernels  5.14 us (15%)
  between operations  1.42 us (4%)
  local copies, waits for them, and re-layouts  1.09 us (3%)
    ppermute x10, starting transfers between devices, swap(): lax.ppermute(block, axis, [(i, i ^ mask) for i in range(lax.axis_size(axi...  10.4 us
    all_to_all x1, waiting for transfers between devices, exchange(): lax.all_to_all(rows.reshape(groups, 2 * capacity, lanes), 'pts', split_ax...  7.77 us
    pallas_call x7, Pallas kernels, call(): pl.pallas_call(kernel, out_shape=shapes, in_specs=[pl.BlockSpec(memory_sp...  5.14 us
    ppermute x10, waiting for transfers between devices, swap(): lax.ppermute(block, axis, [(i, i ^ mask) for i in range(lax.axis_size(axi...  3.99 us
    all_to_all x1, starting transfers between devices, exchange(): lax.all_to_all(rows.reshape(groups, 2 * capacity, lanes), 'pts', split_ax...  3.49 us
    dynamic_slice x1, local copies, waits for them, and re-layouts, sides_of(): lax.dynamic_index_in_dim(sides, side, 1, keepdims=False)  1.05 us
  transfers between devices with their start and end apart: 11, of which 5 were waited for; matrix products, arithmetic and copies ran while one was open for 4% of the time, Pallas kernels for 10%

profile of v8, /device:TPU:0, one launch (start us, length us, event | category | flops | bytes accessed | tf_op | source)
XLA Modules:
  0.0 33.5 jit_solution(7563467398640531604)
XLA Ops:
  0.6 0.0 copy-start
  0.7 0.0 copy-start.2
  0.7 0.5 %collective-permute-start = (bf16[256,768]{1,0:T(8,128)(2,1)}, bf16[256,768]{1,0:T(8,128)(2,1)S(1)}, u32[]{:S(2)}, u32[]{:S(2)}) collective-permute-start(bf16[256,768]{1,0:T(8,128)(2,1)} %refs_1_.1), channel_id=1, source_target_pairs={{0,4},{4,0},{8,12},{12,8},{16,20},{20,16},{24,28},{28,24},{1,5},{5... | collective-permute-start | bytes 1179656 | tf_op jit(solution)/shard_map/ppermute | solution.py:155
  1.2 1.0 %constant_dynamic-slice_fusion = (bf16[4,1,48,512]{3,2,1,0:T(8,128)(2,1)S(1)}, bf16[4,1,48,512]{3,2,1,0:T(8,128)(2,1)S(1)}) fusion(bf16[4,2,48,512]{3,2,1,0:T(8,128)(2,1)} %bitcast.21, s32[]{:T(128)S(6)} %select_n.36, s32[]{:T(128)S(6)} %select_n.35), kind=kLoop, calls=%fused_computation.3 | loop fusion | bytes 786440 | tf_op jit(solution)/shard_map/jit(dynamic_index_in_dim)/dynamic_slice | solution.py:165
  2.2 0.2 collective-permute-start.2
  2.4 0.4 %collective-permute-start.1 = (s32[1,256]{1,0:T(1,128)}, s32[1,256]{1,0:T(1,128)S(1)}, u32[]{:S(2)}, u32[]{:S(2)}) collective-permute-start(s32[1,256]{1,0:T(1,128)} %bitcast.19), channel_id=1, source_target_pairs={{0,4},{4,0},{8,12},{12,8},{16,20},{20,16},{24,28},{28,24},{1,5},{5... | collective-permute-start | bytes 3080 | tf_op jit(solution)/shard_map/ppermute | solution.py:155
  2.8 3.8 %collective-permute-start.4 = (bf16[48,768]{1,0:T(8,128)(2,1)S(1)}, bf16[48,768]{1,0:T(8,128)(2,1)S(1)}, u32[]{:S(2)}, u32[]{:S(2)}) collective-permute-start(bf16[48,768]{1,0:T(8,128)(2,1)S(1)} %constant_dynamic-slice_fusion.2.block_ref.refs_0_), channel_id=1, source_target_pairs={{0,2},{1,3},{2,0},{3,1},{4,6},{5,7},{6,4},{7,5},{8,10},{9,11},{10,... | collective-permute-start | bytes 221192 | tf_op jit(solution)/shard_map/ppermute | solution.py:155
  6.6 1.3 %collective-permute-start.5 = (bf16[48,768]{1,0:T(8,128)(2,1)S(1)}, bf16[48,768]{1,0:T(8,128)(2,1)S(1)}, u32[]{:S(2)}, u32[]{:S(2)}) collective-permute-start(bf16[48,768]{1,0:T(8,128)(2,1)S(1)} %constant_dynamic-slice_fusion.2.block_ref.refs_0_), channel_id=1, source_target_pairs={{0,3},{1,2},{2,1},{3,0},{4,7},{5,6},{6,5},{7,4},{8,11},{9,10},{10,... | collective-permute-start | bytes 221192 | tf_op jit(solution)/shard_map/ppermute | solution.py:155
  8.7 1.6 %collective-permute-start.6 = (bf16[192,512]{1,0:T(8,128)(2,1)S(1)}, bf16[192,512]{1,0:T(8,128)(2,1)S(1)}, u32[]{:S(2)}, u32[]{:S(2)}) collective-permute-start(bf16[192,512]{1,0:T(8,128)(2,1)S(1)} %shard_map.69.after_ref), channel_id=1, source_target_pairs={{0,8},{4,12},{8,0},{12,4},{16,24},{20,28},{24,16},{28,20},{1,9},{5... | collective-permute-start | bytes 589832 | tf_op jit(solution)/shard_map/ppermute | solution.py:155
  10.2 0.2 collective-permute-start.3
  10.5 0.1 pad_add_fusion.refs_0_
  10.5 1.7 %shard_map.68 = (bf16[2,512,768]{2,1,0:T(8,128)(2,1)S(1)}, bf16[512,64]{1,0:T(8,128)(2,1)S(1)}) custom-call(s32[2]{0:T(128)S(1)} %pad_add_fusion.refs_0_, bf16[256,768]{1,0:T(8,128)(2,1)S(1)} %copy-done.1, s32[1,256]{1,0:T(1,128)S(1)} %bitcast.20, bf16[256,768]{1,0:T(8,128)(2,1)S(1)} %collective-permute-done.refs_3_.refs_0_, ...), custom_call_target="tpu_custom_call" | custom-call | tf_op jit(solution)/shard_map/pallas_call | solution.py:140
  12.2 0.7 %collective-permute-done.4.refs_2_ = bf16[48,768]{1,0:T(8,128)(2,1)S(1)} collective-permute-done((bf16[48,768]{1,0:T(8,128)(2,1)S(1)}, bf16[48,768]{1,0:T(8,128)(2,1)S(1)}, u32[]{:S(2)}, u32[]{:S(2)}) %collective-permute-start.4) | collective-permute-done | bytes 73760 | tf_op jit(solution)/shard_map/ppermute | solution.py:155
  12.9 1.7 %collective-permute-done.3.refs_1_ = bf16[48,768]{1,0:T(8,128)(2,1)S(1)} collective-permute-done((bf16[48,768]{1,0:T(8,128)(2,1)S(1)}, bf16[48,768]{1,0:T(8,128)(2,1)S(1)}, u32[]{:S(2)}, u32[]{:S(2)}) %collective-permute-start.3) | collective-permute-done | bytes 73760 | tf_op jit(solution)/shard_map/ppermute | solution.py:155
  14.6 0.1 shard_map.71
  14.8 0.7 %collective-permute-done.6 = bf16[192,512]{1,0:T(8,128)(2,1)S(1)} collective-permute-done((bf16[192,512]{1,0:T(8,128)(2,1)S(1)}, bf16[192,512]{1,0:T(8,128)(2,1)S(1)}, u32[]{:S(2)}, u32[]{:S(2)}) %collective-permute-start.6) | collective-permute-done | bytes 196640 | tf_op jit(solution)/shard_map/ppermute | solution.py:155
  15.5 1.6 %collective-permute-start.7 = (bf16[192,512]{1,0:T(8,128)(2,1)S(1)}, bf16[192,512]{1,0:T(8,128)(2,1)S(1)}, u32[]{:S(2)}, u32[]{:S(2)}) collective-permute-start(bf16[192,512]{1,0:T(8,128)(2,1)S(1)} %broadcast_select_fusion), channel_id=1, source_target_pairs={{0,16},{4,20},{8,24},{12,28},{16,0},{20,4},{24,8},{28,12},{1,17},{... | collective-permute-start | bytes 589832 | tf_op jit(solution)/shard_map/ppermute | solution.py:155
  17.0 1.4 %shard_map.72 = bf16[1024,256]{1,0:T(8,128)(2,1)} custom-call(bf16[2,512,768]{2,1,0:T(8,128)(2,1)S(1)} %get-tuple-element.8.refs_0_, bf16[512,64]{1,0:T(8,128)(2,1)S(1)} %get-tuple-element.9.after_ref.refs_1_, bf16[192,768]{1,0:T(8,128)(2,1)S(1)} %get-tuple-element.10.refs_2_), custom_call_target="tpu_custom_call" | custom-call | tf_op jit(solution)/shard_map/pallas_call | solution.py:140
  18.4 3.5 %all-to-all-start = ((bf16[8,128,256]{2,1,0:T(8,128)(2,1)}), bf16[8,128,256]{2,1,0:T(8,128)(2,1)S(1)}, u32[]{:S(2)}, u32[]{:S(2)}) async-start(bf16[8,128,256]{2,1,0:T(8,128)(2,1)} %bitcast.9), calls=%async_computation | async-start | bytes 1048576 | tf_op jit(solution)/shard_map/all_to_all | solution.py:175
  22.0 0.5 %collective-permute-start.8 = (bf16[96,512]{1,0:T(8,128)(2,1)S(1)}, bf16[96,512]{1,0:T(8,128)(2,1)S(1)}, u32[]{:S(2)}, u32[]{:S(2)}) collective-permute-start(bf16[96,512]{1,0:T(8,128)(2,1)S(1)} %get-tuple-element.17), channel_id=1, source_target_pairs={{0,4},{4,0},{8,12},{12,8},{16,20},{20,16},{24,28},{28,24},{1,5},{5... | collective-permute-start | bytes 294920 | tf_op jit(solution)/shard_map/ppermute | solution.py:155
  22.5 0.9 %collective-permute-done.8.after_ref.refs_3_ = bf16[96,512]{1,0:T(8,128)(2,1)S(1)} collective-permute-done((bf16[96,512]{1,0:T(8,128)(2,1)S(1)}, bf16[96,512]{1,0:T(8,128)(2,1)S(1)}, u32[]{:S(2)}, u32[]{:S(2)}) %collective-permute-start.8) | collective-permute-done | bytes 98336 | tf_op jit(solution)/shard_map/ppermute | solution.py:155
  23.4 0.4 %collective-permute-start.9 = (bf16[96,512]{1,0:T(8,128)(2,1)S(1)}, bf16[96,512]{1,0:T(8,128)(2,1)S(1)}, u32[]{:S(2)}, u32[]{:S(2)}) collective-permute-start(bf16[96,512]{1,0:T(8,128)(2,1)S(1)} %shard_map.73), channel_id=1, source_target_pairs={{0,4},{4,0},{8,12},{12,8},{16,20},{20,16},{24,28},{28,24},{1,5},{5... | collective-permute-start | bytes 294920 | tf_op jit(solution)/shard_map/ppermute | solution.py:155
  23.8 7.8 %all-to-all-done = bf16[8,128,256]{2,1,0:T(8,128)(2,1)S(1)} async-done(((bf16[8,128,256]{2,1,0:T(8,128)(2,1)}), bf16[8,128,256]{2,1,0:T(8,128)(2,1)S(1)}, u32[]{:S(2)}, u32[]{:S(2)}) %all-to-all-start) | async-done | bytes 524320 | tf_op jit(solution)/shard_map/all_to_all | solution.py:175
  31.6 1.9 %shard_map.74 = (f32[512,512]{1,0:T(8,128)}, s32[1,512]{1,0:T(1,128)}) custom-call(s32[1]{0:T(128)} %bitcast.refs_0_, bf16[4,2,128,256]{3,2,1,0:T(8,128)(2,1)S(1)} %bitcast.17, bf16[192,512]{1,0:T(8,128)(2,1)S(1)} %broadcast_select_fusion.1.refs_2_, bf16[96,512]{1,0:T(8,128)(2,1)S(1)} %collective-permute-done.8.after_ref.refs_3_, ...), custom_call_target="tpu_custom_call" | custom-call | tf_op jit(solution)/shard_map/pallas_call | solution.py:140
  (18 shorter events, 0.2 us)
Async XLA Ops:
  0.6 2.2 %copy-start = (bf16[96,768]{1,0:T(8,128)(2,1)S(1)}, bf16[96,768]{1,0:T(8,128)(2,1)}, u32[]{:S(2)}) copy-start(bf16[96,768]{1,0:T(8,128)(2,1)} %param.6) | copy-start | bytes 442372
  0.6 9.9 %copy-start.1 = (bf16[256,768]{1,0:T(8,128)(2,1)S(1)}, bf16[256,768]{1,0:T(8,128)(2,1)}, u32[]{:S(2)}) copy-start(bf16[256,768]{1,0:T(8,128)(2,1)} %refs_1_.1) | copy-start | bytes 1179652
  0.7 9.9 %copy-start.2 = (s32[256]{0:T(256)S(1)}, s32[256]{0:T(256)}, u32[]{:S(2)}) copy-start(s32[256]{0:T(256)} %param.9) | copy-start | bytes 3076
  0.7 7.9 %collective-permute-start = (bf16[256,768]{1,0:T(8,128)(2,1)}, bf16[256,768]{1,0:T(8,128)(2,1)S(1)}, u32[]{:S(2)}, u32[]{:S(2)}) collective-permute-start(bf16[256,768]{1,0:T(8,128)(2,1)} %refs_1_.1), channel_id=1, source_target_pairs={{0,4},{4,0},{8,12},{12,8},{16,20},{20,16},{24,28},{28,24},{1,5},{5... | collective-permute-start | bytes 1179656 | tf_op jit(solution)/shard_map/ppermute | solution.py:155
  2.2 6.4 %collective-permute-start.2 = (bf16[192,512]{1,0:T(8,128)(2,1)S(1)}, bf16[192,512]{1,0:T(8,128)(2,1)S(1)}, u32[]{:S(2)}, u32[]{:S(2)}) collective-permute-start(bf16[192,512]{1,0:T(8,128)(2,1)S(1)} %bitcast.22), channel_id=1, source_target_pairs={{0,4},{4,0},{8,12},{12,8},{16,20},{20,16},{24,28},{28,24},{1,5},{5... | collective-permute-start | bytes 589832 | tf_op jit(solution)/shard_map/ppermute | solution.py:155
  2.4 6.2 %collective-permute-start.1 = (s32[1,256]{1,0:T(1,128)}, s32[1,256]{1,0:T(1,128)S(1)}, u32[]{:S(2)}, u32[]{:S(2)}) collective-permute-start(s32[1,256]{1,0:T(1,128)} %bitcast.19), channel_id=1, source_target_pairs={{0,4},{4,0},{8,12},{12,8},{16,20},{20,16},{24,28},{28,24},{1,5},{5... | collective-permute-start | bytes 3080 | tf_op jit(solution)/shard_map/ppermute | solution.py:155
  2.8 10.1 %collective-permute-start.4 = (bf16[48,768]{1,0:T(8,128)(2,1)S(1)}, bf16[48,768]{1,0:T(8,128)(2,1)S(1)}, u32[]{:S(2)}, u32[]{:S(2)}) collective-permute-start(bf16[48,768]{1,0:T(8,128)(2,1)S(1)} %constant_dynamic-slice_fusion.2.block_ref.refs_0_), channel_id=1, source_target_pairs={{0,2},{1,3},{2,0},{3,1},{4,6},{5,7},{6,4},{7,5},{8,10},{9,11},{10,... | collective-permute-start | bytes 221192 | tf_op jit(solution)/shard_map/ppermute | solution.py:155
  6.6 6.3 %collective-permute-start.5 = (bf16[48,768]{1,0:T(8,128)(2,1)S(1)}, bf16[48,768]{1,0:T(8,128)(2,1)S(1)}, u32[]{:S(2)}, u32[]{:S(2)}) collective-permute-start(bf16[48,768]{1,0:T(8,128)(2,1)S(1)} %constant_dynamic-slice_fusion.2.block_ref.refs_0_), channel_id=1, source_target_pairs={{0,3},{1,2},{2,1},{3,0},{4,7},{5,6},{6,5},{7,4},{8,11},{9,10},{10,... | collective-permute-start | bytes 221192 | tf_op jit(solution)/shard_map/ppermute | solution.py:155
  8.7 6.7 %collective-permute-start.6 = (bf16[192,512]{1,0:T(8,128)(2,1)S(1)}, bf16[192,512]{1,0:T(8,128)(2,1)S(1)}, u32[]{:S(2)}, u32[]{:S(2)}) collective-permute-start(bf16[192,512]{1,0:T(8,128)(2,1)S(1)} %shard_map.69.after_ref), channel_id=1, source_target_pairs={{0,8},{4,12},{8,0},{12,4},{16,24},{20,28},{24,16},{28,20},{1,9},{5... | collective-permute-start | bytes 589832 | tf_op jit(solution)/shard_map/ppermute | solution.py:155
  10.2 4.4 %collective-permute-start.3 = (bf16[48,768]{1,0:T(8,128)(2,1)S(1)}, bf16[48,768]{1,0:T(8,128)(2,1)S(1)}, u32[]{:S(2)}, u32[]{:S(2)}) collective-permute-start(bf16[48,768]{1,0:T(8,128)(2,1)S(1)} %shard_map.70), channel_id=1, source_target_pairs={{0,1},{1,0},{2,3},{3,2},{4,5},{5,4},{6,7},{7,6},{8,9},{9,8},{10,11... | collective-permute-start | bytes 221192 | tf_op jit(solution)/shard_map/ppermute | solution.py:155
  15.5 6.5 %collective-permute-start.7 = (bf16[192,512]{1,0:T(8,128)(2,1)S(1)}, bf16[192,512]{1,0:T(8,128)(2,1)S(1)}, u32[]{:S(2)}, u32[]{:S(2)}) collective-permute-start(bf16[192,512]{1,0:T(8,128)(2,1)S(1)} %broadcast_select_fusion), channel_id=1, source_target_pairs={{0,16},{4,20},{8,24},{12,28},{16,0},{20,4},{24,8},{28,12},{1,17},{... | collective-permute-start | bytes 589832 | tf_op jit(solution)/shard_map/ppermute | solution.py:155
  18.4 13.2 %all-to-all-start = ((bf16[8,128,256]{2,1,0:T(8,128)(2,1)}), bf16[8,128,256]{2,1,0:T(8,128)(2,1)S(1)}, u32[]{:S(2)}, u32[]{:S(2)}) async-start(bf16[8,128,256]{2,1,0:T(8,128)(2,1)} %bitcast.9), calls=%async_computation | async-start | bytes 1048576 | tf_op jit(solution)/shard_map/all_to_all | solution.py:175
  22.0 1.4 %collective-permute-start.8 = (bf16[96,512]{1,0:T(8,128)(2,1)S(1)}, bf16[96,512]{1,0:T(8,128)(2,1)S(1)}, u32[]{:S(2)}, u32[]{:S(2)}) collective-permute-start(bf16[96,512]{1,0:T(8,128)(2,1)S(1)} %get-tuple-element.17), channel_id=1, source_target_pairs={{0,4},{4,0},{8,12},{12,8},{16,20},{20,16},{24,28},{28,24},{1,5},{5... | collective-permute-start | bytes 294920 | tf_op jit(solution)/shard_map/ppermute | solution.py:155
  23.4 8.2 %collective-permute-start.9 = (bf16[96,512]{1,0:T(8,128)(2,1)S(1)}, bf16[96,512]{1,0:T(8,128)(2,1)S(1)}, u32[]{:S(2)}, u32[]{:S(2)}) collective-permute-start(bf16[96,512]{1,0:T(8,128)(2,1)S(1)} %shard_map.73), channel_id=1, source_target_pairs={{0,4},{4,0},{8,12},{12,8},{16,20},{20,16},{24,28},{28,24},{1,5},{5... | collective-permute-start | bytes 294920 | tf_op jit(solution)/shard_map/ppermute | solution.py:155

commit v9 on v8

--- a/solution.py
+++ b/solution.py
@@ -79,11 +79,13 @@
 def rows_kernel(groups, capacity, points_ref, tags_ref, marks_ref, out_ref):
     marks = marks_ref.shape[0]
     no_tags = jnp.zeros(tags_ref.shape, jnp.bfloat16)
+    slots, width = points_ref.shape[1:]
+    scores = lax.dot_general(
+        points_ref[...].reshape(2 * slots, width), marks_ref[...], NT, preferred_element_type=jnp.float32
+    )
+    both = jnp.exp(scores * (0.5 / math.sqrt(width))).astype(jnp.bfloat16)
     for core, tags in enumerate((tags_ref[...], no_tags)):
-        scores = lax.dot_general(
-            points_ref[core], marks_ref[...], NT, preferred_element_type=jnp.float32
-        )
-        rows = jnp.exp(scores * (0.5 / math.sqrt(points_ref.shape[2]))).astype(jnp.bfloat16)
+        rows = both[core * slots : (core + 1) * slots]
         if len(out_ref.shape) == 2:
             for group in range(groups):
                 here = slice(group * capacity, (group + 1) * capacity)

time: 33.7 us -> 33.7 us (level)
  no operation moved by 1% of the time
where the time goes in v9:
time: 33.7 us; the launch traced here: 33.5 us
  starting transfers between devices  13.9 us (41%)
  waiting for transfers between devices  11.8 us (35%)
  Pallas kernels  5.14 us (15%)
  between operations  1.42 us (4%)
  local copies, waits for them, and re-layouts  1.09 us (3%)
    ppermute x10, starting transfers between devices, swap(): lax.ppermute(block, axis, [(i, i ^ mask) for i in range(lax.axis_size(axi...  10.4 us
    all_to_all x1, waiting for transfers between devices, exchange(): lax.all_to_all(rows.reshape(groups, 2 * capacity, lanes), 'pts', split_ax...  7.77 us
    pallas_call x7, Pallas kernels, call(): pl.pallas_call(kernel, out_shape=shapes, in_specs=[pl.BlockSpec(memory_sp...  5.14 us
    ppermute x10, waiting for transfers between devices, swap(): lax.ppermute(block, axis, [(i, i ^ mask) for i in range(lax.axis_size(axi...  3.99 us
    all_to_all x1, starting transfers between devices, exchange(): lax.all_to_all(rows.reshape(groups, 2 * capacity, lanes), 'pts', split_ax...  3.49 us
    dynamic_slice x1, local copies, waits for them, and re-layouts, sides_of(): lax.dynamic_index_in_dim(sides, side, 1, keepdims=False)  1.05 us
  transfers between devices with their start and end apart: 11, of which 5 were waited for; matrix products, arithmetic and copies ran while one was open for 4% of the time, Pallas kernels for 10%

profile of v9, /device:TPU:0, one launch (start us, length us, event | category | flops | bytes accessed | tf_op | source)
XLA Modules:
  0.0 33.5 jit_solution(6909322613825944736)
XLA Ops:
  0.6 0.0 copy-start
  0.7 0.0 copy-start.2
  0.7 0.5 %collective-permute-start = (bf16[256,768]{1,0:T(8,128)(2,1)}, bf16[256,768]{1,0:T(8,128)(2,1)S(1)}, u32[]{:S(2)}, u32[]{:S(2)}) collective-permute-start(bf16[256,768]{1,0:T(8,128)(2,1)} %refs_1_.1), channel_id=1, source_target_pairs={{0,4},{4,0},{8,12},{12,8},{16,20},{20,16},{24,28},{28,24},{1,5},{5... | collective-permute-start | bytes 1179656 | tf_op jit(solution)/shard_map/ppermute | solution.py:157
  1.2 1.0 %constant_dynamic-slice_fusion = (bf16[4,1,48,512]{3,2,1,0:T(8,128)(2,1)S(1)}, bf16[4,1,48,512]{3,2,1,0:T(8,128)(2,1)S(1)}) fusion(bf16[4,2,48,512]{3,2,1,0:T(8,128)(2,1)} %bitcast.21, s32[]{:T(128)S(6)} %select_n.36, s32[]{:T(128)S(6)} %select_n.35), kind=kLoop, calls=%fused_computation.3 | loop fusion | bytes 786440 | tf_op jit(solution)/shard_map/jit(dynamic_index_in_dim)/dynamic_slice | solution.py:167
  2.2 0.2 collective-permute-start.2
  2.4 0.4 %collective-permute-start.1 = (s32[1,256]{1,0:T(1,128)}, s32[1,256]{1,0:T(1,128)S(1)}, u32[]{:S(2)}, u32[]{:S(2)}) collective-permute-start(s32[1,256]{1,0:T(1,128)} %bitcast.19), channel_id=1, source_target_pairs={{0,4},{4,0},{8,12},{12,8},{16,20},{20,16},{24,28},{28,24},{1,5},{5... | collective-permute-start | bytes 3080 | tf_op jit(solution)/shard_map/ppermute | solution.py:157
  2.8 3.8 %collective-permute-start.4 = (bf16[48,768]{1,0:T(8,128)(2,1)S(1)}, bf16[48,768]{1,0:T(8,128)(2,1)S(1)}, u32[]{:S(2)}, u32[]{:S(2)}) collective-permute-start(bf16[48,768]{1,0:T(8,128)(2,1)S(1)} %constant_dynamic-slice_fusion.2.block_ref.refs_0_), channel_id=1, source_target_pairs={{0,2},{1,3},{2,0},{3,1},{4,6},{5,7},{6,4},{7,5},{8,10},{9,11},{10,... | collective-permute-start | bytes 221192 | tf_op jit(solution)/shard_map/ppermute | solution.py:157
  6.6 1.3 %collective-permute-start.5 = (bf16[48,768]{1,0:T(8,128)(2,1)S(1)}, bf16[48,768]{1,0:T(8,128)(2,1)S(1)}, u32[]{:S(2)}, u32[]{:S(2)}) collective-permute-start(bf16[48,768]{1,0:T(8,128)(2,1)S(1)} %constant_dynamic-slice_fusion.2.block_ref.refs_0_), channel_id=1, source_target_pairs={{0,3},{1,2},{2,1},{3,0},{4,7},{5,6},{6,5},{7,4},{8,11},{9,10},{10,... | collective-permute-start | bytes 221192 | tf_op jit(solution)/shard_map/ppermute | solution.py:157
  8.7 1.6 %collective-permute-start.6 = (bf16[192,512]{1,0:T(8,128)(2,1)S(1)}, bf16[192,512]{1,0:T(8,128)(2,1)S(1)}, u32[]{:S(2)}, u32[]{:S(2)}) collective-permute-start(bf16[192,512]{1,0:T(8,128)(2,1)S(1)} %shard_map.69.after_ref), channel_id=1, source_target_pairs={{0,8},{4,12},{8,0},{12,4},{16,24},{20,28},{24,16},{28,20},{1,9},{5... | collective-permute-start | bytes 589832 | tf_op jit(solution)/shard_map/ppermute | solution.py:157
  10.2 0.2 collective-permute-start.3
  10.5 0.1 pad_add_fusion.refs_0_
  10.5 1.7 %shard_map.68 = (bf16[2,512,768]{2,1,0:T(8,128)(2,1)S(1)}, bf16[512,64]{1,0:T(8,128)(2,1)S(1)}) custom-call(s32[2]{0:T(128)S(1)} %pad_add_fusion.refs_0_, bf16[256,768]{1,0:T(8,128)(2,1)S(1)} %copy-done.1, s32[1,256]{1,0:T(1,128)S(1)} %bitcast.20, bf16[256,768]{1,0:T(8,128)(2,1)S(1)} %collective-permute-done.refs_3_.refs_0_, ...), custom_call_target="tpu_custom_call" | custom-call | tf_op jit(solution)/shard_map/pallas_call | solution.py:142
  12.2 0.7 %collective-permute-done.4.refs_2_ = bf16[48,768]{1,0:T(8,128)(2,1)S(1)} collective-permute-done((bf16[48,768]{1,0:T(8,128)(2,1)S(1)}, bf16[48,768]{1,0:T(8,128)(2,1)S(1)}, u32[]{:S(2)}, u32[]{:S(2)}) %collective-permute-start.4) | collective-permute-done | bytes 73760 | tf_op jit(solution)/shard_map/ppermute | solution.py:157
  12.9 1.7 %collective-permute-done.3.refs_1_ = bf16[48,768]{1,0:T(8,128)(2,1)S(1)} collective-permute-done((bf16[48,768]{1,0:T(8,128)(2,1)S(1)}, bf16[48,768]{1,0:T(8,128)(2,1)S(1)}, u32[]{:S(2)}, u32[]{:S(2)}) %collective-permute-start.3) | collective-permute-done | bytes 73760 | tf_op jit(solution)/shard_map/ppermute | solution.py:157
  14.6 0.1 shard_map.71
  14.8 0.7 %collective-permute-done.6 = bf16[192,512]{1,0:T(8,128)(2,1)S(1)} collective-permute-done((bf16[192,512]{1,0:T(8,128)(2,1)S(1)}, bf16[192,512]{1,0:T(8,128)(2,1)S(1)}, u32[]{:S(2)}, u32[]{:S(2)}) %collective-permute-start.6) | collective-permute-done | bytes 196640 | tf_op jit(solution)/shard_map/ppermute | solution.py:157
  15.5 1.6 %collective-permute-start.7 = (bf16[192,512]{1,0:T(8,128)(2,1)S(1)}, bf16[192,512]{1,0:T(8,128)(2,1)S(1)}, u32[]{:S(2)}, u32[]{:S(2)}) collective-permute-start(bf16[192,512]{1,0:T(8,128)(2,1)S(1)} %broadcast_select_fusion), channel_id=1, source_target_pairs={{0,16},{4,20},{8,24},{12,28},{16,0},{20,4},{24,8},{28,12},{1,17},{... | collective-permute-start | bytes 589832 | tf_op jit(solution)/shard_map/ppermute | solution.py:157
  17.0 1.4 %shard_map.72 = bf16[1024,256]{1,0:T(8,128)(2,1)} custom-call(bf16[2,512,768]{2,1,0:T(8,128)(2,1)S(1)} %get-tuple-element.8.refs_0_, bf16[512,64]{1,0:T(8,128)(2,1)S(1)} %get-tuple-element.9.after_ref.refs_1_, bf16[192,768]{1,0:T(8,128)(2,1)S(1)} %get-tuple-element.10.refs_2_), custom_call_target="tpu_custom_call" | custom-call | tf_op jit(solution)/shard_map/pallas_call | solution.py:142
  18.4 3.5 %all-to-all-start = ((bf16[8,128,256]{2,1,0:T(8,128)(2,1)}), bf16[8,128,256]{2,1,0:T(8,128)(2,1)S(1)}, u32[]{:S(2)}, u32[]{:S(2)}) async-start(bf16[8,128,256]{2,1,0:T(8,128)(2,1)} %bitcast.9), calls=%async_computation | async-start | bytes 1048576 | tf_op jit(solution)/shard_map/all_to_all | solution.py:177
  22.0 0.5 %collective-permute-start.8 = (bf16[96,512]{1,0:T(8,128)(2,1)S(1)}, bf16[96,512]{1,0:T(8,128)(2,1)S(1)}, u32[]{:S(2)}, u32[]{:S(2)}) collective-permute-start(bf16[96,512]{1,0:T(8,128)(2,1)S(1)} %get-tuple-element.17), channel_id=1, source_target_pairs={{0,4},{4,0},{8,12},{12,8},{16,20},{20,16},{24,28},{28,24},{1,5},{5... | collective-permute-start | bytes 294920 | tf_op jit(solution)/shard_map/ppermute | solution.py:157
  22.5 0.9 %collective-permute-done.8.after_ref.refs_3_ = bf16[96,512]{1,0:T(8,128)(2,1)S(1)} collective-permute-done((bf16[96,512]{1,0:T(8,128)(2,1)S(1)}, bf16[96,512]{1,0:T(8,128)(2,1)S(1)}, u32[]{:S(2)}, u32[]{:S(2)}) %collective-permute-start.8) | collective-permute-done | bytes 98336 | tf_op jit(solution)/shard_map/ppermute | solution.py:157
  23.4 0.4 %collective-permute-start.9 = (bf16[96,512]{1,0:T(8,128)(2,1)S(1)}, bf16[96,512]{1,0:T(8,128)(2,1)S(1)}, u32[]{:S(2)}, u32[]{:S(2)}) collective-permute-start(bf16[96,512]{1,0:T(8,128)(2,1)S(1)} %shard_map.73), channel_id=1, source_target_pairs={{0,4},{4,0},{8,12},{12,8},{16,20},{20,16},{24,28},{28,24},{1,5},{5... | collective-permute-start | bytes 294920 | tf_op jit(solution)/shard_map/ppermute | solution.py:157
  23.8 7.8 %all-to-all-done = bf16[8,128,256]{2,1,0:T(8,128)(2,1)S(1)} async-done(((bf16[8,128,256]{2,1,0:T(8,128)(2,1)}), bf16[8,128,256]{2,1,0:T(8,128)(2,1)S(1)}, u32[]{:S(2)}, u32[]{:S(2)}) %all-to-all-start) | async-done | bytes 524320 | tf_op jit(solution)/shard_map/all_to_all | solution.py:177
  31.6 1.9 %shard_map.74 = (f32[512,512]{1,0:T(8,128)}, s32[1,512]{1,0:T(1,128)}) custom-call(s32[1]{0:T(128)} %bitcast.refs_0_, bf16[4,2,128,256]{3,2,1,0:T(8,128)(2,1)S(1)} %bitcast.17, bf16[192,512]{1,0:T(8,128)(2,1)S(1)} %broadcast_select_fusion.1.refs_2_, bf16[96,512]{1,0:T(8,128)(2,1)S(1)} %collective-permute-done.8.after_ref.refs_3_, ...), custom_call_target="tpu_custom_call" | custom-call | tf_op jit(solution)/shard_map/pallas_call | solution.py:142
  (18 shorter events, 0.2 us)
Async XLA Ops:
  0.6 2.2 %copy-start = (bf16[96,768]{1,0:T(8,128)(2,1)S(1)}, bf16[96,768]{1,0:T(8,128)(2,1)}, u32[]{:S(2)}) copy-start(bf16[96,768]{1,0:T(8,128)(2,1)} %param.6) | copy-start | bytes 442372
  0.6 9.9 %copy-start.1 = (bf16[256,768]{1,0:T(8,128)(2,1)S(1)}, bf16[256,768]{1,0:T(8,128)(2,1)}, u32[]{:S(2)}) copy-start(bf16[256,768]{1,0:T(8,128)(2,1)} %refs_1_.1) | copy-start | bytes 1179652
  0.7 9.9 %copy-start.2 = (s32[256]{0:T(256)S(1)}, s32[256]{0:T(256)}, u32[]{:S(2)}) copy-start(s32[256]{0:T(256)} %param.9) | copy-start | bytes 3076
  0.7 7.9 %collective-permute-start = (bf16[256,768]{1,0:T(8,128)(2,1)}, bf16[256,768]{1,0:T(8,128)(2,1)S(1)}, u32[]{:S(2)}, u32[]{:S(2)}) collective-permute-start(bf16[256,768]{1,0:T(8,128)(2,1)} %refs_1_.1), channel_id=1, source_target_pairs={{0,4},{4,0},{8,12},{12,8},{16,20},{20,16},{24,28},{28,24},{1,5},{5... | collective-permute-start | bytes 1179656 | tf_op jit(solution)/shard_map/ppermute | solution.py:157
  2.2 6.4 %collective-permute-start.2 = (bf16[192,512]{1,0:T(8,128)(2,1)S(1)}, bf16[192,512]{1,0:T(8,128)(2,1)S(1)}, u32[]{:S(2)}, u32[]{:S(2)}) collective-permute-start(bf16[192,512]{1,0:T(8,128)(2,1)S(1)} %bitcast.22), channel_id=1, source_target_pairs={{0,4},{4,0},{8,12},{12,8},{16,20},{20,16},{24,28},{28,24},{1,5},{5... | collective-permute-start | bytes 589832 | tf_op jit(solution)/shard_map/ppermute | solution.py:157
  2.4 6.2 %collective-permute-start.1 = (s32[1,256]{1,0:T(1,128)}, s32[1,256]{1,0:T(1,128)S(1)}, u32[]{:S(2)}, u32[]{:S(2)}) collective-permute-start(s32[1,256]{1,0:T(1,128)} %bitcast.19), channel_id=1, source_target_pairs={{0,4},{4,0},{8,12},{12,8},{16,20},{20,16},{24,28},{28,24},{1,5},{5... | collective-permute-start | bytes 3080 | tf_op jit(solution)/shard_map/ppermute | solution.py:157
  2.8 10.1 %collective-permute-start.4 = (bf16[48,768]{1,0:T(8,128)(2,1)S(1)}, bf16[48,768]{1,0:T(8,128)(2,1)S(1)}, u32[]{:S(2)}, u32[]{:S(2)}) collective-permute-start(bf16[48,768]{1,0:T(8,128)(2,1)S(1)} %constant_dynamic-slice_fusion.2.block_ref.refs_0_), channel_id=1, source_target_pairs={{0,2},{1,3},{2,0},{3,1},{4,6},{5,7},{6,4},{7,5},{8,10},{9,11},{10,... | collective-permute-start | bytes 221192 | tf_op jit(solution)/shard_map/ppermute | solution.py:157
  6.6 6.3 %collective-permute-start.5 = (bf16[48,768]{1,0:T(8,128)(2,1)S(1)}, bf16[48,768]{1,0:T(8,128)(2,1)S(1)}, u32[]{:S(2)}, u32[]{:S(2)}) collective-permute-start(bf16[48,768]{1,0:T(8,128)(2,1)S(1)} %constant_dynamic-slice_fusion.2.block_ref.refs_0_), channel_id=1, source_target_pairs={{0,3},{1,2},{2,1},{3,0},{4,7},{5,6},{6,5},{7,4},{8,11},{9,10},{10,... | collective-permute-start | bytes 221192 | tf_op jit(solution)/shard_map/ppermute | solution.py:157
  8.7 6.7 %collective-permute-start.6 = (bf16[192,512]{1,0:T(8,128)(2,1)S(1)}, bf16[192,512]{1,0:T(8,128)(2,1)S(1)}, u32[]{:S(2)}, u32[]{:S(2)}) collective-permute-start(bf16[192,512]{1,0:T(8,128)(2,1)S(1)} %shard_map.69.after_ref), channel_id=1, source_target_pairs={{0,8},{4,12},{8,0},{12,4},{16,24},{20,28},{24,16},{28,20},{1,9},{5... | collective-permute-start | bytes 589832 | tf_op jit(solution)/shard_map/ppermute | solution.py:157
  10.2 4.4 %collective-permute-start.3 = (bf16[48,768]{1,0:T(8,128)(2,1)S(1)}, bf16[48,768]{1,0:T(8,128)(2,1)S(1)}, u32[]{:S(2)}, u32[]{:S(2)}) collective-permute-start(bf16[48,768]{1,0:T(8,128)(2,1)S(1)} %shard_map.70), channel_id=1, source_target_pairs={{0,1},{1,0},{2,3},{3,2},{4,5},{5,4},{6,7},{7,6},{8,9},{9,8},{10,11... | collective-permute-start | bytes 221192 | tf_op jit(solution)/shard_map/ppermute | solution.py:157
  15.5 6.5 %collective-permute-start.7 = (bf16[192,512]{1,0:T(8,128)(2,1)S(1)}, bf16[192,512]{1,0:T(8,128)(2,1)S(1)}, u32[]{:S(2)}, u32[]{:S(2)}) collective-permute-start(bf16[192,512]{1,0:T(8,128)(2,1)S(1)} %broadcast_select_fusion), channel_id=1, source_target_pairs={{0,16},{4,20},{8,24},{12,28},{16,0},{20,4},{24,8},{28,12},{1,17},{... | collective-permute-start | bytes 589832 | tf_op jit(solution)/shard_map/ppermute | solution.py:157
  18.4 13.2 %all-to-all-start = ((bf16[8,128,256]{2,1,0:T(8,128)(2,1)}), bf16[8,128,256]{2,1,0:T(8,128)(2,1)S(1)}, u32[]{:S(2)}, u32[]{:S(2)}) async-start(bf16[8,128,256]{2,1,0:T(8,128)(2,1)} %bitcast.9), calls=%async_computation | async-start | bytes 1048576 | tf_op jit(solution)/shard_map/all_to_all | solution.py:177
  22.0 1.4 %collective-permute-start.8 = (bf16[96,512]{1,0:T(8,128)(2,1)S(1)}, bf16[96,512]{1,0:T(8,128)(2,1)S(1)}, u32[]{:S(2)}, u32[]{:S(2)}) collective-permute-start(bf16[96,512]{1,0:T(8,128)(2,1)S(1)} %get-tuple-element.17), channel_id=1, source_target_pairs={{0,4},{4,0},{8,12},{12,8},{16,20},{20,16},{24,28},{28,24},{1,5},{5... | collective-permute-start | bytes 294920 | tf_op jit(solution)/shard_map/ppermute | solution.py:157
  23.4 8.2 %collective-permute-start.9 = (bf16[96,512]{1,0:T(8,128)(2,1)S(1)}, bf16[96,512]{1,0:T(8,128)(2,1)S(1)}, u32[]{:S(2)}, u32[]{:S(2)}) collective-permute-start(bf16[96,512]{1,0:T(8,128)(2,1)S(1)} %shard_map.73), channel_id=1, source_target_pairs={{0,4},{4,0},{8,12},{12,8},{16,20},{20,16},{24,28},{28,24},{1,5},{5... | collective-permute-start | bytes 294920 | tf_op jit(solution)/shard_map/ppermute | solution.py:157

commit v10 on v8

--- a/solution.py
+++ b/solution.py
@@ -203,7 +203,7 @@
     halves = [marks] + [
         swap(near if mask == 1 else marks, "lmk", mask) for mask in range(1, parts)
     ]
-    masks = [1 << bit for bit in range(1, groups.bit_length() - 1)]
+    masks = [1 << bit for bit in range(groups.bit_length() - 2, 0, -1)]
     panel_met = swap(panel, "pts", masks[0])
     placed, tags = call(
         lambda *refs: place_kernel(groups, capacity, *refs),

time: 33.7 us -> 33.7 us (level)
  no operation moved by 1% of the time
where the time goes in v10:
time: 33.7 us; the launch traced here: 33.5 us
  starting transfers between devices  13.9 us (41%)
  waiting for transfers between devices  11.7 us (35%)
  Pallas kernels  5.16 us (15%)
  between operations  1.42 us (4%)
  local copies, waits for them, and re-layouts  1.09 us (3%)
    ppermute x10, starting transfers between devices, swap(): lax.ppermute(block, axis, [(i, i ^ mask) for i in range(lax.axis_size(axi...  10.4 us
    all_to_all x1, waiting for transfers between devices, exchange(): lax.all_to_all(rows.reshape(groups, 2 * capacity, lanes), 'pts', split_ax...  7.77 us
    pallas_call x7, Pallas kernels, call(): pl.pallas_call(kernel, out_shape=shapes, in_specs=[pl.BlockSpec(memory_sp...  5.16 us
    ppermute x10, waiting for transfers between devices, swap(): lax.ppermute(block, axis, [(i, i ^ mask) for i in range(lax.axis_size(axi...  3.96 us
    all_to_all x1, starting transfers between devices, exchange(): lax.all_to_all(rows.reshape(groups, 2 * capacity, lanes), 'pts', split_ax...  3.49 us
    dynamic_slice x1, local copies, waits for them, and re-layouts, sides_of(): lax.dynamic_index_in_dim(sides, side, 1, keepdims=False)  1.05 us
  transfers between devices with their start and end apart: 11, of which 5 were waited for; matrix products, arithmetic and copies ran while one was open for 4% of the time, Pallas kernels for 10%

profile of v10, /device:TPU:0, one launch (start us, length us, event | category | flops | bytes accessed | tf_op | source)
XLA Modules:
  0.0 33.5 jit_solution(14176621929290110776)
XLA Ops:
  0.6 0.0 copy-start
  0.7 0.0 copy-start.2
  0.7 0.5 %collective-permute-start = (bf16[256,768]{1,0:T(8,128)(2,1)}, bf16[256,768]{1,0:T(8,128)(2,1)S(1)}, u32[]{:S(2)}, u32[]{:S(2)}) collective-permute-start(bf16[256,768]{1,0:T(8,128)(2,1)} %refs_1_.1), channel_id=1, source_target_pairs={{0,4},{4,0},{8,12},{12,8},{16,20},{20,16},{24,28},{28,24},{1,5},{5... | collective-permute-start | bytes 1179656 | tf_op jit(solution)/shard_map/ppermute | solution.py:155
  1.2 1.0 %constant_dynamic-slice_fusion = (bf16[4,1,48,512]{3,2,1,0:T(8,128)(2,1)S(1)}, bf16[4,1,48,512]{3,2,1,0:T(8,128)(2,1)S(1)}) fusion(bf16[4,2,48,512]{3,2,1,0:T(8,128)(2,1)} %bitcast.21, s32[]{:T(128)S(6)} %select_n.36, s32[]{:T(128)S(6)} %select_n.35), kind=kLoop, calls=%fused_computation.3 | loop fusion | bytes 786440 | tf_op jit(solution)/shard_map/jit(dynamic_index_in_dim)/dynamic_slice | solution.py:165
  2.2 0.2 collective-permute-start.2
  2.4 0.4 %collective-permute-start.1 = (s32[1,256]{1,0:T(1,128)}, s32[1,256]{1,0:T(1,128)S(1)}, u32[]{:S(2)}, u32[]{:S(2)}) collective-permute-start(s32[1,256]{1,0:T(1,128)} %bitcast.19), channel_id=1, source_target_pairs={{0,4},{4,0},{8,12},{12,8},{16,20},{20,16},{24,28},{28,24},{1,5},{5... | collective-permute-start | bytes 3080 | tf_op jit(solution)/shard_map/ppermute | solution.py:155
  2.8 3.8 %collective-permute-start.4 = (bf16[48,768]{1,0:T(8,128)(2,1)S(1)}, bf16[48,768]{1,0:T(8,128)(2,1)S(1)}, u32[]{:S(2)}, u32[]{:S(2)}) collective-permute-start(bf16[48,768]{1,0:T(8,128)(2,1)S(1)} %constant_dynamic-slice_fusion.2.block_ref.refs_0_), channel_id=1, source_target_pairs={{0,2},{1,3},{2,0},{3,1},{4,6},{5,7},{6,4},{7,5},{8,10},{9,11},{10,... | collective-permute-start | bytes 221192 | tf_op jit(solution)/shard_map/ppermute | solution.py:155
  6.6 1.3 %collective-permute-start.5 = (bf16[48,768]{1,0:T(8,128)(2,1)S(1)}, bf16[48,768]{1,0:T(8,128)(2,1)S(1)}, u32[]{:S(2)}, u32[]{:S(2)}) collective-permute-start(bf16[48,768]{1,0:T(8,128)(2,1)S(1)} %constant_dynamic-slice_fusion.2.block_ref.refs_0_), channel_id=1, source_target_pairs={{0,3},{1,2},{2,1},{3,0},{4,7},{5,6},{6,5},{7,4},{8,11},{9,10},{10,... | collective-permute-start | bytes 221192 | tf_op jit(solution)/shard_map/ppermute | solution.py:155
  8.7 1.6 %collective-permute-start.6 = (bf16[192,512]{1,0:T(8,128)(2,1)S(1)}, bf16[192,512]{1,0:T(8,128)(2,1)S(1)}, u32[]{:S(2)}, u32[]{:S(2)}) collective-permute-start(bf16[192,512]{1,0:T(8,128)(2,1)S(1)} %shard_map.69.after_ref), channel_id=1, source_target_pairs={{0,16},{4,20},{8,24},{12,28},{16,0},{20,4},{24,8},{28,12},{1,17},{... | collective-permute-start | bytes 589832 | tf_op jit(solution)/shard_map/ppermute | solution.py:155
  10.3 0.2 collective-permute-start.3
  10.5 0.1 pad_add_fusion.refs_0_
  10.6 1.7 %shard_map.68 = (bf16[2,512,768]{2,1,0:T(8,128)(2,1)S(1)}, bf16[512,64]{1,0:T(8,128)(2,1)S(1)}) custom-call(s32[2]{0:T(128)S(1)} %pad_add_fusion.refs_0_, bf16[256,768]{1,0:T(8,128)(2,1)S(1)} %copy-done.1, s32[1,256]{1,0:T(1,128)S(1)} %bitcast.20, bf16[256,768]{1,0:T(8,128)(2,1)S(1)} %collective-permute-done.refs_3_.refs_0_, ...), custom_call_target="tpu_custom_call" | custom-call | tf_op jit(solution)/shard_map/pallas_call | solution.py:140
  12.2 0.6 %collective-permute-done.4.refs_2_ = bf16[48,768]{1,0:T(8,128)(2,1)S(1)} collective-permute-done((bf16[48,768]{1,0:T(8,128)(2,1)S(1)}, bf16[48,768]{1,0:T(8,128)(2,1)S(1)}, u32[]{:S(2)}, u32[]{:S(2)}) %collective-permute-start.4) | collective-permute-done | bytes 73760 | tf_op jit(solution)/shard_map/ppermute | solution.py:155
  12.9 1.7 %collective-permute-done.3.refs_1_ = bf16[48,768]{1,0:T(8,128)(2,1)S(1)} collective-permute-done((bf16[48,768]{1,0:T(8,128)(2,1)S(1)}, bf16[48,768]{1,0:T(8,128)(2,1)S(1)}, u32[]{:S(2)}, u32[]{:S(2)}) %collective-permute-start.3) | collective-permute-done | bytes 73760 | tf_op jit(solution)/shard_map/ppermute | solution.py:155
  14.6 0.1 shard_map.71
  14.8 0.6 %collective-permute-done.6 = bf16[192,512]{1,0:T(8,128)(2,1)S(1)} collective-permute-done((bf16[192,512]{1,0:T(8,128)(2,1)S(1)}, bf16[192,512]{1,0:T(8,128)(2,1)S(1)}, u32[]{:S(2)}, u32[]{:S(2)}) %collective-permute-start.6) | collective-permute-done | bytes 196640 | tf_op jit(solution)/shard_map/ppermute | solution.py:155
  15.5 1.6 %collective-permute-start.7 = (bf16[192,512]{1,0:T(8,128)(2,1)S(1)}, bf16[192,512]{1,0:T(8,128)(2,1)S(1)}, u32[]{:S(2)}, u32[]{:S(2)}) collective-permute-start(bf16[192,512]{1,0:T(8,128)(2,1)S(1)} %broadcast_select_fusion), channel_id=1, source_target_pairs={{0,8},{4,12},{8,0},{12,4},{16,24},{20,28},{24,16},{28,20},{1,9},{5... | collective-permute-start | bytes 589832 | tf_op jit(solution)/shard_map/ppermute | solution.py:155
  17.0 1.4 %shard_map.72 = bf16[1024,256]{1,0:T(8,128)(2,1)} custom-call(bf16[2,512,768]{2,1,0:T(8,128)(2,1)S(1)} %get-tuple-element.8.refs_0_, bf16[512,64]{1,0:T(8,128)(2,1)S(1)} %get-tuple-element.9.after_ref.refs_1_, bf16[192,768]{1,0:T(8,128)(2,1)S(1)} %get-tuple-element.10.refs_2_), custom_call_target="tpu_custom_call" | custom-call | tf_op jit(solution)/shard_map/pallas_call | solution.py:140
  18.4 3.5 %all-to-all-start = ((bf16[8,128,256]{2,1,0:T(8,128)(2,1)}), bf16[8,128,256]{2,1,0:T(8,128)(2,1)S(1)}, u32[]{:S(2)}, u32[]{:S(2)}) async-start(bf16[8,128,256]{2,1,0:T(8,128)(2,1)} %bitcast.9), calls=%async_computation | async-start | bytes 1048576 | tf_op jit(solution)/shard_map/all_to_all | solution.py:175
  22.0 0.5 %collective-permute-start.8 = (bf16[96,512]{1,0:T(8,128)(2,1)S(1)}, bf16[96,512]{1,0:T(8,128)(2,1)S(1)}, u32[]{:S(2)}, u32[]{:S(2)}) collective-permute-start(bf16[96,512]{1,0:T(8,128)(2,1)S(1)} %get-tuple-element.17), channel_id=1, source_target_pairs={{0,4},{4,0},{8,12},{12,8},{16,20},{20,16},{24,28},{28,24},{1,5},{5... | collective-permute-start | bytes 294920 | tf_op jit(solution)/shard_map/ppermute | solution.py:155
  22.4 0.9 %collective-permute-done.8.after_ref.refs_3_ = bf16[96,512]{1,0:T(8,128)(2,1)S(1)} collective-permute-done((bf16[96,512]{1,0:T(8,128)(2,1)S(1)}, bf16[96,512]{1,0:T(8,128)(2,1)S(1)}, u32[]{:S(2)}, u32[]{:S(2)}) %collective-permute-start.8) | collective-permute-done | bytes 98336 | tf_op jit(solution)/shard_map/ppermute | solution.py:155
  23.4 0.4 %collective-permute-start.9 = (bf16[96,512]{1,0:T(8,128)(2,1)S(1)}, bf16[96,512]{1,0:T(8,128)(2,1)S(1)}, u32[]{:S(2)}, u32[]{:S(2)}) collective-permute-start(bf16[96,512]{1,0:T(8,128)(2,1)S(1)} %shard_map.73), channel_id=1, source_target_pairs={{0,4},{4,0},{8,12},{12,8},{16,20},{20,16},{24,28},{28,24},{1,5},{5... | collective-permute-start | bytes 294920 | tf_op jit(solution)/shard_map/ppermute | solution.py:155
  23.8 7.8 %all-to-all-done = bf16[8,128,256]{2,1,0:T(8,128)(2,1)S(1)} async-done(((bf16[8,128,256]{2,1,0:T(8,128)(2,1)}), bf16[8,128,256]{2,1,0:T(8,128)(2,1)S(1)}, u32[]{:S(2)}, u32[]{:S(2)}) %all-to-all-start) | async-done | bytes 524320 | tf_op jit(solution)/shard_map/all_to_all | solution.py:175
  31.6 1.9 %shard_map.74 = (f32[512,512]{1,0:T(8,128)}, s32[1,512]{1,0:T(1,128)}) custom-call(s32[1]{0:T(128)} %bitcast.refs_0_, bf16[4,2,128,256]{3,2,1,0:T(8,128)(2,1)S(1)} %bitcast.17, bf16[192,512]{1,0:T(8,128)(2,1)S(1)} %broadcast_select_fusion.1.refs_2_, bf16[96,512]{1,0:T(8,128)(2,1)S(1)} %collective-permute-done.8.after_ref.refs_3_, ...), custom_call_target="tpu_custom_call" | custom-call | tf_op jit(solution)/shard_map/pallas_call | solution.py:140
  (18 shorter events, 0.2 us)
Async XLA Ops:
  0.6 2.2 %copy-start = (bf16[96,768]{1,0:T(8,128)(2,1)S(1)}, bf16[96,768]{1,0:T(8,128)(2,1)}, u32[]{:S(2)}) copy-start(bf16[96,768]{1,0:T(8,128)(2,1)} %param.6) | copy-start | bytes 442372
  0.6 9.9 %copy-start.1 = (bf16[256,768]{1,0:T(8,128)(2,1)S(1)}, bf16[256,768]{1,0:T(8,128)(2,1)}, u32[]{:S(2)}) copy-start(bf16[256,768]{1,0:T(8,128)(2,1)} %refs_1_.1) | copy-start | bytes 1179652
  0.7 9.9 %copy-start.2 = (s32[256]{0:T(256)S(1)}, s32[256]{0:T(256)}, u32[]{:S(2)}) copy-start(s32[256]{0:T(256)} %param.9) | copy-start | bytes 3076
  0.7 7.9 %collective-permute-start = (bf16[256,768]{1,0:T(8,128)(2,1)}, bf16[256,768]{1,0:T(8,128)(2,1)S(1)}, u32[]{:S(2)}, u32[]{:S(2)}) collective-permute-start(bf16[256,768]{1,0:T(8,128)(2,1)} %refs_1_.1), channel_id=1, source_target_pairs={{0,4},{4,0},{8,12},{12,8},{16,20},{20,16},{24,28},{28,24},{1,5},{5... | collective-permute-start | bytes 1179656 | tf_op jit(solution)/shard_map/ppermute | solution.py:155
  2.2 6.4 %collective-permute-start.2 = (bf16[192,512]{1,0:T(8,128)(2,1)S(1)}, bf16[192,512]{1,0:T(8,128)(2,1)S(1)}, u32[]{:S(2)}, u32[]{:S(2)}) collective-permute-start(bf16[192,512]{1,0:T(8,128)(2,1)S(1)} %bitcast.22), channel_id=1, source_target_pairs={{0,4},{4,0},{8,12},{12,8},{16,20},{20,16},{24,28},{28,24},{1,5},{5... | collective-permute-start | bytes 589832 | tf_op jit(solution)/shard_map/ppermute | solution.py:155
  2.4 6.2 %collective-permute-start.1 = (s32[1,256]{1,0:T(1,128)}, s32[1,256]{1,0:T(1,128)S(1)}, u32[]{:S(2)}, u32[]{:S(2)}) collective-permute-start(s32[1,256]{1,0:T(1,128)} %bitcast.19), channel_id=1, source_target_pairs={{0,4},{4,0},{8,12},{12,8},{16,20},{20,16},{24,28},{28,24},{1,5},{5... | collective-permute-start | bytes 3080 | tf_op jit(solution)/shard_map/ppermute | solution.py:155
  2.8 10.0 %collective-permute-start.4 = (bf16[48,768]{1,0:T(8,128)(2,1)S(1)}, bf16[48,768]{1,0:T(8,128)(2,1)S(1)}, u32[]{:S(2)}, u32[]{:S(2)}) collective-permute-start(bf16[48,768]{1,0:T(8,128)(2,1)S(1)} %constant_dynamic-slice_fusion.2.block_ref.refs_0_), channel_id=1, source_target_pairs={{0,2},{1,3},{2,0},{3,1},{4,6},{5,7},{6,4},{7,5},{8,10},{9,11},{10,... | collective-permute-start | bytes 221192 | tf_op jit(solution)/shard_map/ppermute | solution.py:155
  6.6 6.3 %collective-permute-start.5 = (bf16[48,768]{1,0:T(8,128)(2,1)S(1)}, bf16[48,768]{1,0:T(8,128)(2,1)S(1)}, u32[]{:S(2)}, u32[]{:S(2)}) collective-permute-start(bf16[48,768]{1,0:T(8,128)(2,1)S(1)} %constant_dynamic-slice_fusion.2.block_ref.refs_0_), channel_id=1, source_target_pairs={{0,3},{1,2},{2,1},{3,0},{4,7},{5,6},{6,5},{7,4},{8,11},{9,10},{10,... | collective-permute-start | bytes 221192 | tf_op jit(solution)/shard_map/ppermute | solution.py:155
  8.7 6.7 %collective-permute-start.6 = (bf16[192,512]{1,0:T(8,128)(2,1)S(1)}, bf16[192,512]{1,0:T(8,128)(2,1)S(1)}, u32[]{:S(2)}, u32[]{:S(2)}) collective-permute-start(bf16[192,512]{1,0:T(8,128)(2,1)S(1)} %shard_map.69.after_ref), channel_id=1, source_target_pairs={{0,16},{4,20},{8,24},{12,28},{16,0},{20,4},{24,8},{28,12},{1,17},{... | collective-permute-start | bytes 589832 | tf_op jit(solution)/shard_map/ppermute | solution.py:155
  10.3 4.4 %collective-permute-start.3 = (bf16[48,768]{1,0:T(8,128)(2,1)S(1)}, bf16[48,768]{1,0:T(8,128)(2,1)S(1)}, u32[]{:S(2)}, u32[]{:S(2)}) collective-permute-start(bf16[48,768]{1,0:T(8,128)(2,1)S(1)} %shard_map.70), channel_id=1, source_target_pairs={{0,1},{1,0},{2,3},{3,2},{4,5},{5,4},{6,7},{7,6},{8,9},{9,8},{10,11... | collective-permute-start | bytes 221192 | tf_op jit(solution)/shard_map/ppermute | solution.py:155
  15.5 6.5 %collective-permute-start.7 = (bf16[192,512]{1,0:T(8,128)(2,1)S(1)}, bf16[192,512]{1,0:T(8,128)(2,1)S(1)}, u32[]{:S(2)}, u32[]{:S(2)}) collective-permute-start(bf16[192,512]{1,0:T(8,128)(2,1)S(1)} %broadcast_select_fusion), channel_id=1, source_target_pairs={{0,8},{4,12},{8,0},{12,4},{16,24},{20,28},{24,16},{28,20},{1,9},{5... | collective-permute-start | bytes 589832 | tf_op jit(solution)/shard_map/ppermute | solution.py:155
  18.4 13.2 %all-to-all-start = ((bf16[8,128,256]{2,1,0:T(8,128)(2,1)}), bf16[8,128,256]{2,1,0:T(8,128)(2,1)S(1)}, u32[]{:S(2)}, u32[]{:S(2)}) async-start(bf16[8,128,256]{2,1,0:T(8,128)(2,1)} %bitcast.9), calls=%async_computation | async-start | bytes 1048576 | tf_op jit(solution)/shard_map/all_to_all | solution.py:175
  22.0 1.4 %collective-permute-start.8 = (bf16[96,512]{1,0:T(8,128)(2,1)S(1)}, bf16[96,512]{1,0:T(8,128)(2,1)S(1)}, u32[]{:S(2)}, u32[]{:S(2)}) collective-permute-start(bf16[96,512]{1,0:T(8,128)(2,1)S(1)} %get-tuple-element.17), channel_id=1, source_target_pairs={{0,4},{4,0},{8,12},{12,8},{16,20},{20,16},{24,28},{28,24},{1,5},{5... | collective-permute-start | bytes 294920 | tf_op jit(solution)/shard_map/ppermute | solution.py:155
  23.4 8.2 %collective-permute-start.9 = (bf16[96,512]{1,0:T(8,128)(2,1)S(1)}, bf16[96,512]{1,0:T(8,128)(2,1)S(1)}, u32[]{:S(2)}, u32[]{:S(2)}) collective-permute-start(bf16[96,512]{1,0:T(8,128)(2,1)S(1)} %shard_map.73), channel_id=1, source_target_pairs={{0,4},{4,0},{8,12},{12,8},{16,20},{20,16},{24,28},{28,24},{1,5},{5... | collective-permute-start | bytes 294920 | tf_op jit(solution)/shard_map/ppermute | solution.py:155

commit v11 on v9

--- a/solution.py
+++ b/solution.py
@@ -200,7 +200,7 @@
     points_met, assignment_met = swap(points, "pts", 1), swap(assignment, "pts", 1)
     differs = panel_index[0] ^ me
     mine, other = sides_of(panels[0], parts, me % 2)
-    panel = pick((differs & 1) == 0, mine, swap(other, "pts", 1), points_met, assignment_met)
+    panel = pick((differs & 1) == 0, mine, swap(other, "pts", 1), assignment_met)
     near = call(pass_kernel, array(marks.shape), marks, panel)
     halves = [marks] + [
         swap(near if mask == 1 else marks, "lmk", mask) for mask in range(1, parts)

time: 33.7 us -> 33.7 us (level)
    all_to_all x1, waiting for transfers between devices: 7.77 us -> 6.83 us  [exchange(): lax.all_to_all(rows.reshape(groups, 2 * capacity, lanes), 'pts', split_ax...]
    ppermute x10, waiting for transfers between devices: 3.99 us -> 4.92 us  [swap(): lax.ppermute(block, axis, [(i, i ^ mask) for i in range(lax.axis_size(axi...]
  transfers between devices with their start and end apart: 11 -> 11, of which waited for: 5 -> 6; matrix products, arithmetic and copies ran while one was open for 4% -> 4% of each run, Pallas kernels for 10% -> 10%
where the time goes in v11:
time: 33.7 us; the launch traced here: 33.5 us
  starting transfers between devices  13.9 us (41%)
  waiting for transfers between devices  11.8 us (35%)
  Pallas kernels  5.14 us (15%)
  between operations  1.41 us (4%)
  local copies, waits for them, and re-layouts  1.09 us (3%)
    ppermute x10, starting transfers between devices, swap(): lax.ppermute(block, axis, [(i, i ^ mask) for i in range(lax.axis_size(axi...  10.4 us
    all_to_all x1, waiting for transfers between devices, exchange(): lax.all_to_all(rows.reshape(groups, 2 * capacity, lanes), 'pts', split_ax...  6.83 us
    pallas_call x7, Pallas kernels, call(): pl.pallas_call(kernel, out_shape=shapes, in_specs=[pl.BlockSpec(memory_sp...  5.14 us
    ppermute x10, waiting for transfers between devices, swap(): lax.ppermute(block, axis, [(i, i ^ mask) for i in range(lax.axis_size(axi...  4.92 us
    all_to_all x1, starting transfers between devices, exchange(): lax.all_to_all(rows.reshape(groups, 2 * capacity, lanes), 'pts', split_ax...  3.49 us
    dynamic_slice x1, local copies, waits for them, and re-layouts, sides_of(): lax.dynamic_index_in_dim(sides, side, 1, keepdims=False)  1.05 us
  transfers between devices with their start and end apart: 11, of which 6 were waited for; matrix products, arithmetic and copies ran while one was open for 4% of the time, Pallas kernels for 10%

profile of v11, /device:TPU:0, one launch (start us, length us, event | category | flops | bytes accessed | tf_op | source)
XLA Modules:
  0.0 33.5 jit_solution(12511491190058343108)
XLA Ops:
  0.6 0.0 copy-start
  0.7 0.5 %collective-permute-start = (bf16[256,768]{1,0:T(8,128)(2,1)}, bf16[256,768]{1,0:T(8,128)(2,1)S(1)}, u32[]{:S(2)}, u32[]{:S(2)}) collective-permute-start(bf16[256,768]{1,0:T(8,128)(2,1)} %refs_1_.1), channel_id=1, source_target_pairs={{0,4},{4,0},{8,12},{12,8},{16,20},{20,16},{24,28},{28,24},{1,5},{5... | collective-permute-start | bytes 1179656 | tf_op jit(solution)/shard_map/ppermute | solution.py:157
  1.2 1.0 %constant_dynamic-slice_fusion = (bf16[4,1,48,512]{3,2,1,0:T(8,128)(2,1)S(1)}, bf16[4,1,48,512]{3,2,1,0:T(8,128)(2,1)S(1)}) fusion(bf16[4,2,48,512]{3,2,1,0:T(8,128)(2,1)} %bitcast.21, s32[]{:T(128)S(6)} %select_n.36, s32[]{:T(128)S(6)} %select_n.35), kind=kLoop, calls=%fused_computation.3 | loop fusion | bytes 786440 | tf_op jit(solution)/shard_map/jit(dynamic_index_in_dim)/dynamic_slice | solution.py:167
  2.2 0.2 collective-permute-start.2
  2.4 0.4 %collective-permute-start.1 = (s32[1,256]{1,0:T(1,128)}, s32[1,256]{1,0:T(1,128)S(1)}, u32[]{:S(2)}, u32[]{:S(2)}) collective-permute-start(s32[1,256]{1,0:T(1,128)} %bitcast.19), channel_id=1, source_target_pairs={{0,4},{4,0},{8,12},{12,8},{16,20},{20,16},{24,28},{28,24},{1,5},{5... | collective-permute-start | bytes 3080 | tf_op jit(solution)/shard_map/ppermute | solution.py:157
  2.8 3.8 %collective-permute-start.4 = (bf16[48,768]{1,0:T(8,128)(2,1)S(1)}, bf16[48,768]{1,0:T(8,128)(2,1)S(1)}, u32[]{:S(2)}, u32[]{:S(2)}) collective-permute-start(bf16[48,768]{1,0:T(8,128)(2,1)S(1)} %constant_dynamic-slice_fusion.2.block_ref.refs_0_), channel_id=1, source_target_pairs={{0,2},{1,3},{2,0},{3,1},{4,6},{5,7},{6,4},{7,5},{8,10},{9,11},{10,... | collective-permute-start | bytes 221192 | tf_op jit(solution)/shard_map/ppermute | solution.py:157
  6.6 1.3 %collective-permute-start.5 = (bf16[48,768]{1,0:T(8,128)(2,1)S(1)}, bf16[48,768]{1,0:T(8,128)(2,1)S(1)}, u32[]{:S(2)}, u32[]{:S(2)}) collective-permute-start(bf16[48,768]{1,0:T(8,128)(2,1)S(1)} %constant_dynamic-slice_fusion.2.block_ref.refs_0_), channel_id=1, source_target_pairs={{0,3},{1,2},{2,1},{3,0},{4,7},{5,6},{6,5},{7,4},{8,11},{9,10},{10,... | collective-permute-start | bytes 221192 | tf_op jit(solution)/shard_map/ppermute | solution.py:157
  8.7 1.6 %collective-permute-start.6 = (bf16[192,512]{1,0:T(8,128)(2,1)S(1)}, bf16[192,512]{1,0:T(8,128)(2,1)S(1)}, u32[]{:S(2)}, u32[]{:S(2)}) collective-permute-start(bf16[192,512]{1,0:T(8,128)(2,1)S(1)} %shard_map.69.after_ref), channel_id=1, source_target_pairs={{0,8},{4,12},{8,0},{12,4},{16,24},{20,28},{24,16},{28,20},{1,9},{5... | collective-permute-start | bytes 589832 | tf_op jit(solution)/shard_map/ppermute | solution.py:157
  10.2 0.2 collective-permute-start.3
  10.4 0.1 pad_add_fusion.refs_0_
  10.5 1.7 %shard_map.68 = (bf16[2,512,768]{2,1,0:T(8,128)(2,1)S(1)}, bf16[512,64]{1,0:T(8,128)(2,1)S(1)}) custom-call(s32[2]{0:T(128)S(1)} %pad_add_fusion.refs_0_, bf16[256,768]{1,0:T(8,128)(2,1)S(1)} %copy-done.1, s32[1,256]{1,0:T(1,128)S(1)} %bitcast.20, bf16[256,768]{1,0:T(8,128)(2,1)S(1)} %collective-permute-done.refs_3_, ...), custom_call_target="tpu_custom_call" | custom-call | tf_op jit(solution)/shard_map/pallas_call | solution.py:142
  12.2 0.7 %collective-permute-done.4.refs_2_ = bf16[48,768]{1,0:T(8,128)(2,1)S(1)} collective-permute-done((bf16[48,768]{1,0:T(8,128)(2,1)S(1)}, bf16[48,768]{1,0:T(8,128)(2,1)S(1)}, u32[]{:S(2)}, u32[]{:S(2)}) %collective-permute-start.4) | collective-permute-done | bytes 73760 | tf_op jit(solution)/shard_map/ppermute | solution.py:157
  12.9 1.7 %collective-permute-done.3.refs_1_ = bf16[48,768]{1,0:T(8,128)(2,1)S(1)} collective-permute-done((bf16[48,768]{1,0:T(8,128)(2,1)S(1)}, bf16[48,768]{1,0:T(8,128)(2,1)S(1)}, u32[]{:S(2)}, u32[]{:S(2)}) %collective-permute-start.3) | collective-permute-done | bytes 73760 | tf_op jit(solution)/shard_map/ppermute | solution.py:157
  14.6 0.1 shard_map.71
  14.7 0.7 %collective-permute-done.6 = bf16[192,512]{1,0:T(8,128)(2,1)S(1)} collective-permute-done((bf16[192,512]{1,0:T(8,128)(2,1)S(1)}, bf16[192,512]{1,0:T(8,128)(2,1)S(1)}, u32[]{:S(2)}, u32[]{:S(2)}) %collective-permute-start.6) | collective-permute-done | bytes 196640 | tf_op jit(solution)/shard_map/ppermute | solution.py:157
  15.4 1.6 %collective-permute-start.7 = (bf16[192,512]{1,0:T(8,128)(2,1)S(1)}, bf16[192,512]{1,0:T(8,128)(2,1)S(1)}, u32[]{:S(2)}, u32[]{:S(2)}) collective-permute-start(bf16[192,512]{1,0:T(8,128)(2,1)S(1)} %broadcast_select_fusion), channel_id=1, source_target_pairs={{0,16},{4,20},{8,24},{12,28},{16,0},{20,4},{24,8},{28,12},{1,17},{... | collective-permute-start | bytes 589832 | tf_op jit(solution)/shard_map/ppermute | solution.py:157
  17.0 1.4 %shard_map.72 = bf16[1024,256]{1,0:T(8,128)(2,1)} custom-call(bf16[2,512,768]{2,1,0:T(8,128)(2,1)S(1)} %get-tuple-element.8.refs_0_, bf16[512,64]{1,0:T(8,128)(2,1)S(1)} %get-tuple-element.9.after_ref.refs_1_, bf16[192,768]{1,0:T(8,128)(2,1)S(1)} %get-tuple-element.10.refs_2_), custom_call_target="tpu_custom_call" | custom-call | tf_op jit(solution)/shard_map/pallas_call | solution.py:142
  18.4 3.5 %all-to-all-start = ((bf16[8,128,256]{2,1,0:T(8,128)(2,1)}), bf16[8,128,256]{2,1,0:T(8,128)(2,1)S(1)}, u32[]{:S(2)}, u32[]{:S(2)}) async-start(bf16[8,128,256]{2,1,0:T(8,128)(2,1)} %bitcast.9), calls=%async_computation | async-start | bytes 1048576 | tf_op jit(solution)/shard_map/all_to_all | solution.py:177
  22.0 0.5 %collective-permute-start.8 = (bf16[96,512]{1,0:T(8,128)(2,1)S(1)}, bf16[96,512]{1,0:T(8,128)(2,1)S(1)}, u32[]{:S(2)}, u32[]{:S(2)}) collective-permute-start(bf16[96,512]{1,0:T(8,128)(2,1)S(1)} %get-tuple-element.17), channel_id=1, source_target_pairs={{0,4},{4,0},{8,12},{12,8},{16,20},{20,16},{24,28},{28,24},{1,5},{5... | collective-permute-start | bytes 294920 | tf_op jit(solution)/shard_map/ppermute | solution.py:157
  22.4 0.9 %collective-permute-done.8.after_ref.refs_3_ = bf16[96,512]{1,0:T(8,128)(2,1)S(1)} collective-permute-done((bf16[96,512]{1,0:T(8,128)(2,1)S(1)}, bf16[96,512]{1,0:T(8,128)(2,1)S(1)}, u32[]{:S(2)}, u32[]{:S(2)}) %collective-permute-start.8) | collective-permute-done | bytes 98336 | tf_op jit(solution)/shard_map/ppermute | solution.py:157
  23.4 0.4 %collective-permute-start.9 = (bf16[96,512]{1,0:T(8,128)(2,1)S(1)}, bf16[96,512]{1,0:T(8,128)(2,1)S(1)}, u32[]{:S(2)}, u32[]{:S(2)}) collective-permute-start(bf16[96,512]{1,0:T(8,128)(2,1)S(1)} %shard_map.73), channel_id=1, source_target_pairs={{0,4},{4,0},{8,12},{12,8},{16,20},{20,16},{24,28},{28,24},{1,5},{5... | collective-permute-start | bytes 294920 | tf_op jit(solution)/shard_map/ppermute | solution.py:157
  23.8 0.9 %collective-permute-done.9.refs_4_ = bf16[96,512]{1,0:T(8,128)(2,1)S(1)} collective-permute-done((bf16[96,512]{1,0:T(8,128)(2,1)S(1)}, bf16[96,512]{1,0:T(8,128)(2,1)S(1)}, u32[]{:S(2)}, u32[]{:S(2)}) %collective-permute-start.9) | collective-permute-done | bytes 98336 | tf_op jit(solution)/shard_map/ppermute | solution.py:157
  24.8 6.8 %all-to-all-done = bf16[8,128,256]{2,1,0:T(8,128)(2,1)S(1)} async-done(((bf16[8,128,256]{2,1,0:T(8,128)(2,1)}), bf16[8,128,256]{2,1,0:T(8,128)(2,1)S(1)}, u32[]{:S(2)}, u32[]{:S(2)}) %all-to-all-start) | async-done | bytes 524320 | tf_op jit(solution)/shard_map/all_to_all | solution.py:177
  31.6 1.9 %shard_map.74 = (f32[512,512]{1,0:T(8,128)}, s32[1,512]{1,0:T(1,128)}) custom-call(s32[1]{0:T(128)} %bitcast.refs_0_, bf16[4,2,128,256]{3,2,1,0:T(8,128)(2,1)S(1)} %bitcast.17, bf16[192,512]{1,0:T(8,128)(2,1)S(1)} %broadcast_select_fusion.1.refs_2_, bf16[96,512]{1,0:T(8,128)(2,1)S(1)} %collective-permute-done.8.after_ref.refs_3_, ...), custom_call_target="tpu_custom_call" | custom-call | tf_op jit(solution)/shard_map/pallas_call | solution.py:142
  (18 shorter events, 0.2 us)
Async XLA Ops:
  0.6 2.2 %copy-start = (bf16[96,768]{1,0:T(8,128)(2,1)S(1)}, bf16[96,768]{1,0:T(8,128)(2,1)}, u32[]{:S(2)}) copy-start(bf16[96,768]{1,0:T(8,128)(2,1)} %param.6) | copy-start | bytes 442372
  0.6 9.9 %copy-start.1 = (bf16[256,768]{1,0:T(8,128)(2,1)S(1)}, bf16[256,768]{1,0:T(8,128)(2,1)}, u32[]{:S(2)}) copy-start(bf16[256,768]{1,0:T(8,128)(2,1)} %refs_1_.1) | copy-start | bytes 1179652
  0.7 9.9 %copy-start.2 = (s32[256]{0:T(256)S(1)}, s32[256]{0:T(256)}, u32[]{:S(2)}) copy-start(s32[256]{0:T(256)} %param.9) | copy-start | bytes 3076
  0.7 9.9 %collective-permute-start = (bf16[256,768]{1,0:T(8,128)(2,1)}, bf16[256,768]{1,0:T(8,128)(2,1)S(1)}, u32[]{:S(2)}, u32[]{:S(2)}) collective-permute-start(bf16[256,768]{1,0:T(8,128)(2,1)} %refs_1_.1), channel_id=1, source_target_pairs={{0,4},{4,0},{8,12},{12,8},{16,20},{20,16},{24,28},{28,24},{1,5},{5... | collective-permute-start | bytes 1179656 | tf_op jit(solution)/shard_map/ppermute | solution.py:157
  2.2 6.4 %collective-permute-start.2 = (bf16[192,512]{1,0:T(8,128)(2,1)S(1)}, bf16[192,512]{1,0:T(8,128)(2,1)S(1)}, u32[]{:S(2)}, u32[]{:S(2)}) collective-permute-start(bf16[192,512]{1,0:T(8,128)(2,1)S(1)} %bitcast.22), channel_id=1, source_target_pairs={{0,4},{4,0},{8,12},{12,8},{16,20},{20,16},{24,28},{28,24},{1,5},{5... | collective-permute-start | bytes 589832 | tf_op jit(solution)/shard_map/ppermute | solution.py:157
  2.4 6.2 %collective-permute-start.1 = (s32[1,256]{1,0:T(1,128)}, s32[1,256]{1,0:T(1,128)S(1)}, u32[]{:S(2)}, u32[]{:S(2)}) collective-permute-start(s32[1,256]{1,0:T(1,128)} %bitcast.19), channel_id=1, source_target_pairs={{0,4},{4,0},{8,12},{12,8},{16,20},{20,16},{24,28},{28,24},{1,5},{5... | collective-permute-start | bytes 3080 | tf_op jit(solution)/shard_map/ppermute | solution.py:157
  2.8 10.1 %collective-permute-start.4 = (bf16[48,768]{1,0:T(8,128)(2,1)S(1)}, bf16[48,768]{1,0:T(8,128)(2,1)S(1)}, u32[]{:S(2)}, u32[]{:S(2)}) collective-permute-start(bf16[48,768]{1,0:T(8,128)(2,1)S(1)} %constant_dynamic-slice_fusion.2.block_ref.refs_0_), channel_id=1, source_target_pairs={{0,2},{1,3},{2,0},{3,1},{4,6},{5,7},{6,4},{7,5},{8,10},{9,11},{10,... | collective-permute-start | bytes 221192 | tf_op jit(solution)/shard_map/ppermute | solution.py:157
  6.6 6.3 %collective-permute-start.5 = (bf16[48,768]{1,0:T(8,128)(2,1)S(1)}, bf16[48,768]{1,0:T(8,128)(2,1)S(1)}, u32[]{:S(2)}, u32[]{:S(2)}) collective-permute-start(bf16[48,768]{1,0:T(8,128)(2,1)S(1)} %constant_dynamic-slice_fusion.2.block_ref.refs_0_), channel_id=1, source_target_pairs={{0,3},{1,2},{2,1},{3,0},{4,7},{5,6},{6,5},{7,4},{8,11},{9,10},{10,... | collective-permute-start | bytes 221192 | tf_op jit(solution)/shard_map/ppermute | solution.py:157
  8.7 6.7 %collective-permute-start.6 = (bf16[192,512]{1,0:T(8,128)(2,1)S(1)}, bf16[192,512]{1,0:T(8,128)(2,1)S(1)}, u32[]{:S(2)}, u32[]{:S(2)}) collective-permute-start(bf16[192,512]{1,0:T(8,128)(2,1)S(1)} %shard_map.69.after_ref), channel_id=1, source_target_pairs={{0,8},{4,12},{8,0},{12,4},{16,24},{20,28},{24,16},{28,20},{1,9},{5... | collective-permute-start | bytes 589832 | tf_op jit(solution)/shard_map/ppermute | solution.py:157
  10.2 4.4 %collective-permute-start.3 = (bf16[48,768]{1,0:T(8,128)(2,1)S(1)}, bf16[48,768]{1,0:T(8,128)(2,1)S(1)}, u32[]{:S(2)}, u32[]{:S(2)}) collective-permute-start(bf16[48,768]{1,0:T(8,128)(2,1)S(1)} %shard_map.70), channel_id=1, source_target_pairs={{0,1},{1,0},{2,3},{3,2},{4,5},{5,4},{6,7},{7,6},{8,9},{9,8},{10,11... | collective-permute-start | bytes 221192 | tf_op jit(solution)/shard_map/ppermute | solution.py:157
  15.4 6.5 %collective-permute-start.7 = (bf16[192,512]{1,0:T(8,128)(2,1)S(1)}, bf16[192,512]{1,0:T(8,128)(2,1)S(1)}, u32[]{:S(2)}, u32[]{:S(2)}) collective-permute-start(bf16[192,512]{1,0:T(8,128)(2,1)S(1)} %broadcast_select_fusion), channel_id=1, source_target_pairs={{0,16},{4,20},{8,24},{12,28},{16,0},{20,4},{24,8},{28,12},{1,17},{... | collective-permute-start | bytes 589832 | tf_op jit(solution)/shard_map/ppermute | solution.py:157
  18.4 13.2 %all-to-all-start = ((bf16[8,128,256]{2,1,0:T(8,128)(2,1)}), bf16[8,128,256]{2,1,0:T(8,128)(2,1)S(1)}, u32[]{:S(2)}, u32[]{:S(2)}) async-start(bf16[8,128,256]{2,1,0:T(8,128)(2,1)} %bitcast.9), calls=%async_computation | async-start | bytes 1048576 | tf_op jit(solution)/shard_map/all_to_all | solution.py:177
  22.0 1.4 %collective-permute-start.8 = (bf16[96,512]{1,0:T(8,128)(2,1)S(1)}, bf16[96,512]{1,0:T(8,128)(2,1)S(1)}, u32[]{:S(2)}, u32[]{:S(2)}) collective-permute-start(bf16[96,512]{1,0:T(8,128)(2,1)S(1)} %get-tuple-element.17), channel_id=1, source_target_pairs={{0,4},{4,0},{8,12},{12,8},{16,20},{20,16},{24,28},{28,24},{1,5},{5... | collective-permute-start | bytes 294920 | tf_op jit(solution)/shard_map/ppermute | solution.py:157
  23.4 1.4 %collective-permute-start.9 = (bf16[96,512]{1,0:T(8,128)(2,1)S(1)}, bf16[96,512]{1,0:T(8,128)(2,1)S(1)}, u32[]{:S(2)}, u32[]{:S(2)}) collective-permute-start(bf16[96,512]{1,0:T(8,128)(2,1)S(1)} %shard_map.73), channel_id=1, source_target_pairs={{0,4},{4,0},{8,12},{12,8},{16,20},{20,16},{24,28},{28,24},{1,5},{5... | collective-permute-start | bytes 294920 | tf_op jit(solution)/shard_map/ppermute | solution.py:157
